TPU v7x, 32 devices: a whole 2x2x4 slice. The times are simulated.
32 devices in a mesh: seq: 4 (over z), fsdp: 8 (over y, x, core).
Axes of the slice: x: 2, y: 2, z: 4, core: 2. Of those that a mesh axis runs over, the one named last changes fastest.
Arguments:
- inputs: bfloat16 [16, 1024, 1024], P('fsdp', 'seq'), may hold values from -6 to 6
- qkv_proj: bfloat16 [3, 1024, 1024], P(None, ('seq', 'fsdp')), may hold values from -0.1875 to 0.1875
- out_proj: bfloat16 [1024, 1024], P(('seq', 'fsdp')), may hold values from -1.5 to 1.5
- ffn_in: bfloat16 [1024, 4096], P(('seq', 'fsdp')), may hold values from -0.1875 to 0.1875
- ffn_out: bfloat16 [4096, 1024], P(('seq', 'fsdp')), may hold values from -0.09375 to 0.09375
- norm_gains: bfloat16 [3, 1024], P(None, ('seq', 'fsdp')), may hold values from 0.099609375 to 1.8984375
- norm_biases: bfloat16 [3, 1024], P(None, ('seq', 'fsdp')), may hold values from -1.1953125 to 1.1953125
- centroids: bfloat16 [8, 1024], P('fsdp', 'seq'), may hold values from -0.125 to 0.125
- expert_in: bfloat16 [8, 1024, 4096], P('fsdp', None, 'seq'), may hold values from -0.1875 to 0.1875
- expert_out: bfloat16 [8, 4096, 1024], P('fsdp', 'seq'), may hold values from -0.1875 to 0.1875
- doc_lengths: int32 [16, 8], P('fsdp'), may hold values from 1 to 896, 1024 in all within a row
- routes: int32 [4, 16, 256, 1], P('seq', 'fsdp'), may hold values from 0 to 7; in each aligned block of 512 rows (0 to 511, 512 to 1023, ..., all dimensions but the last counted through in order) at most 96 rows name the same one
- out_grad: bfloat16 [16, 1024, 1024], P('fsdp', 'seq'), may hold values from -6 to 6
Outputs:
- outputs: bfloat16 [16, 1024, 1024], P('fsdp', 'seq')
- input_grad: float32 [16, 1024, 1024], P('fsdp', 'seq')
- qkv_proj_grad: float32 [3, 1024, 1024], P(None, ('seq', 'fsdp'))
- out_proj_grad: float32 [1024, 1024], P(('seq', 'fsdp'))
- ffn_in_grad: float32 [1024, 4096], P(('seq', 'fsdp'))
- ffn_out_grad: float32 [4096, 1024], P(('seq', 'fsdp'))
- gains_grad: float32 [3, 1024], P(None, ('seq', 'fsdp'))
- biases_grad: float32 [3, 1024], P(None, ('seq', 'fsdp'))
- centroids_grad: float32 [8, 1024], P('fsdp', 'seq')
- expert_in_grad: float32 [8, 1024, 4096], P('fsdp', None, 'seq')
- expert_out_grad: float32 [8, 4096, 1024], P('fsdp', 'seq')
Inputs may be any that keep to these rules, and one draw needn't show every extreme that they name: `doc_lengths`: each row's lengths sum to 1024; the longest is exactly 896. `routes`: each token names one expert; among the tokens of one device no expert is named more than 96 times, a bound that some block reaches.
All inputs are finite; a program needn't handle non-finite values.
Results may differ from a plain program's by a relative error of at most 0.015.
Values may be sent and summed in bfloat16 or wider, within the bound.
A program may use at most 320 MiB of HBM per device.

v0:
```python
import jax
import jax.numpy as jnp
from jax import lax
from jax.sharding import PartitionSpec as P

HEADS = 16
HEAD_DIM = 64


norm_eps = 1e-05


def layer_norm(values, gain_row, shift_row):
    average = jnp.mean(values, axis=-1, keepdims=True)
    centered = values - average
    variance = jnp.mean(centered * centered, axis=-1, keepdims=True)
    return centered * lax.rsqrt(variance + norm_eps) * gain_row + shift_row


def gelu_exact(values):
    return jax.nn.gelu(values, approximate=False)


def on_device(
    inputs,
    qkv_proj,
    out_proj,
    ffn_in,
    ffn_out,
    norm_gains,
    norm_biases,
    centroids,
    expert_in,
    expert_out,
    doc_lengths,
    routes,
    out_grad,
):
    rows_here, local_span, model_width = inputs.shape
    tokens_here = rows_here * local_span
    seq_index = lax.axis_index("seq")
    experts_all = lax.axis_size("fsdp")
    capacity = max(2, 3 * tokens_here // (2 * experts_all))
    row_length = local_span * lax.axis_size("seq")
    score_scale = HEAD_DIM ** (-0.5)
    qkv_all, out_all, ffin_all, ffout_all, gains_all, biases_all = (
        lax.all_gather(qkv_proj, ("seq", "fsdp"), axis=1, tiled=True),
        lax.all_gather(out_proj, ("seq", "fsdp"), axis=0, tiled=True),
        lax.all_gather(ffn_in, ("seq", "fsdp"), axis=0, tiled=True),
        lax.all_gather(ffn_out, ("seq", "fsdp"), axis=0, tiled=True),
        lax.all_gather(norm_gains, ("seq", "fsdp"), axis=1, tiled=True),
        lax.all_gather(norm_biases, ("seq", "fsdp"), axis=1, tiled=True),
    )
    gain_rows = gains_all.astype(jnp.float32)
    bias_rows = biases_all.astype(jnp.float32)
    doc_ends = jnp.cumsum(doc_lengths, axis=1)
    key_pos = jnp.arange(row_length, dtype=jnp.int32)
    key_ids = jnp.sum((key_pos[None, :, None] >= doc_ends[:, None, :-1]).astype(jnp.int32), axis=-1)
    query_pos = seq_index * local_span + jnp.arange(local_span, dtype=jnp.int32)
    query_ids = lax.dynamic_slice_in_dim(key_ids, seq_index * local_span, local_span, 1)
    allowed = (query_ids[:, :, None] == key_ids[:, None, :]) & (
        key_pos[None, None, :] <= query_pos[None, :, None]
    )
    allowed = allowed[:, None]
    resid_in = inputs.reshape(tokens_here, model_width).astype(jnp.float32)
    normed_one, norm_one_back = jax.vjp(layer_norm, resid_in, gain_rows[0], bias_rows[0])
    normed_low = normed_one.astype(jnp.bfloat16)
    projected = jnp.einsum(
        "td,sde->ste", normed_low, qkv_all, preferred_element_type=jnp.float32
    ).astype(jnp.bfloat16)
    queries = projected[0].reshape(rows_here, local_span, HEADS, HEAD_DIM)
    kv_whole = lax.all_gather(
        projected[1:].reshape(2, rows_here, local_span, model_width), "seq", axis=2, tiled=True
    )
    key_all = kv_whole[0].reshape(rows_here, row_length, HEADS, HEAD_DIM)
    value_all = kv_whole[1].reshape(rows_here, row_length, HEADS, HEAD_DIM)

    def attention_scores():
        raw_scores = (
            jnp.einsum("rqhd,rkhd->rhqk", queries, key_all, preferred_element_type=jnp.float32)
            * score_scale
        )
        return jnp.where(allowed, raw_scores, -1e30)

    scores = attention_scores()
    row_max = jnp.max(scores, axis=-1, keepdims=True)
    log_total = row_max + jnp.log(jnp.sum(jnp.exp(scores - row_max), axis=-1, keepdims=True))
    weights_low = jnp.exp(scores - log_total).astype(jnp.bfloat16)
    attended = jnp.einsum(
        "rhqk,rkhd->rqhd", weights_low, value_all, preferred_element_type=jnp.float32
    )
    attended = attended.reshape(tokens_here, model_width).astype(jnp.bfloat16)
    middle = resid_in + jnp.dot(attended, out_all, preferred_element_type=jnp.float32)
    normed_two, norm_two_back = jax.vjp(layer_norm, middle, gain_rows[1], bias_rows[1])
    hidden_low = normed_two.astype(jnp.bfloat16)
    hidden = jnp.dot(hidden_low, ffin_all, preferred_element_type=jnp.float32)
    activated, gelu_back = jax.vjp(gelu_exact, hidden)
    active_low = activated.astype(jnp.bfloat16)
    block_out = middle + jnp.dot(active_low, ffout_all, preferred_element_type=jnp.float32)
    normed_three, norm_three_back = jax.vjp(layer_norm, block_out, gain_rows[2], bias_rows[2])
    routed_low = normed_three.astype(jnp.bfloat16)
    expert_of = routes.reshape(tokens_here)
    choose = (expert_of[:, None] == jnp.arange(experts_all, dtype=jnp.int32)[None, :]).astype(
        jnp.int32
    )
    slot_rank = jnp.sum((jnp.cumsum(choose, axis=0) - 1) * choose, axis=1)
    target = expert_of * capacity + slot_rank
    placing = (
        target[:, None] == jnp.arange(experts_all * capacity, dtype=jnp.int32)[None, :]
    ).astype(jnp.bfloat16)

    def to_slots(values):
        slotted = jnp.einsum("ts,td->sd", placing, values, preferred_element_type=jnp.float32)
        return slotted.astype(jnp.bfloat16).reshape(experts_all, capacity, model_width)

    def from_slots(values):
        return jnp.dot(
            placing,
            values.reshape(experts_all * capacity, model_width),
            preferred_element_type=jnp.float32,
        )

    arrived = lax.all_to_all(
        to_slots(routed_low), "fsdp", split_axis=0, concat_axis=0, tiled=True
    ).reshape(experts_all * capacity, model_width)
    weight_in, weight_out, centroid_all = (
        lax.all_gather(expert_in, "seq", axis=2, tiled=True),
        lax.all_gather(expert_out, "seq", axis=1, tiled=True),
        lax.all_gather(centroids, "seq", axis=1, tiled=True),
    )
    gate_value = jax.nn.sigmoid(
        jnp.dot(arrived, centroid_all[0], preferred_element_type=jnp.float32)
    )
    expert_hidden = jnp.dot(arrived, weight_in[0], preferred_element_type=jnp.float32)
    expert_act, expert_gelu_back = jax.vjp(gelu_exact, expert_hidden)
    expert_low = expert_act.astype(jnp.bfloat16)
    result = jnp.dot(expert_low, weight_out[0], preferred_element_type=jnp.float32)
    gated_low = (gate_value[:, None] * result).astype(jnp.bfloat16)
    returned = lax.all_to_all(
        gated_low.reshape(experts_all, capacity, model_width),
        "fsdp",
        split_axis=0,
        concat_axis=0,
        tiled=True,
    )
    outputs = (
        (block_out + from_slots(returned))
        .astype(jnp.bfloat16)
        .reshape(rows_here, local_span, model_width)
    )
    cotangent = out_grad.reshape(tokens_here, model_width).astype(jnp.float32)
    to_experts = lax.all_to_all(
        to_slots(out_grad.reshape(tokens_here, model_width)),
        "fsdp",
        split_axis=0,
        concat_axis=0,
        tiled=True,
    )
    gated_grad = to_experts.reshape(experts_all * capacity, model_width).astype(jnp.float32)
    result_grad = (gate_value[:, None] * gated_grad).astype(jnp.bfloat16)
    gate_grad = jnp.sum(gated_grad * result, axis=-1)
    logit_grad = gate_grad * gate_value * (1.0 - gate_value)
    centroid_term = jnp.dot(logit_grad, arrived.astype(jnp.float32))
    act_grad = jnp.dot(result_grad, weight_out[0].T, preferred_element_type=jnp.float32)
    hidden_grad = expert_gelu_back(act_grad)[0].astype(jnp.bfloat16)
    out_term = jnp.dot(expert_low.T, result_grad, preferred_element_type=jnp.float32)
    in_term = jnp.dot(arrived.T, hidden_grad, preferred_element_type=jnp.float32)
    rows_grad = jnp.dot(hidden_grad, weight_in[0].T, preferred_element_type=jnp.float32)
    expert_in_grad, expert_out_grad, centroids_grad = (
        lax.psum_scatter(
            in_term[None].astype(jnp.bfloat16), "seq", scatter_dimension=2, tiled=True
        ).astype(jnp.float32),
        lax.psum_scatter(
            out_term[None].astype(jnp.bfloat16), "seq", scatter_dimension=1, tiled=True
        ).astype(jnp.float32),
        lax.psum_scatter(
            centroid_term[None].astype(jnp.bfloat16), "seq", scatter_dimension=1, tiled=True
        ).astype(jnp.float32),
    )
    rows_grad = rows_grad + logit_grad[:, None] * centroid_all[0].astype(jnp.float32)
    back_rows = lax.all_to_all(
        rows_grad.astype(jnp.bfloat16).reshape(experts_all, capacity, model_width),
        "fsdp",
        split_axis=0,
        concat_axis=0,
        tiled=True,
    )
    block_norm_grad, gain_three, bias_three = norm_three_back(from_slots(back_rows))
    block_grad = cotangent + block_norm_grad
    block_low_grad = block_grad.astype(jnp.bfloat16)
    act_dense_grad = jnp.dot(block_low_grad, ffout_all.T, preferred_element_type=jnp.float32)
    hidden_dense_grad = gelu_back(act_dense_grad)[0].astype(jnp.bfloat16)
    ffn_out_term = jnp.dot(active_low.T, block_low_grad, preferred_element_type=jnp.float32)
    ffn_in_term = jnp.dot(hidden_low.T, hidden_dense_grad, preferred_element_type=jnp.float32)
    normed_two_grad = jnp.dot(hidden_dense_grad, ffin_all.T, preferred_element_type=jnp.float32)
    middle_norm_grad, gain_two, bias_two = norm_two_back(normed_two_grad)
    middle_grad = block_grad + middle_norm_grad
    branch_grad = middle_grad.astype(jnp.bfloat16)
    out_proj_term = jnp.dot(attended.T, branch_grad, preferred_element_type=jnp.float32)
    attended_grad = jnp.dot(branch_grad, out_all.T, preferred_element_type=jnp.float32).astype(
        jnp.bfloat16
    )
    attended_grad = attended_grad.reshape(rows_here, local_span, HEADS, HEAD_DIM)
    prob_rows = jnp.exp(attention_scores() - log_total)
    prob_grad = jnp.einsum(
        "rqhd,rkhd->rhqk", attended_grad, value_all, preferred_element_type=jnp.float32
    )
    row_total = jnp.sum(prob_rows * prob_grad, axis=-1, keepdims=True)
    score_grad = (prob_rows * (prob_grad - row_total)).astype(jnp.bfloat16)
    value_grad = jnp.einsum(
        "rhqk,rqhd->rkhd",
        prob_rows.astype(jnp.bfloat16),
        attended_grad,
        preferred_element_type=jnp.float32,
    )
    query_grad = (
        jnp.einsum("rhqk,rkhd->rqhd", score_grad, key_all, preferred_element_type=jnp.float32)
        * score_scale
    ).astype(jnp.bfloat16)
    key_grad = (
        jnp.einsum("rhqk,rqhd->rkhd", score_grad, queries, preferred_element_type=jnp.float32)
        * score_scale
    )
    kv_terms = jnp.stack([key_grad, value_grad]).reshape(2, rows_here, row_length, model_width)
    kv_grad = lax.psum_scatter(
        kv_terms.astype(jnp.bfloat16), "seq", scatter_dimension=2, tiled=True
    )
    projected_grad = jnp.concatenate(
        [
            query_grad.reshape(1, tokens_here, model_width),
            kv_grad.reshape(2, tokens_here, model_width),
        ],
        axis=0,
    )
    qkv_term = jnp.einsum(
        "td,ste->sde", normed_low, projected_grad, preferred_element_type=jnp.float32
    )
    normed_one_grad = jnp.einsum(
        "ste,sde->td", projected_grad, qkv_all, preferred_element_type=jnp.float32
    )
    input_norm_grad, gain_one, bias_one = norm_one_back(normed_one_grad)
    input_grad = (middle_grad + input_norm_grad).reshape(rows_here, local_span, model_width)
    gains_term = jnp.stack([gain_one, gain_two, gain_three])
    biases_term = jnp.stack([bias_one, bias_two, bias_three])
    dense_terms = (
        lax.psum_scatter(qkv_term, ("seq", "fsdp"), scatter_dimension=1, tiled=True),
        lax.psum_scatter(out_proj_term, ("seq", "fsdp"), scatter_dimension=0, tiled=True),
        lax.psum_scatter(ffn_in_term, ("seq", "fsdp"), scatter_dimension=0, tiled=True),
        lax.psum_scatter(ffn_out_term, ("seq", "fsdp"), scatter_dimension=0, tiled=True),
        lax.psum_scatter(gains_term, ("seq", "fsdp"), scatter_dimension=1, tiled=True),
        lax.psum_scatter(biases_term, ("seq", "fsdp"), scatter_dimension=1, tiled=True),
    )
    return (
        outputs,
        input_grad,
        dense_terms[0],
        dense_terms[1],
        dense_terms[2],
        dense_terms[3],
        dense_terms[4],
        dense_terms[5],
        centroids_grad,
        expert_in_grad,
        expert_out_grad,
    )


def solution(mesh):
    placed = (
        P("fsdp", "seq", None),
        P(None, ("seq", "fsdp"), None),
        P(("seq", "fsdp"), None),
        P(("seq", "fsdp"), None),
        P(("seq", "fsdp"), None),
        P(None, ("seq", "fsdp")),
        P(None, ("seq", "fsdp")),
        P("fsdp", "seq"),
        P("fsdp", None, "seq"),
        P("fsdp", "seq", None),
        P("fsdp", None),
        P("seq", "fsdp", None, None),
        P("fsdp", "seq", None),
    )
    return jax.shard_map(
        on_device,
        mesh=mesh,
        in_specs=placed,
        out_specs=(
            P("fsdp", "seq", None),
            P("fsdp", "seq", None),
            P(None, ("seq", "fsdp"), None),
            P(("seq", "fsdp"), None),
            P(("seq", "fsdp"), None),
            P(("seq", "fsdp"), None),
            P(None, ("seq", "fsdp")),
            P(None, ("seq", "fsdp")),
            P("fsdp", "seq"),
            P("fsdp", None, "seq"),
            P("fsdp", "seq", None),
        ),
        check_vma=False,
    )
```

profile of v0, /device:TPU:0, one launch (start us, length us, event | category | flops | bytes accessed | tf_op | source)
XLA Modules:
  0.0 2483.9 jit_solution(1234178055148215638)
XLA Ops:
  11.6 43.5 %all-gather = bf16[32,32,3]{1,2,0:T(4,128)(2,1)S(1)} all-gather(bf16[1,32,3]{1,2,0:T(4,128)(2,1)} %bitcast.264), channel_id=1, replica_groups=mesh['seq'=4,'fsdp'=8] {'seq','fsdp'}, dimensions={0}, use_global_device_ids=true | all-gather | bytes 6336 | tf_op jit(solution)/shard_map/all_gather | solution.py:51
  55.2 37.2 %all-gather.1 = bf16[32,32,3]{1,2,0:T(4,128)(2,1)S(1)} all-gather(bf16[1,32,3]{1,2,0:T(4,128)(2,1)} %bitcast.265), channel_id=1, replica_groups=mesh['seq'=4,'fsdp'=8] {'seq','fsdp'}, dimensions={0}, use_global_device_ids=true | all-gather | bytes 6336 | tf_op jit(solution)/shard_map/all_gather | solution.py:52
  115.9 136.0 %all-gather.12.cloned.1.call-done = bf16[2,2,1024,1024]{3,2,1,0:T(8,128)(2,1)} async-done(((bf16[2,2,256,1024]{3,2,1,0:T(8,128)(2,1)}), bf16[2,2,1024,1024]{3,2,1,0:T(8,128)(2,1)}) %all-gather.12.cloned.1.call-update) | async-done | bytes 8388624 | tf_op jit(solution)/shard_map/all_gather | solution.py:72
  324.0 64.4 %all-gather.16.cloned.1.call-done = bf16[1024,4096]{1,0:T(8,128)(2,1)} async-done(((bf16[32,4096]{1,0:T(8,128)(2,1)}), bf16[1024,4096]{1,0:T(8,128)(2,1)}) %all-gather.16.cloned.1.call-update) | async-done | bytes 8388624 | tf_op jit(solution)/shard_map/all_gather | solution.py:49
  388.5 27.3 %multiply_convert_fusion.3 = (bf16[512,4096]{1,0:T(8,128)(2,1)}, f32[512,4096]{1,0:T(8,128)}, f32[512,4096]{1,0:T(8,128)}) fusion(bf16[1024,4096]{1,0:T(8,128)(2,1)} %all-gather.16.cloned.1.call-done, f32[512,1024]{1,0:T(8,128)S(1)} %get-tuple-element.100, f32[1024]{0:T(1024)S(1)} %bitcast.261, f32[1024]{0:T(1024)S(1)} %bitcast.248, f32[512]{0:T(512)S(1)} %fusion.63, ...), kind=kOutput, calls=%fused_computation.39 | convolution fusion | flops 4433903616 | bytes 31469568 | tf_op jit(solution)/shard_map/dot_general | solution.py:96
  415.8 51.5 %all-gather.18.cloned.1.call-done = bf16[4096,1024]{1,0:T(8,128)(2,1)} async-done(((bf16[128,1024]{1,0:T(8,128)(2,1)}), bf16[4096,1024]{1,0:T(8,128)(2,1)}) %all-gather.18.cloned.1.call-update) | async-done | bytes 8388624 | tf_op jit(solution)/shard_map/all_gather | solution.py:50
  507.5 109.5 %all-gather.20.cloned.1.call-done = bf16[1,1024,4096]{2,1,0:T(8,128)(2,1)} async-done(((bf16[1,1024,1024]{2,1,0:T(8,128)(2,1)}), bf16[1,1024,4096]{2,1,0:T(8,128)(2,1)}) %all-gather.20.cloned.1.call-update) | async-done | bytes 8388624 | tf_op jit(solution)/shard_map/all_gather | solution.py:127
  617.0 36.1 %multiply_convert_fusion.1 = (bf16[768,4096]{1,0:T(8,128)(2,1)}, f32[768,4096]{1,0:T(8,128)}, f32[768,4096]{1,0:T(8,128)}) fusion(bf16[768,1024]{1,0:T(8,128)(2,1)S(1)} %bitcast.206, bf16[1,1024,4096]{2,1,0:T(8,128)(2,1)} %all-gather.20.cloned.1.call-done), kind=kOutput, calls=%fused_computation.10 | convolution fusion | flops 6646923264 | bytes 41418752 | tf_op jit(solution)/shard_map/dot_general | solution.py:134
  653.7 112.7 %all-gather.22.cloned.1.call-done = bf16[1,4096,1024]{2,1,0:T(8,128)(2,1)} async-done(((bf16[1,1024,1024]{2,1,0:T(8,128)(2,1)}), bf16[1,4096,1024]{2,1,0:T(8,128)(2,1)}) %all-gather.22.cloned.1.call-update) | async-done | bytes 8388624 | tf_op jit(solution)/shard_map/all_gather | solution.py:128
  779.4 18.6 add_convert_fusion
  809.3 24.6 all_to_all.20
  888.5 26.6 %multiply_reduce_fusion = (f32[2,16,256]{2,1,0:T(8,128)S(1)}, f32[2,16,256,1024]{3,2,1,0:T(8,128)}) fusion(f32[2,16,256,1024]{3,2,1,0:T(8,128)} %get-tuple-element.98, f32[2,16,256]{2,1,0:T(8,128)S(1)} %copy-done.18, pred[2,256,1024]{2,1,0:T(8,128)(4,1)S(1)} %copy-done.3, bf16[2,256,16,64]{1,3,2,0:T(8,128)(2,1)} %copy.93, bf16[2,1024,16,64]{1,3,2,0:T(8,128)(2,1)} %bitcast.204), kind=kOutput, calls=%fused_computation.1 | convolution fusion | flops 1115676672 | bytes 72941568 | tf_op jit(solution)/shard_map/rqhd,rkhd->rhqk/dot_general | solution.py:205
  915.1 27.8 %multiply_convert_fusion = bf16[2,16,256,1024]{3,2,1,0:T(8,128)(2,1)} fusion(f32[2,16,256,1024]{3,2,1,0:T(8,128)} %get-tuple-element.108, f32[2,16,256,1024]{3,2,1,0:T(8,128)} %get-tuple-element.98, f32[2,16,256]{2,1,0:T(8,128)S(1)} %get-tuple-element.107, f32[2,16,256]{2,1,0:T(8,128)S(1)} %copy-done.18, pred[2,256,1024]{2,1,0:T(8,128)(4,1)S(1)} %copy-done.3), kind=kLoop, calls=%fused_computation | loop fusion | flops 50331648 | bytes 84475904 | tf_op jit(solution)/shard_map/convert_element_type | solution.py:209
  1005.7 93.6 %reduce-scatter.16.cloned.1.call-done = bf16[2,2,256,1024]{2,3,1,0:T(8,128)(2,1)} async-done(((bf16[2,2,1024,1024]{2,3,1,0:T(8,128)(2,1)}), bf16[2,2,256,1024]{2,3,1,0:T(8,128)(2,1)}) %reduce-scatter.16.cloned.1.call-update) | async-done | bytes 2097168 | tf_op jit(solution)/shard_map/reduce_scatter | solution.py:225
  1125.5 17.5 copy.100
  1180.5 19.6 all-to-all-done.1
  1204.2 63.4 %reduce-scatter.24.cloned.1.call-done = bf16[1,1024,1024]{2,1,0:T(8,128)(2,1)} async-done(((bf16[1,1024,4096]{2,1,0:T(8,128)(2,1)}), bf16[1,1024,1024]{2,1,0:T(8,128)(2,1)}) %reduce-scatter.24.cloned.1.call-update) | async-done | bytes 2097168 | tf_op jit(solution)/shard_map/reduce_scatter | solution.py:170
  1271.7 143.6 %reduce-scatter.26.cloned.1.call-done = bf16[1,1024,1024]{2,1,0:T(8,128)(2,1)} async-done(((bf16[1,4096,1024]{2,1,0:T(8,128)(2,1)}), bf16[1,1024,1024]{2,1,0:T(8,128)(2,1)}) %reduce-scatter.26.cloned.1.call-update) | async-done | bytes 2097168 | tf_op jit(solution)/shard_map/reduce_scatter | solution.py:173
  1423.0 129.0 %reduce-scatter.28.cloned.1.call-done = f32[32,3]{1,0:T(8,128)} async-done(((f32[1024,3]{1,0:T(8,128)}), f32[32,3]{1,0:T(8,128)}) %reduce-scatter.28.cloned.1.call-update) | async-done | bytes 400
  1553.4 130.4 %reduce-scatter.30.cloned.1.call-done = f32[32,3]{1,0:T(8,128)} async-done(((f32[1024,3]{1,0:T(8,128)}), f32[32,3]{1,0:T(8,128)}) %reduce-scatter.30.cloned.1.call-update) | async-done | bytes 400
  1685.2 279.5 %all-reduce.3.cloned.1.call-done = f32[3,1024,1024]{2,0,1:T(4,128)} async-done(((f32[3,1024,1024]{2,0,1:T(4,128)}), f32[3,1024,1024]{2,0,1:T(4,128)}) %all-reduce.3.cloned.1.call-update) | async-done | bytes 12582928
  1966.8 141.4 %reduce-scatter.18.cloned.1.call-done = f32[32,1024]{1,0:T(8,128)} async-done(((f32[1024,1024]{1,0:T(8,128)}), f32[32,1024]{1,0:T(8,128)}) %reduce-scatter.18.cloned.1.call-update) | async-done | bytes 131088 | tf_op jit(solution)/shard_map/reduce_scatter | solution.py:247
  2108.2 181.7 %reduce-scatter.20.cloned.1.call-done = f32[32,4096]{1,0:T(8,128)} async-done(((f32[1024,4096]{1,0:T(8,128)}), f32[32,4096]{1,0:T(8,128)}) %reduce-scatter.20.cloned.1.call-update) | async-done | bytes 524304 | tf_op jit(solution)/shard_map/reduce_scatter | solution.py:248
  2289.9 187.2 %reduce-scatter.22.cloned.1.call-done = f32[128,1024]{1,0:T(8,128)} async-done(((f32[4096,1024]{1,0:T(8,128)}), f32[128,1024]{1,0:T(8,128)}) %reduce-scatter.22.cloned.1.call-update) | async-done | bytes 524304 | tf_op jit(solution)/shard_map/reduce_scatter | solution.py:249
  (268 shorter events, 366.0 us)
Async XLA Ops:
  7.2 87.6 %all-gather.10.cloned.1.call-start = ((), (), s32[]{:S(2)}) async-start(), calls=%async_computation.13 | async-start | bytes 6488064 | tf_op jit(solution)/shard_map/all_gather | solution.py:47
  7.9 244.0 %all-gather.12.cloned.1.call-start = ((), (), s32[]{:S(2)}) async-start(), calls=%async_computation.14 | async-start | bytes 10485760 | tf_op jit(solution)/shard_map/all_gather | solution.py:72
  92.5 295.9 %copy-start.37 = (f32[1,1024]{1,0:T(1,128)}, f32[1,1024]{1,0:T(1,128)S(1)}, u32[]{:S(2)}) copy-start(f32[1,1024]{1,0:T(1,128)S(1)} %get-tuple-element.90) | copy-start | bytes 12292
  92.5 384.0 %copy-start.40 = (f32[1,1024]{1,0:T(1,128)}, f32[1,1024]{1,0:T(1,128)S(1)}, u32[]{:S(2)}) copy-start(f32[1,1024]{1,0:T(1,128)S(1)} %get-tuple-element.89) | copy-start | bytes 12292
  92.6 295.9 %copy-start.50 = (f32[1,1024]{1,0:T(1,128)}, f32[1,1024]{1,0:T(1,128)S(1)}, u32[]{:S(2)}) copy-start(f32[1,1024]{1,0:T(1,128)S(1)} %get-tuple-element.93) | copy-start | bytes 12292
  104.8 215.5 %all-gather.14.cloned.1.call-start = ((), (), s32[]{:S(2)}) async-start(), calls=%async_computation.15 | async-start | bytes 2162688 | tf_op jit(solution)/shard_map/all_gather | solution.py:48
  105.5 282.9 %all-gather.16.cloned.1.call-start = ((), (), s32[]{:S(2)}) async-start(), calls=%async_computation.16 | async-start | bytes 8650752 | tf_op jit(solution)/shard_map/all_gather | solution.py:49
  106.1 361.1 %all-gather.18.cloned.1.call-start = ((), (), s32[]{:S(2)}) async-start(), calls=%async_computation.17 | async-start | bytes 8650752 | tf_op jit(solution)/shard_map/all_gather | solution.py:50
  106.7 510.3 %all-gather.20.cloned.1.call-start = ((), (), s32[]{:S(2)}) async-start(), calls=%async_computation.18 | async-start | bytes 10485760 | tf_op jit(solution)/shard_map/all_gather | solution.py:127
  107.3 659.1 %all-gather.22.cloned.1.call-start = ((), (), s32[]{:S(2)}) async-start(), calls=%async_computation.19 | async-start | bytes 10485760 | tf_op jit(solution)/shard_map/all_gather | solution.py:128
  110.0 384.7 %copy-start.52 = (s32[512]{0:T(512)}, s32[512]{0:T(512)S(1)}, u32[]{:S(2)}) copy-start(s32[512]{0:T(512)S(1)} %multiply_add_fusion.1) | copy-start | bytes 6148
  479.3 24.5 all-to-all-start
  503.9 149.8 %all-to-all-start.2 = ((bf16[8,96,1024]{2,1,0:T(8,128)(2,1)}), bf16[8,96,1024]{2,1,0:T(8,128)(2,1)S(1)}, u32[]{:S(2)}, u32[]{:S(2)}) async-start(bf16[8,96,1024]{2,1,0:T(8,128)(2,1)} %bitcast.222), calls=%async_computation.2 | async-start | bytes 3145728 | tf_op jit(solution)/shard_map/all_to_all | solution.py:152
  507.4 591.9 %reduce-scatter.16.cloned.1.call-start = ((), (), s32[]{:S(2)}) async-start(), calls=%async_computation.20 | async-start | bytes 10485760 | tf_op jit(solution)/shard_map/reduce_scatter | solution.py:225
  958.2 220.7 %reduce-scatter.32.cloned.1.call-start = ((), (), s32[]{:S(2)}) async-start(), calls=%async_computation.28 | async-start | bytes 327680
  961.4 306.2 %reduce-scatter.24.cloned.1.call-start = ((), (), s32[]{:S(2)}) async-start(), calls=%async_computation.24 | async-start | bytes 10485760 | tf_op jit(solution)/shard_map/reduce_scatter | solution.py:170
  972.8 442.5 %reduce-scatter.26.cloned.1.call-start = ((), (), s32[]{:S(2)}) async-start(), calls=%async_computation.25 | async-start | bytes 10485760 | tf_op jit(solution)/shard_map/reduce_scatter | solution.py:173
  984.2 567.8 %reduce-scatter.28.cloned.1.call-start = ((), (), s32[]{:S(2)}) async-start(), calls=%async_computation.26 | async-start | bytes 540672
  1114.0 569.9 %reduce-scatter.30.cloned.1.call-start = ((), (), s32[]{:S(2)}) async-start(), calls=%async_computation.27 | async-start | bytes 540672
  1115.1 849.6 %all-reduce.3.cloned.1.call-start = ((), (), s32[]{:S(2)}) async-start(), calls=%async_computation.29 | async-start | bytes 33554432
  1143.1 965.1 %reduce-scatter.18.cloned.1.call-start = ((), (), s32[]{:S(2)}) async-start(), calls=%async_computation.21 | async-start | bytes 4325376 | tf_op jit(solution)/shard_map/reduce_scatter | solution.py:247
  1147.7 1142.3 %reduce-scatter.20.cloned.1.call-start = ((), (), s32[]{:S(2)}) async-start(), calls=%async_computation.22 | async-start | bytes 17301504 | tf_op jit(solution)/shard_map/reduce_scatter | solution.py:248
  1161.1 1315.9 %reduce-scatter.22.cloned.1.call-start = ((), (), s32[]{:S(2)}) async-start(), calls=%async_computation.23 | async-start | bytes 17301504 | tf_op jit(solution)/shard_map/reduce_scatter | solution.py:249
  1174.3 25.8 %all-to-all-start.1 = ((bf16[8,96,1024]{2,1,0:T(8,128)(2,1)}), bf16[8,96,1024]{2,1,0:T(8,128)(2,1)}, u32[]{:S(2)}, u32[]{:S(2)}) async-start(bf16[8,96,1024]{2,1,0:T(8,128)(2,1)} %bitcast.221), calls=%async_computation.1 | async-start | bytes 3145728 | tf_op jit(solution)/shard_map/all_to_all | solution.py:139
  (54 other events, 1964.1 us)
Sparse Core Ops, SparseCore 0:
  10.9 71.8 all-gather.9
  104.9 146.9 all-gather.11
  254.8 54.5 all-gather.13
  312.1 76.2 all-gather.15
  391.2 76.0 all-gather.17
  468.7 148.2 all-gather.19
  618.6 147.7 all-gather.21
  958.4 140.9 reduce-scatter.15
  1102.2 20.3 reduce-scatter.31
  1124.9 142.6 reduce-scatter.23
  1270.1 145.1 reduce-scatter.25
  1417.5 134.4 reduce-scatter.27
  1554.3 129.5 reduce-scatter.29
  1690.8 273.8 all-reduce.2
  1967.5 140.6 reduce-scatter.17
  2111.0 178.8 reduce-scatter.19
  2292.7 184.2 reduce-scatter.21
where the time goes:
time: 2490 us; the launch traced here: 2480 us
  waiting for transfers between devices  1850 us (74%)
  matrix products  332 us (13%)
  blocking collectives  116 us (5%)
  local copies, waits for them, and re-layouts  79.5 us (3%)
  other arithmetic  73.2 us (3%)
    unnamed x21, waiting for transfers between devices  543 us
    reduce_scatter x1, waiting for transfers between devices, on_device(): lax.psum_scatter(ffn_out_term, ('seq', 'fsdp'), scatter_dimension=0, tile...  187 us
    reduce_scatter x1, waiting for transfers between devices, on_device(): lax.psum_scatter(ffn_in_term, ('seq', 'fsdp'), scatter_dimension=0, tiled...  182 us
    reduce_scatter x1, waiting for transfers between devices, on_device(): lax.psum_scatter(out_term[None].astype(jnp.bfloat16), 'seq', scatter_dime...  144 us
    reduce_scatter x1, waiting for transfers between devices, on_device(): lax.psum_scatter(out_proj_term, ('seq', 'fsdp'), scatter_dimension=0, til...  141 us
    all_gather x1, waiting for transfers between devices, on_device(): lax.all_gather(projected[1:].reshape(2, rows_here, local_span, model_widt...  136 us
    all_gather x1, waiting for transfers between devices, on_device(): lax.all_gather(expert_out, 'seq', axis=1, tiled=True)  113 us
    all_gather x1, waiting for transfers between devices, on_device(): lax.all_gather(expert_in, 'seq', axis=2, tiled=True)  109 us
  transfers between devices with their start and end apart: 20, of which 16 were waited for; matrix products, arithmetic and copies ran while one was open for 12% of the time, Pallas kernels for 0%

commit v1 on v0

v1 whole, which is shorter than its diff:
```python
import functools

import jax
import jax.numpy as jnp
from jax import lax
from jax.experimental import pallas as pl
from jax.experimental.pallas import tpu as pltpu
from jax.sharding import PartitionSpec as P

HEAD_DIM = 64
LANES = 128
norm_eps = 1e-05
BF = jnp.bfloat16
F32 = jnp.float32


def layer_norm(values, gain_row, shift_row):
    average = jnp.mean(values, axis=-1, keepdims=True)
    centered = values - average
    variance = jnp.mean(centered * centered, axis=-1, keepdims=True)
    return centered * lax.rsqrt(variance + norm_eps) * gain_row + shift_row


def gelu_pair(values):
    cdf = 0.5 * (1.0 + lax.erf(values * (0.5**0.5)))
    pdf = 0.3989422804014327 * jnp.exp(-0.5 * values * values)
    return values * cdf, cdf + values * pdf


def mm(left, right):
    return jnp.dot(left, right, preferred_element_type=F32)


def mm_nt(left, right):
    return lax.dot_general(left, right, (((1,), (1,)), ((), ())), preferred_element_type=F32)


def mm_tn(left, right):
    return lax.dot_general(left, right, (((0,), (0,)), ((), ())), preferred_element_type=F32)


def norm_parts(values):
    average = jnp.mean(values, axis=-1, keepdims=True)
    centered = values - average
    variance = jnp.mean(centered * centered, axis=-1, keepdims=True)
    return average, lax.rsqrt(variance + norm_eps)


def norm_back(values, parts, gain_row, grads):
    average, scale = parts
    unit = (values - average) * scale
    unit_grad = grads * gain_row
    first = jnp.mean(unit_grad, axis=-1, keepdims=True)
    second = jnp.mean(unit_grad * unit, axis=-1, keepdims=True)
    return scale * (unit_grad - first - unit * second), jnp.sum(grads * unit, axis=0), jnp.sum(grads, axis=0)


def after(values, *earlier):
    return lax.optimization_barrier((values, *earlier))[0]


def seq_shift(values, step):
    size = lax.axis_size("seq")
    return lax.ppermute(values, "seq", [(i, (i + step) % size) for i in range(size)])


def seq_pair(values):
    size = lax.axis_size("seq")
    return lax.ppermute(values, "seq", [(i, i ^ 1) for i in range(size)])


def put(buffer, values, place):
    return lax.dynamic_update_index_in_dim(buffer, values, place, 0)


def pick(values, place):
    return lax.dynamic_index_in_dim(values, place, 0, keepdims=False)


def seq_exchange(values):
    size = lax.axis_size("seq")
    here = lax.axis_index("seq")
    result = put(jnp.zeros_like(values), pick(values, here), here)
    for step in range(1, size):
        arrived = seq_shift(pick(values, (here + step) % size), step)
        result = put(result, arrived, (here - step) % size)
    return result


def seq_sum_scatter(values):
    size = lax.axis_size("seq")
    here = lax.axis_index("seq")
    total = pick(values, here).astype(F32)
    for step in range(1, size):
        arrived = seq_shift(pick(values, (here + step) % size).astype(BF), step)
        total = total + arrived.astype(F32)
    return total


def masked_pair(block):
    lane = lax.broadcasted_iota(jnp.int32, block.shape, 1)
    zero = jnp.zeros_like(block)
    return jnp.where(lane < HEAD_DIM, block, zero), jnp.where(lane < HEAD_DIM, zero, block)


def allowed_block(id_col, id_row, start, size, end):
    key_pos = lax.broadcasted_iota(jnp.int32, (end, size), 0)
    query_pos = start + lax.broadcasted_iota(jnp.int32, (end, size), 1)
    return (id_col[:end, :] == id_row[:, start:end]) & (key_pos <= query_pos)


def attend_kernel(size, q_ref, k_ref, v_ref, id_row_ref, id_col_ref, o_ref, lse_ref, o_all):
    length = id_row_ref.shape[-1]
    queries = q_ref[...].reshape(length, LANES) * jnp.asarray(HEAD_DIM**-0.5, BF)
    keys = k_ref[...].reshape(length, LANES)
    values_t = v_ref[...].reshape(length, LANES).T
    id_row = id_row_ref[0]
    id_col = id_col_ref[0]
    for start in range(0, length, size):
        end = start + size
        mask = allowed_block(id_col, id_row, start, size, end)
        parts = []
        for head, query in enumerate(masked_pair(queries[start:end])):
            scores = jnp.where(mask, mm_nt(keys[:end], query), -1e30)
            top = jnp.max(scores, axis=0, keepdims=True)
            lse = top + jnp.log(jnp.sum(jnp.exp(scores - top), axis=0, keepdims=True))
            weights = jnp.exp(scores - lse).astype(BF)
            lse_ref[0, 0, pl.ds(head, 1), pl.ds(start, size)] = lse
            part = values_t[head * HEAD_DIM : (head + 1) * HEAD_DIM, :end]
            parts.append(mm(part, weights))
        o_all[pl.ds(start, size), :] = jnp.concatenate(parts, axis=0).T
    o_ref[...] = o_all[...].astype(BF).reshape(o_ref.shape)


def attend_back_kernel(
    size, q_ref, k_ref, v_ref, do_ref, lse_ref, id_row_ref, id_col_ref, dq_ref, dk_ref, dv_ref, dq_all, dk_all, dv_all
):
    length = id_row_ref.shape[-1]
    scale = HEAD_DIM**-0.5
    queries = q_ref[...].reshape(length, LANES) * jnp.asarray(scale, BF)
    keys = k_ref[...].reshape(length, LANES)
    keys_t = keys.T
    values = v_ref[...].reshape(length, LANES)
    grads = do_ref[...].reshape(length, LANES)
    id_row = id_row_ref[0]
    id_col = id_col_ref[0]
    dk_all[...] = jnp.zeros_like(dk_all)
    dv_all[...] = jnp.zeros_like(dv_all)
    for start in range(0, length, size):
        end = start + size
        mask = allowed_block(id_col, id_row, start, size, end)
        parts = []
        heads = zip(masked_pair(queries[start:end]), masked_pair(grads[start:end]), strict=True)
        for head, (query, grad) in enumerate(heads):
            scores = jnp.where(mask, mm_nt(keys[:end], query), -1e30)
            probs = jnp.exp(scores - lse_ref[0, 0, pl.ds(head, 1), pl.ds(start, size)])
            prob_grad = mm_nt(values[:end], grad)
            total = jnp.sum(probs * prob_grad, axis=0, keepdims=True)
            score_grad = (probs * (prob_grad - total)).astype(BF)
            dv_all[pl.ds(0, end), :] += mm(probs.astype(BF), grad)
            dk_all[pl.ds(0, end), :] += mm(score_grad, query)
            parts.append(mm(keys_t[head * HEAD_DIM : (head + 1) * HEAD_DIM, :end], score_grad))
        dq_all[pl.ds(start, size), :] = jnp.concatenate(parts, axis=0).T * scale
    dq_ref[...] = dq_all[...].astype(BF).reshape(dq_ref.shape)
    dk_ref[...] = dk_all[...].astype(BF).reshape(dk_ref.shape)
    dv_ref[...] = dv_all[...].astype(BF).reshape(dv_ref.shape)


def attention_specs(projected, length):
    blocks, rows, span, width3 = projected.shape
    columns = width3 // 3 // LANES

    def part(index):
        return pl.BlockSpec((blocks, 1, span, LANES), lambda r, c: (0, r, 0, index * columns + c))

    id_row = pl.BlockSpec((1, 1, length), lambda r, c: (r, 0, 0))
    id_col = pl.BlockSpec((1, length, 1), lambda r, c: (r, 0, 0))
    lse = pl.BlockSpec((1, 1, 2, length), lambda r, c: (r, c, 0, 0))
    return rows, columns, part, id_row, id_col, lse


def attend(projected, id_rows, id_cols):
    length = id_rows.shape[-1]
    blocks, rows, span, width3 = projected.shape
    rows, columns, part, id_row, id_col, lse = attention_specs(projected, length)
    return pl.pallas_call(
        functools.partial(attend_kernel, min(256, length)),
        grid=(rows, columns),
        in_specs=[part(0), part(1), part(2), id_row, id_col],
        out_specs=[part(0), lse],
        out_shape=[
            jax.ShapeDtypeStruct((blocks, rows, span, width3 // 3), BF),
            jax.ShapeDtypeStruct((rows, columns, 2, length), F32),
        ],
        scratch_shapes=[pltpu.VMEM((length, LANES), F32)],
        compiler_params=pltpu.CompilerParams(vmem_limit_bytes=40 * 2**20),
        cost_estimate=pl.CostEstimate(flops=3 * 10**9, bytes_accessed=8 * 2**20, transcendentals=10**7),
    )(projected, projected, projected, id_rows, id_cols)


def attend_back(projected, grads, lse_rows, id_rows, id_cols):
    length = id_rows.shape[-1]
    blocks, rows, span, width3 = projected.shape
    rows, columns, part, id_row, id_col, lse = attention_specs(projected, length)
    shape = jax.ShapeDtypeStruct((blocks, rows, span, width3 // 3), BF)
    return pl.pallas_call(
        functools.partial(attend_back_kernel, min(256, length)),
        grid=(rows, columns),
        in_specs=[part(0), part(1), part(2), part(0), lse, id_row, id_col],
        out_specs=[part(0)] * 3,
        out_shape=[shape] * 3,
        scratch_shapes=[pltpu.VMEM((length, LANES), F32)] * 3,
        compiler_params=pltpu.CompilerParams(vmem_limit_bytes=48 * 2**20),
        cost_estimate=pl.CostEstimate(flops=8 * 10**9, bytes_accessed=12 * 2**20, transcendentals=10**7),
    )(projected, projected, projected, grads, lse_rows, id_rows, id_cols)


def fsdp_flip(values, bit):
    size = lax.axis_size("fsdp")
    return lax.ppermute(values, "fsdp", [(i, i ^ bit) for i in range(size)])


def fsdp_bits(crossed):
    bits = [1 << i for i in range(1, lax.axis_size("fsdp").bit_length() - 1)]
    return (bits[::-1] if crossed else bits) + [1]


def hyper_split(parts):
    count = parts.shape[1].bit_length() - 1
    return parts.reshape(parts.shape[0], *[2] * count, *parts.shape[2:])


def hyper_scatter_step(held, bit):
    count = lax.axis_size("fsdp").bit_length() - 1
    axis = count + 1 - bit.bit_length()
    bit_here = (lax.axis_index("fsdp") // bit) % 2
    sent = lax.dynamic_slice_in_dim(held, 1 - bit_here, 1, axis)
    kept = lax.dynamic_slice_in_dim(held, bit_here, 1, axis)
    arrived = fsdp_flip(sent, bit)
    return (kept.astype(F32) + arrived.astype(F32)).astype(BF)


def hyper_scatter(held, bits):
    for bit in bits:
        held = hyper_scatter_step(held, bit)
    return held


def by_device(term):
    seq_size, fsdp_size = lax.axis_size("seq"), lax.axis_size("fsdp")
    return term.astype(BF).reshape(seq_size, fsdp_size, -1, term.shape[-1])


def gather_kernel(seq_size, bits, proj_ref, in_ref, out_ref, x_ref, proj_all, in_all, out_all, x_all, *sems):
    own_sem, proj_send, proj_recv, line_send, line_recv, cube_send, cube_recv = sems
    z = lax.axis_index("seq")
    f = lax.axis_index("fsdp")
    count = len(bits)
    high_first = sorted(bits, reverse=True)
    bit_of = {bit: (f // bit) % 2 for bit in bits}
    mesh_id = pl.DeviceIdType.MESH

    barrier = pltpu.get_barrier_semaphore()
    for step in range(1, seq_size):
        pl.semaphore_signal(barrier, inc=1, device_id={"seq": lax.rem(z + step, seq_size)}, device_id_type=mesh_id)
    for bit in bits:
        pl.semaphore_signal(barrier, inc=1, device_id={"fsdp": f + bit * (1 - 2 * bit_of[bit])}, device_id_type=mesh_id)
    pl.semaphore_wait(barrier, seq_size - 1 + count)

    def place(buffer, s, done=()):
        if buffer is x_all:
            return buffer.at[s]
        return buffer.at[(s, *(slice(None) if bit in done else bit_of[bit] for bit in high_first))]

    def order_of(index, turn):
        return bits if (index + turn) % 2 == 0 else bits[-2::-1] + bits[-1:]

    cubes = ((proj_all, 0), (in_all, 0), (out_all, 1))

    def cube(index, s, turn, step):
        buffer, crossed = cubes[index]
        order = order_of(crossed, turn if index == 0 else 0)
        view = place(buffer, s, order[:step])
        bit = order[step]
        return pltpu.make_async_remote_copy(
            src_ref=view,
            dst_ref=view,
            send_sem=cube_send.at[index, turn, step],
            recv_sem=cube_recv.at[index, turn, step],
            device_id={"fsdp": f + bit * (1 - 2 * bit_of[bit])},
            device_id_type=mesh_id,
        )

    lines = ((in_all, in_ref), (out_all, out_ref), (x_all, x_ref))

    def line(index, side, hop):
        buffer, own = lines[index]
        ahead = 1 - 2 * side
        s = z - ahead * (hop - 1)
        view = place(buffer, s)
        return pltpu.make_async_remote_copy(
            src_ref=own if hop == 1 else view,
            dst_ref=view,
            send_sem=line_send.at[index, side, hop - 1],
            recv_sem=line_recv.at[index, side, hop - 1],
            device_id={"seq": z + ahead},
            device_id_type=mesh_id,
        )

    def line_wait(index, side, hop):
        view = place(lines[index][0], z - (1 - 2 * side) * hop)
        pltpu.make_async_remote_copy(
            src_ref=view,
            dst_ref=view,
            send_sem=line_send.at[index, side, hop - 1],
            recv_sem=line_recv.at[index, side, hop - 1],
            device_id={"seq": z - (1 - 2 * side)},
            device_id_type=mesh_id,
        ).wait_recv()

    def has_next(side):
        return z < seq_size - 1 if side == 0 else z > 0

    def has_block(side, hop):
        return z - hop >= 0 if side == 0 else z + hop < seq_size

    def proj(step):
        to = lax.rem(z + step, seq_size)
        return pltpu.make_async_remote_copy(
            src_ref=proj_ref.at[to],
            dst_ref=place(proj_all, z),
            send_sem=proj_send.at[step - 1],
            recv_sem=proj_recv.at[step - 1],
            device_id={"seq": to},
            device_id_type=mesh_id,
        )

    def proj_wait(step):
        view = place(proj_all, lax.rem(z + seq_size - step, seq_size))
        pltpu.make_async_remote_copy(
            src_ref=view,
            dst_ref=view,
            send_sem=proj_send.at[step - 1],
            recv_sem=proj_recv.at[step - 1],
            device_id={"seq": lax.rem(z + step, seq_size)},
            device_id_type=mesh_id,
        ).wait_recv()

    def turn_of(side, hop):
        return 0 if hop == 0 else 2 * hop - 1 + side

    def each_block(hop, act):
        act(0, lax.rem(z + seq_size - hop, seq_size), turn_of(0, hop))
        for index in (1, 2):
            if hop == 0:
                act(index, z, 0)
                continue
            for side in (0, 1):

                @pl.when(has_block(side, hop))
                def _(index=index, side=side):
                    act(index, z - (1 - 2 * side) * hop, turn_of(side, hop))

    owns = [
        pltpu.make_async_copy(own, place(buffer, z), own_sem.at[i])
        for i, (own, buffer) in enumerate(((proj_ref.at[z], proj_all), (in_ref, in_all), (out_ref, out_all), (x_ref, x_all)))
    ]
    for copy in owns:
        copy.start()
    for step in range(1, seq_size):
        proj(step).start()
    for index in range(3):
        for side in (0, 1):

            @pl.when(has_next(side))
            def _(index=index, side=side):
                line(index, side, 1).start()

    for copy in owns:
        copy.wait()
    each_block(0, lambda index, s, turn: cube(index, s, turn, 0).start())

    def advance(hop):
        for step in range(1, count):

            def act(index, s, turn, step=step):
                cube(index, s, turn, step - 1).wait()
                cube(index, s, turn, step).start()

            each_block(hop, act)

    for hop in range(1, seq_size):
        advance(hop - 1)
        proj_wait(hop)
        cube(0, lax.rem(z + seq_size - hop, seq_size), turn_of(0, hop), 0).start()
        for index in range(3):
            for side in (0, 1):

                @pl.when(has_block(side, hop))
                def _(index=index, side=side, hop=hop):
                    line_wait(index, side, hop)
                    if hop < seq_size - 1:

                        @pl.when(has_next(side))
                        def _():
                            line(index, side, hop + 1).start()

                    if index < 2:
                        cube(index + 1, z - (1 - 2 * side) * hop, turn_of(side, hop), 0).start()

    advance(seq_size - 1)
    for hop in range(seq_size):
        each_block(hop, lambda index, s, turn: cube(index, s, turn, count - 1).wait())
    for step in range(1, seq_size):
        proj(step).wait_send()
    for index in range(3):
        for side in (0, 1):
            for hop in range(1, seq_size):

                @pl.when(has_next(side) & has_block(side, hop - 1))
                def _(index=index, side=side, hop=hop):
                    line(index, side, hop).wait_send()


def start_gathers(proj, ffn_in, ffn_out, tokens_in):
    seq_size, fsdp_size = lax.axis_size("seq"), lax.axis_size("fsdp")
    bits = fsdp_bits(False)
    count = len(bits)

    def whole(shard):
        return jax.ShapeDtypeStruct((seq_size, *[2] * count, *shard), BF)

    turns = 2 * seq_size - 1
    dma = pltpu.SemaphoreType.DMA
    anywhere = pl.BlockSpec(memory_space=pl.ANY)
    outs = pl.pallas_call(
        functools.partial(gather_kernel, seq_size, bits),
        in_specs=[anywhere] * 4,
        out_specs=[anywhere] * 4,
        out_shape=[
            whole(proj.shape[1:]),
            whole(ffn_in.shape),
            whole(ffn_out.shape),
            jax.ShapeDtypeStruct((seq_size, *tokens_in.shape), BF),
        ],
        scratch_shapes=[
            dma((4,)),
            dma((seq_size - 1,)),
            dma((seq_size - 1,)),
            dma((3, 2, seq_size - 1)),
            dma((3, 2, seq_size - 1)),
            dma((3, turns, count)),
            dma((3, turns, count)),
        ],
        compiler_params=pltpu.CompilerParams(collective_id=0, has_side_effects=True),
        cost_estimate=pl.CostEstimate(flops=0, bytes_accessed=100 * 2**20, transcendentals=0),
    )(proj, ffn_in, ffn_out, tokens_in)
    proj_all, in_all, out_all, inputs_all = outs
    flat = (seq_size, fsdp_size)
    return (
        proj_all.reshape(*flat, *proj.shape[1:]),
        in_all.reshape(*flat, *ffn_in.shape),
        out_all.reshape(*flat, *ffn_out.shape),
        inputs_all,
    )


def whole_tiles(shard, rows=16):
    return shard if shard.shape[0] % rows == 0 else shard.reshape(rows, -1)


def on_device(
    inputs,
    qkv_proj,
    out_proj,
    ffn_in,
    ffn_out,
    norm_gains,
    norm_biases,
    centroids,
    expert_in,
    expert_out,
    doc_lengths,
    routes,
    out_grad,
):
    rows, span, width = inputs.shape
    tokens = rows * span
    seq_size, fsdp_size = lax.axis_size("seq"), lax.axis_size("fsdp")
    here = lax.axis_index("seq")
    length = span * seq_size
    cols = width // seq_size
    capacity = max(2, 3 * tokens // (2 * fsdp_size))
    groups = seq_size // 2

    docs = doc_lengths.shape[1]
    key_pos = jnp.arange(length, dtype=jnp.int32)
    doc_ids = jnp.zeros((rows, length), jnp.int32)
    doc_end = jnp.zeros((rows, 1), jnp.int32)
    for j in range(docs - 1):
        doc_end = doc_end + doc_lengths[:, j : j + 1]
        doc_ids = doc_ids + (key_pos[None, :] >= doc_end).astype(jnp.int32)
    id_rows, id_cols = doc_ids[:, None, :], doc_ids[:, :, None]

    depth = out_proj.shape[0]
    wide = 3 * cols + width
    slices = qkv_proj.reshape(3, depth, seq_size, cols).transpose(2, 1, 0, 3).reshape(seq_size, depth, 3 * cols)
    slices = jnp.concatenate([slices, jnp.broadcast_to(out_proj[None], (seq_size, depth, width))], axis=2)
    small = jnp.concatenate([norm_gains.reshape(-1), norm_biases.reshape(-1), centroids[0]])
    spare = 32 - depth % 16 if depth % 16 else 16
    extra = jnp.pad(small, (0, spare * wide - small.shape[0])).reshape(1, spare, wide)
    extra = jnp.broadcast_to(extra, (seq_size, spare, wide))
    bits = fsdp_bits(False)
    crossed = fsdp_bits(True)
    tokens_in = inputs.reshape(tokens, width)
    proj_all, ffin_all, ffout_all, inputs_all = start_gathers(
        jnp.concatenate([slices, extra], axis=1), whole_tiles(ffn_in), whole_tiles(ffn_out), tokens_in
    )
    inputs_all = inputs_all.reshape(seq_size * tokens, width)
    ffin_all, ffout_all = ffin_all.reshape(width, -1), ffout_all.reshape(-1, width)
    qkv_mine = proj_all[:, :, :depth, : 3 * cols].reshape(width, 3 * cols)
    out_all = proj_all[:, :, :depth, 3 * cols :].reshape(width, width)
    small = proj_all[:, :, depth, :]
    rows_of = small[:, :, : 6 * depth].astype(F32).reshape(-1, 6, depth).transpose(1, 0, 2).reshape(6, width)
    gain_rows, bias_rows = rows_of[:3], rows_of[3:]
    mine = small[:, :, 6 * depth : 6 * depth + cols]
    centroid = lax.dynamic_index_in_dim(mine, lax.axis_index("fsdp"), 1, keepdims=False).reshape(width)
    win_mine, wout_mine, dr_mine = after((expert_in[0], expert_out[0], out_grad.reshape(tokens, width)), inputs_all)
    parts_all = norm_parts(inputs_all.astype(F32))
    normed_flat = ((inputs_all.astype(F32) - parts_all[0]) * parts_all[1] * gain_rows[0] + bias_rows[0]).astype(BF)
    projected = mm(normed_flat, qkv_mine).astype(BF).reshape(seq_size, rows, span, 3 * cols)

    attended_mine, lse_rows = attend(projected, id_rows, id_cols)
    attended = seq_exchange(attended_mine).transpose(1, 2, 0, 3).reshape(tokens, width)

    route = routes.reshape(tokens)
    later = (jnp.arange(tokens)[:, None] > jnp.arange(tokens)[None, :]).astype(BF)
    choose = route[:, None] == jnp.arange(fsdp_size, dtype=jnp.int32)[None, :]
    before = mm(later, choose.astype(BF))
    slot_rank = jnp.sum(jnp.where(choose, before, 0.0), axis=1).astype(jnp.int32)
    target = route * capacity + slot_rank
    grad_tokens = out_grad.reshape(tokens, width)
    placings = []
    for group in range(groups):
        slot_of = target if group == 0 else seq_shift(target, 2 * group)
        placing = (slot_of[:, None] == jnp.arange(fsdp_size * capacity, dtype=jnp.int32)[None, :]).astype(BF)
        placings.append(placing)

    def slots_of(placing, values):
        return mm_tn(placing, values).astype(BF).reshape(fsdp_size, capacity, width)

    def swap_slots(values):
        return lax.all_to_all(values, "fsdp", split_axis=0, concat_axis=0, tiled=True)

    def tokens_of(placing, values):
        return mm(placing, values.reshape(fsdp_size * capacity, width))

    grad_arrived = []
    for group in range(groups):
        values = grad_tokens if group == 0 else seq_shift(dr_mine, 2 * group)
        grad_arrived.append(swap_slots(slots_of(placings[group], values)).reshape(-1, width))

    win = jnp.concatenate([win_mine, seq_pair(win_mine)], axis=1)
    wout = jnp.concatenate([wout_mine, seq_pair(wout_mine)], axis=0)

    resid_in = tokens_in.astype(F32)
    middle = resid_in + mm(attended, out_all)
    parts_two = norm_parts(middle)
    hidden_low = ((middle - parts_two[0]) * parts_two[1] * gain_rows[1] + bias_rows[1]).astype(BF)
    active, active_slope = gelu_pair(mm(hidden_low, ffin_all))
    active_low, active_slope = lax.optimization_barrier((active.astype(BF), active_slope.astype(BF)))
    block_out = middle + mm(active_low, ffout_all)
    parts_three = norm_parts(block_out)
    routed = ((block_out - parts_three[0]) * parts_three[1] * gain_rows[2] + bias_rows[2]).astype(BF)

    arrived_all, dz_all, du_all, act_all, back_terms, gated_all = [], [], [], [], [], []
    centroid_term = jnp.zeros((width,), F32)
    for group in range(groups):
        values = routed if group == 0 else seq_shift(routed, 2 * group)
        arrived = swap_slots(slots_of(placings[group], values)).reshape(-1, width)
        gated = grad_arrived[group].astype(F32)
        gate = jax.nn.sigmoid(mm(arrived, centroid))
        dz = (gate[:, None] * gated).astype(BF)
        act, slope = gelu_pair(mm(arrived, win))
        act, slope = lax.optimization_barrier((act.astype(BF), slope.astype(BF)))
        result = mm(act, wout)
        dl = jnp.sum(gated * result, axis=-1) * gate * (1.0 - gate)
        du = (slope.astype(F32) * mm_nt(dz, wout)).astype(BF)
        rows_grad = mm_nt(du, win) + dl[:, None] * centroid.astype(F32)
        centroid_term = centroid_term + jnp.sum(dl[:, None] * arrived.astype(F32), axis=0)
        back = tokens_of(placings[group], swap_slots(rows_grad.astype(BF).reshape(fsdp_size, capacity, width)))
        if group:
            back = seq_shift(back.astype(BF), -2 * group).astype(F32)
        back_terms.append(back)
        gated_all.append((gate[:, None] * result).astype(BF).reshape(fsdp_size, capacity, width))
        arrived_all.append(arrived)
        dz_all.append(dz)
        du_all.append(du)
        act_all.append(act)

    half = expert_in.shape[2]
    arrived, dz, du, act = (jnp.concatenate(v, axis=0) for v in (arrived_all, dz_all, du_all, act_all))
    in_sent = mm_tn(arrived, du[:, half:]).astype(BF)
    out_sent = mm_tn(act[:, half:], dz).astype(BF)
    in_kept = mm_tn(arrived, du[:, :half])
    out_kept = mm_tn(act[:, :half], dz)
    in_pair, out_pair = seq_pair(in_sent), seq_pair(out_sent)
    back_sum, in_sent, out_sent, in_kept, out_kept = lax.optimization_barrier(
        (sum(back_terms), in_sent, out_sent, in_kept, out_kept)
    )

    block_norm_grad, gain_three, bias_three = norm_back(block_out, parts_three, gain_rows[2], back_sum)
    block_grad = grad_tokens.astype(F32) + block_norm_grad
    block_low = block_grad.astype(BF)
    hidden_grad = (active_slope.astype(F32) * mm_nt(block_low, ffout_all)).astype(BF)
    normed_two_grad = mm_nt(hidden_grad, ffin_all)
    middle_norm_grad, gain_two, bias_two = norm_back(middle, parts_two, gain_rows[1], normed_two_grad)
    middle_grad = block_grad + middle_norm_grad
    branch = middle_grad.astype(BF)
    attended_grad = mm_nt(branch, out_all).astype(BF)
    attended_grad = attended_grad.reshape(rows, span, seq_size, cols).transpose(2, 0, 1, 3)
    attended_grad = seq_exchange(attended_grad)

    gated_back = swap_slots(jnp.concatenate(gated_all, axis=1)).reshape(fsdp_size, groups, capacity, width)
    outputs = block_out
    for group in range(groups):
        out = tokens_of(placings[group], gated_back[:, group])
        if group:
            out = seq_shift(out.astype(BF), -2 * group).astype(F32)
        outputs = outputs + out
    outputs = outputs.astype(BF).reshape(rows, span, width)

    ffout_terms = hyper_split(by_device(mm_tn(active_low, block_low)))
    ffin_terms = hyper_split(by_device(mm_tn(hidden_low, hidden_grad)))
    out_terms = mm_tn(attended, branch)
    ffout_terms = hyper_scatter_step(ffout_terms, crossed[-1])
    ffin_terms = hyper_scatter_step(ffin_terms, bits[-1])
    attended_grad, ffout_terms, ffin_terms = lax.optimization_barrier((attended_grad, ffout_terms, ffin_terms))
    ffout_terms = hyper_scatter(ffout_terms, crossed[-2:0:-1])
    ffin_terms = hyper_scatter(ffin_terms, bits[-2:0:-1])

    dq, dk, dv = attend_back(projected, attended_grad, lse_rows, id_rows, id_cols)
    projected_grad = jnp.concatenate([dq, dk, dv], axis=-1).reshape(seq_size * tokens, 3 * cols)
    projected_grad, ffout_terms, ffin_terms = lax.optimization_barrier((projected_grad, ffout_terms, ffin_terms))
    normed_low_terms = mm_nt(projected_grad, qkv_mine).astype(BF)
    normed_one_grad = seq_sum_scatter(normed_low_terms.reshape(seq_size, tokens, width))
    unit_all = (inputs_all.astype(F32) - parts_all[0]) * parts_all[1]
    terms_wide = normed_low_terms.astype(F32)
    gain_one, bias_one = jnp.sum(terms_wide * unit_all, axis=0), jnp.sum(terms_wide, axis=0)
    small_terms = jnp.stack([gain_one, gain_two, gain_three, bias_one, bias_two, bias_three])

    ffout_terms = hyper_scatter_step(ffout_terms, crossed[0])
    ffin_terms = hyper_scatter_step(ffin_terms, bits[0])
    ffn_out_grad = seq_sum_scatter(ffout_terms.reshape(seq_size, *ffn_out.shape))
    ffn_in_grad = seq_sum_scatter(ffin_terms.reshape(seq_size, *ffn_in.shape))

    proj_terms = jnp.concatenate([mm_tn(normed_flat, projected_grad).astype(BF), out_terms.astype(BF)], axis=1)
    proj_terms = proj_terms.reshape(seq_size, fsdp_size, depth, wide)
    small_rows = small_terms.astype(BF).reshape(6, seq_size, fsdp_size, depth).transpose(1, 2, 0, 3)
    small_rows = small_rows.reshape(seq_size, fsdp_size, 1, 6 * depth)
    small_rows = jnp.pad(small_rows, ((0, 0), (0, 0), (0, 7), (0, wide - 6 * depth)))
    proj_terms = hyper_split(jnp.concatenate([proj_terms, small_rows], axis=2))
    proj_terms = hyper_scatter(proj_terms, bits[::-1]).reshape(seq_size, depth + 8, wide)
    centroid_rows = centroid_term.astype(BF).reshape(seq_size, 1, cols)
    proj_terms = lax.dynamic_update_slice(proj_terms, centroid_rows, (0, depth + 1, 0))
    proj_sums = seq_exchange(proj_terms).astype(F32)
    qkv_grad = proj_sums[:, :depth, : 3 * cols].reshape(seq_size, depth, 3, cols)
    qkv_grad = qkv_grad.transpose(2, 1, 0, 3).reshape(qkv_proj.shape)
    out_proj_grad = jnp.sum(proj_sums[:, :depth, 3 * cols :], axis=0)
    small_grad = jnp.sum(proj_sums[:, depth, : 6 * depth], axis=0).reshape(6, depth)
    centroids_grad = jnp.sum(proj_sums[:, depth + 1, :cols], axis=0)[None]

    in_pair, out_pair = lax.optimization_barrier((in_pair, out_pair, normed_low_terms))[:2]
    expert_in_grad = (in_kept + in_pair.astype(F32))[None]
    expert_out_grad = (out_kept + out_pair.astype(F32))[None]

    input_norm_grad, _, _ = norm_back(resid_in, norm_parts(resid_in), gain_rows[0], normed_one_grad)
    input_grad = (middle_grad + input_norm_grad).reshape(rows, span, width)
    return (
        outputs,
        input_grad,
        qkv_grad,
        out_proj_grad,
        ffn_in_grad,
        ffn_out_grad,
        small_grad[:3],
        small_grad[3:],
        centroids_grad,
        expert_in_grad,
        expert_out_grad,
    )


def solution(mesh):
    dense = P(("seq", "fsdp"), None)
    placed = (
        P("fsdp", "seq", None),
        P(None, ("seq", "fsdp"), None),
        dense,
        dense,
        dense,
        P(None, ("seq", "fsdp")),
        P(None, ("seq", "fsdp")),
        P("fsdp", "seq"),
        P("fsdp", None, "seq"),
        P("fsdp", "seq", None),
        P("fsdp", None),
        P("seq", "fsdp", None, None),
        P("fsdp", "seq", None),
    )
    returned = (
        P("fsdp", "seq", None),
        P("fsdp", "seq", None),
        P(None, ("seq", "fsdp"), None),
        dense,
        dense,
        dense,
        P(None, ("seq", "fsdp")),
        P(None, ("seq", "fsdp")),
        P("fsdp", "seq"),
        P("fsdp", None, "seq"),
        P("fsdp", "seq", None),
    )
    return jax.shard_map(on_device, mesh=mesh, in_specs=placed, out_specs=returned, check_vma=False)
```

time: 2490 us -> 984 us (0.40)
  waiting for transfers between devices: 1850 us -> 303 us
  Pallas kernels: 0 us -> 222 us
  matrix products: 332 us -> 182 us
  blocking collectives: 116 us -> 0 us
  starting transfers between devices: 13.8 us -> 104 us
    reduce_scatter x6 -> x0, waiting for transfers between devices: 811 us -> none  [the longest x1 187 us: on_device(): lax.psum_scatter(ffn_out_term, ('seq', 'fsdp'), scatter_dimension=0, tile...]
    unnamed x21 -> x0, waiting for transfers between devices: 543 us -> none
    all_gather x7 -> x0, waiting for transfers between devices: 474 us -> none  [the longest x1 136 us: on_device(): lax.all_gather(projected[1:].reshape(2, rows_here, local_span, model_widt...]
    ppermute x0 -> x36, waiting for transfers between devices: none -> 289 us  [the longest x23 194 us: seq_shift(): lax.ppermute(values, 'seq', [(i, (i + step) % size) for i in range(size)])]
    pallas_call x0 -> x3, Pallas kernels: none -> 222 us  [the longest x1 181 us: start_gathers(): pl.pallas_call(functools.partial(gather_kernel, seq_size, bits), in_specs...]
    dot_general x30 -> x35, matrix products: 332 us -> 182 us  [the longest x15 70 us: mm(): return jnp.dot(left, right, preferred_element_type=F32)]
    all_gather x3 -> x0, blocking collectives: 91.8 us -> none  [the longest x1 43.5 us: on_device(): lax.all_gather(norm_gains, ('seq', 'fsdp'), axis=1, tiled=True)]
    ppermute x0 -> x36, starting transfers between devices: none -> 72.8 us  [the longest x23 58 us: seq_shift(): lax.ppermute(values, 'seq', [(i, (i + step) % size) for i in range(size)])]
  transfers between devices with their start and end apart: 20 -> 43, of which waited for: 16 -> 18; matrix products, arithmetic and copies ran while one was open for 12% -> 27% of each run, Pallas kernels for 0% -> 2%
where the time goes in v1:
time: 984 us; the launch traced here: 974 us
  waiting for transfers between devices  303 us (31%)
  Pallas kernels  222 us (23%)
  matrix products  182 us (18%)
  starting transfers between devices  104 us (11%)
  local copies, waits for them, and re-layouts  86.3 us (9%)
  other arithmetic  74.2 us (8%)
    ppermute x23, waiting for transfers between devices, seq_shift(): lax.ppermute(values, 'seq', [(i, (i + step) % size) for i in range(size)])  194 us
    pallas_call x1, Pallas kernels, start_gathers(): pl.pallas_call(functools.partial(gather_kernel, seq_size, bits), in_specs...  181 us
    dot_general x15, matrix products, mm(): return jnp.dot(left, right, preferred_element_type=F32)  70 us
    dot_general x12, matrix products, mm_tn(): lax.dot_general(left, right, (((0,), (0,)), ((), ())), preferred_element_...  61.3 us
    ppermute x9, waiting for transfers between devices, fsdp_flip(): return lax.ppermute(values, 'fsdp', [(i, i ^ bit) for i in range(size)])  60.7 us
    ppermute x23, starting transfers between devices, seq_shift(): lax.ppermute(values, 'seq', [(i, (i + step) % size) for i in range(size)])  58 us
    dot_general x8, matrix products, mm_nt(): lax.dot_general(left, right, (((1,), (1,)), ((), ())), preferred_element_...  50.6 us
    ppermute x4, waiting for transfers between devices, seq_pair(): return lax.ppermute(values, 'seq', [(i, i ^ 1) for i in range(size)])  34.4 us
  transfers between devices with their start and end apart: 43, of which 18 were waited for; matrix products, arithmetic and copies ran while one was open for 27% of the time, Pallas kernels for 2%

profile of v1, /device:TPU:0, one launch (start us, length us, event | category | flops | bytes accessed | tf_op | source)
XLA Modules:
  0.0 974.5 jit_solution(12498165100045573332)
XLA Ops:
  6.3 180.7 %shard_map.212 = (bf16[4,2,2,2,48,1792]{5,4,3,2,1,0:T(8,128)(2,1)}, bf16[4,2,2,2,32,4096]{5,4,3,2,1,0:T(8,128)(2,1)}, bf16[4,2,2,2,128,1024]{5,4,3,2,1,0:T(8,128)(2,1)}, bf16[4,512,1024]{2,1,0:T(8,128)(2,1)}) custom-call(bf16[4,48,1792]{2,1,0:T(8,128)(2,1)} %pad_maximum_fusion.15.proj_ref, bf16[32,4096]{1,0:T(8,128)(2,1)} %in_ref.1, ...), custom_call_target="tpu_custom_call" | custom-call | bytes 104857600 | tf_op jit(solution)/shard_map/pallas_call | solution.py:436
  206.3 20.0 %shard_map.213 = (bf16[4,2,256,256]{3,2,1,0:T(8,128)(2,1)S(1)}, f32[2,2,2,1024]{3,2,1,0:T(2,128)S(1)}) custom-call(bf16[4,2,256,768]{3,2,1,0:T(8,128)(2,1)S(1)} %bitcast.202, bf16[4,2,256,768]{3,2,1,0:T(8,128)(2,1)S(1)} %bitcast.203, bf16[4,2,256,768]{3,2,1,0:T(8,128)(2,1)S(1)} %bitcast.204, s32[2,1,1024]{2,1,0:T(1,128)S(1)} %fusion.95.id_row_ref, ...), custom_call_target="tpu_custom_call" | custom-call | flops 3000000000 | bytes 8388608 | tf_op jit(solution)/shard_map/pallas_call | solution.py:186
  253.8 11.9 %fusion.10 = (bf16[512,4096]{1,0:T(8,128)(2,1)}, bf16[512,4096]{1,0:T(8,128)(2,1)S(1)}) fusion(bf16[1024,4096]{1,0:T(8,128)(2,1)} %bitcast.272, f32[512,1024]{1,0:T(8,128)S(1)} %get-tuple-element.141, f32[1024]{0:T(1024)S(1)} %copy-done.58, f32[1024]{0:T(1024)S(1)} %copy-done.50, f32[512]{0:T(512)S(1)} %add_rsqrt_fusion.2, f32[512]{0:T(512)S(1)} %broadcast_multiply_fusion.9), kind=kOutput, calls=%fused_computation.15 | convolution fusion | flops 4320657408 | bytes 18886656 | tf_op jit(solution)/shard_map/dot_general | solution.py:31
  291.8 43.7 %collective-permute-done.5 = s32[512]{0:T(512)} collective-permute-done((s32[512]{0:T(512)}, s32[512]{0:T(512)}, u32[]{:S(2)}, u32[]{:S(2)}) %collective-permute-start.5) | collective-permute-done | bytes 2080 | tf_op jit(solution)/shard_map/ppermute | solution.py:64
  335.5 22.5 %collective-permute-done.8 = bf16[512,1024]{1,0:T(8,128)(2,1)} collective-permute-done((bf16[512,1024]{1,0:T(8,128)(2,1)}, bf16[512,1024]{1,0:T(8,128)(2,1)}, u32[]{:S(2)}, u32[]{:S(2)}) %collective-permute-start.8) | collective-permute-done | bytes 1048608 | tf_op jit(solution)/shard_map/ppermute | solution.py:64
  361.5 18.7 %collective-permute-done.6 = bf16[512,1024]{1,0:T(8,128)(2,1)} collective-permute-done((bf16[512,1024]{1,0:T(8,128)(2,1)}, bf16[512,1024]{1,0:T(8,128)(2,1)}, u32[]{:S(2)}, u32[]{:S(2)}) %collective-permute-start.6) | collective-permute-done | bytes 1048608 | tf_op jit(solution)/shard_map/ppermute | solution.py:64
  393.0 9.2 fusion.15
  413.6 8.5 fusion.27
  442.2 9.2 fusion.20
  453.3 9.9 %all-to-all-done.5 = bf16[8,96,1024]{2,1,0:T(8,128)(2,1)} async-done(((bf16[8,96,1024]{2,1,0:T(8,128)(2,1)}), bf16[8,96,1024]{2,1,0:T(8,128)(2,1)}, u32[]{:S(2)}, u32[]{:S(2)}) %all-to-all-start.5) | async-done | bytes 1572896 | tf_op jit(solution)/shard_map/all_to_all | solution.py:553
  468.0 8.5 fusion.29
  498.6 11.3 %fusion.35 = f32[1024,1024]{1,0:T(8,128)} fusion(bf16[768,2048]{1,0:T(8,128)(2,1)S(1)} %copy-done.70, bf16[768,2048]{1,0:T(8,128)(2,1)S(1)} %copy-done.68, bf16[768,1024]{1,0:T(8,128)(2,1)} %bitcast.27, bf16[768,1024]{1,0:T(8,128)(2,1)} %bitcast.20), kind=kOutput, calls=%fused_computation.74 | convolution fusion | flops 3233808384 | bytes 13631488 | tf_op jit(solution)/shard_map/dot_general | solution.py:39
  545.8 38.7 %collective-permute-done.9 = bf16[512,1024]{1,0:T(8,128)(2,1)S(1)} collective-permute-done((bf16[512,1024]{1,0:T(8,128)(2,1)S(1)}, bf16[512,1024]{1,0:T(8,128)(2,1)S(1)}, u32[]{:S(2)}, u32[]{:S(2)}) %collective-permute-start.9) | collective-permute-done | bytes 1048608 | tf_op jit(solution)/shard_map/ppermute | solution.py:64
  592.5 46.2 %collective-permute-done.7 = bf16[512,1024]{1,0:T(8,128)(2,1)S(1)} collective-permute-done((bf16[512,1024]{1,0:T(8,128)(2,1)S(1)}, bf16[512,1024]{1,0:T(8,128)(2,1)S(1)}, u32[]{:S(2)}, u32[]{:S(2)}) %collective-permute-start.7) | collective-permute-done | bytes 1048608 | tf_op jit(solution)/shard_map/ppermute | solution.py:64
  647.3 14.8 %multiply_convert_fusion = bf16[512,4096]{1,0:T(8,128)(2,1)} fusion(bf16[512,4096]{1,0:T(8,128)(2,1)} %get-tuple-element.54, bf16[4096,1024]{1,0:T(8,128)(2,1)} %bitcast.274, f32[512,1024]{1,0:T(8,128)} %copy-done.22), kind=kOutput, calls=%fused_computation.21 | convolution fusion | flops 4301783040 | bytes 18874368 | tf_op jit(solution)/shard_map/dot_general | solution.py:35
  678.0 7.7 multiply_reduce_fusion.4
  705.6 9.2 collective-permute-done.11
  745.2 21.4 %shard_map.214 = (bf16[4,2,256,256]{3,2,1,0:T(8,128)(2,1)S(1)}, bf16[4,2,256,256]{3,2,1,0:T(8,128)(2,1)S(1)}, bf16[4,2,256,256]{3,2,1,0:T(8,128)(2,1)S(1)}) custom-call(bf16[4,2,256,768]{3,2,1,0:T(8,128)(2,1)} %bitcast.199, bf16[4,2,256,768]{3,2,1,0:T(8,128)(2,1)} %bitcast.200, bf16[4,2,256,768]{3,2,1,0:T(8,128)(2,1)} %bitcast.201, ...), custom_call_target="tpu_custom_call" | custom-call | flops 8000000000 | bytes 12582912 | tf_op jit(solution)/shard_map/pallas_call | solution.py:206
  766.9 8.7 collective-permute-done.15
  819.9 34.4 %collective-permute-done.35 = bf16[1024,1024]{1,0:T(8,128)(2,1)} collective-permute-done((bf16[1024,1024]{1,0:T(8,128)(2,1)}, bf16[1024,1024]{1,0:T(8,128)(2,1)}, u32[]{:S(2)}, u32[]{:S(2)}) %collective-permute-start.35) | collective-permute-done | bytes 2097184 | tf_op jit(solution)/shard_map/ppermute | solution.py:69
  864.6 23.7 %collective-permute-done.30 = bf16[4,1,1,1,128,1024]{5,4,3,2,1,0:T(8,128)(2,1)S(1)} collective-permute-done((bf16[4,1,1,1,128,1024]{5,4,3,2,1,0:T(8,128)(2,1)}, bf16[4,1,1,1,128,1024]{5,4,3,2,1,0:T(8,128)(2,1)S(1)}, u32[]{:S(2)}, u32[]{:S(2)}) %collective-permute-start.30) | collective-permute-done | bytes 1048608 | tf_op jit(solution)/shard_map/ppermute | solution.py:220
  888.2 22.9 %collective-permute-start.29 = (bf16[32,4096]{1,0:T(8,128)(2,1)S(1)}, bf16[32,4096]{1,0:T(8,128)(2,1)S(1)}, u32[]{:S(2)}, u32[]{:S(2)}) collective-permute-start(bf16[32,4096]{1,0:T(8,128)(2,1)S(1)} %get-tuple-element.118), channel_id=1, source_target_pairs={{0,24},{8,0},{16,8},{24,16},{1,25},{9,1},{17,9},{25,17},{2,26},{10... | collective-permute-start | bytes 786440 | tf_op jit(solution)/shard_map/ppermute | solution.py:64
  924.4 16.6 %collective-permute-done.21 = bf16[4,1,2,1,40,1792]{5,4,3,2,1,0:T(8,128)(2,1)S(1)} collective-permute-done((bf16[4,1,2,1,40,1792]{5,4,3,2,1,0:T(8,128)(2,1)S(1)}, bf16[4,1,2,1,40,1792]{5,4,3,2,1,0:T(8,128)(2,1)S(1)}, u32[]{:S(2)}, u32[]{:S(2)}) %collective-permute-start.21) | collective-permute-done | bytes 1146912 | tf_op jit(solution)/shard_map/ppermute | solution.py:220
  943.7 11.7 %collective-permute-done.22 = bf16[4,1,1,1,40,1792]{5,4,3,2,1,0:T(8,128)(2,1)S(1)} collective-permute-done((bf16[4,1,1,1,40,1792]{5,4,3,2,1,0:T(8,128)(2,1)S(1)}, bf16[4,1,1,1,40,1792]{5,4,3,2,1,0:T(8,128)(2,1)S(1)}, u32[]{:S(2)}, u32[]{:S(2)}) %collective-permute-start.22) | collective-permute-done | bytes 573472 | tf_op jit(solution)/shard_map/ppermute | solution.py:220
  (418 shorter events, 361.6 us)
Async XLA Ops:
  231.3 158.7 %collective-permute-start.3 = (bf16[1024,1024]{1,0:T(8,128)(2,1)}, bf16[1024,1024]{1,0:T(8,128)(2,1)}, u32[]{:S(2)}, u32[]{:S(2)}) collective-permute-start(bf16[1024,1024]{1,0:T(8,128)(2,1)} %bitcast.21), channel_id=1, source_target_pairs={{0,8},{8,0},{16,24},{24,16},{1,9},{9,1},{17,25},{25,17},{2,10},{10... | collective-permute-start | bytes 6291464 | tf_op jit(solution)/shard_map/ppermute | solution.py:69
  231.9 170.3 %collective-permute-start.4 = (bf16[1024,1024]{1,0:T(8,128)(2,1)}, bf16[1024,1024]{1,0:T(8,128)(2,1)}, u32[]{:S(2)}, u32[]{:S(2)}) collective-permute-start(bf16[1024,1024]{1,0:T(8,128)(2,1)} %bitcast.22), channel_id=1, source_target_pairs={{0,8},{8,0},{16,24},{24,16},{1,9},{9,1},{17,25},{25,17},{2,10},{10... | collective-permute-start | bytes 6291464 | tf_op jit(solution)/shard_map/ppermute | solution.py:69
  243.7 91.8 %collective-permute-start.5 = (s32[512]{0:T(512)}, s32[512]{0:T(512)}, u32[]{:S(2)}, u32[]{:S(2)}) collective-permute-start(s32[512]{0:T(512)} %convert_add_fusion.6), channel_id=1, source_target_pairs={{0,16},{8,24},{16,0},{24,8},{1,17},{9,25},{17,1},{25,9},{2,18},{10... | collective-permute-start | bytes 6152 | tf_op jit(solution)/shard_map/ppermute | solution.py:64
  248.9 109.1 %collective-permute-start.8 = (bf16[512,1024]{1,0:T(8,128)(2,1)}, bf16[512,1024]{1,0:T(8,128)(2,1)}, u32[]{:S(2)}, u32[]{:S(2)}) collective-permute-start(bf16[512,1024]{1,0:T(8,128)(2,1)} %bitcast.244), channel_id=1, source_target_pairs={{0,16},{8,24},{16,0},{24,8},{1,17},{9,25},{17,1},{25,9},{2,18},{10... | collective-permute-start | bytes 3145736 | tf_op jit(solution)/shard_map/ppermute | solution.py:64
  273.5 110.2 %all-to-all-start = ((bf16[8,96,1024]{2,1,0:T(8,128)(2,1)}), bf16[8,96,1024]{2,1,0:T(8,128)(2,1)}, u32[]{:S(2)}, u32[]{:S(2)}) async-start(bf16[8,96,1024]{2,1,0:T(8,128)(2,1)} %bitcast.236), calls=%async_computation | async-start | bytes 3145728 | tf_op jit(solution)/shard_map/all_to_all | solution.py:553
  281.2 99.0 %collective-permute-start.6 = (bf16[512,1024]{1,0:T(8,128)(2,1)}, bf16[512,1024]{1,0:T(8,128)(2,1)}, u32[]{:S(2)}, u32[]{:S(2)}) collective-permute-start(bf16[512,1024]{1,0:T(8,128)(2,1)} %copy-done.39), channel_id=1, source_target_pairs={{0,16},{8,24},{16,0},{24,8},{1,17},{9,25},{17,1},{25,9},{2,18},{10... | collective-permute-start | bytes 3145736 | tf_op jit(solution)/shard_map/ppermute | solution.py:64
  409.0 28.8 %all-to-all-start.1 = ((bf16[8,96,1024]{2,1,0:T(8,128)(2,1)}), bf16[8,96,1024]{2,1,0:T(8,128)(2,1)}, u32[]{:S(2)}, u32[]{:S(2)}) async-start(bf16[8,96,1024]{2,1,0:T(8,128)(2,1)} %bitcast.237), calls=%async_computation.1 | async-start | bytes 3145728 | tf_op jit(solution)/shard_map/all_to_all | solution.py:553
  516.7 69.5 %all-to-all-start.2 = ((bf16[8,192,1024]{2,1,0:T(8,128)(2,1)}), bf16[8,192,1024]{2,1,0:T(8,128)(2,1)}, u32[]{:S(2)}, u32[]{:S(2)}) async-start(bf16[8,192,1024]{2,1,0:T(8,128)(2,1)} %pad_maximum_fusion.3), calls=%async_computation.2 | async-start | bytes 6291456 | tf_op jit(solution)/shard_map/all_to_all | solution.py:553
  534.9 49.7 %collective-permute-start.9 = (bf16[512,1024]{1,0:T(8,128)(2,1)S(1)}, bf16[512,1024]{1,0:T(8,128)(2,1)S(1)}, u32[]{:S(2)}, u32[]{:S(2)}) collective-permute-start(bf16[512,1024]{1,0:T(8,128)(2,1)S(1)} %fusion.65), channel_id=1, source_target_pairs={{0,16},{8,24},{16,0},{24,8},{1,17},{9,25},{17,1},{25,9},{2,18},{10... | collective-permute-start | bytes 3145736 | tf_op jit(solution)/shard_map/ppermute | solution.py:64
  590.3 48.4 %collective-permute-start.7 = (bf16[512,1024]{1,0:T(8,128)(2,1)S(1)}, bf16[512,1024]{1,0:T(8,128)(2,1)S(1)}, u32[]{:S(2)}, u32[]{:S(2)}) collective-permute-start(bf16[512,1024]{1,0:T(8,128)(2,1)S(1)} %fusion.64), channel_id=1, source_target_pairs={{0,16},{8,24},{16,0},{24,8},{1,17},{9,25},{17,1},{25,9},{2,18},{10... | collective-permute-start | bytes 3145736 | tf_op jit(solution)/shard_map/ppermute | solution.py:64
  664.7 50.3 %collective-permute-start.13 = (bf16[4,2,2,1,128,1024]{5,4,3,2,1,0:T(8,128)(2,1)}, bf16[4,2,2,1,128,1024]{5,4,3,2,1,0:T(8,128)(2,1)}, u32[]{:S(2)}, u32[]{:S(2)}) collective-permute-start(bf16[4,2,2,1,128,1024]{5,4,3,2,1,0:T(8,128)(2,1)} %constant_dynamic-slice_fusion.7), channel_id=1, source_target_pairs={{0,1},{1,0},{2,3},{3,2},{4,5},{5,4},{6,7},{7,6},{8,9},{9,8},{10,11... | collective-permute-start | bytes 12582920 | tf_op jit(solution)/shard_map/ppermute | solution.py:220
  677.5 43.2 %collective-permute-start.14 = (bf16[4,2,2,1,32,4096]{5,4,3,2,1,0:T(8,128)(2,1)}, bf16[4,2,2,1,32,4096]{5,4,3,2,1,0:T(8,128)(2,1)}, u32[]{:S(2)}, u32[]{:S(2)}) collective-permute-start(bf16[4,2,2,1,32,4096]{5,4,3,2,1,0:T(8,128)(2,1)} %constant_dynamic-slice_fusion.6), channel_id=1, source_target_pairs={{0,1},{1,0},{2,3},{3,2},{4,5},{5,4},{6,7},{7,6},{8,9},{9,8},{10,11... | collective-permute-start | bytes 12582920 | tf_op jit(solution)/shard_map/ppermute | solution.py:220
  727.8 47.8 %collective-permute-start.15 = (bf16[4,2,1,1,128,1024]{5,4,3,2,1,0:T(8,128)(2,1)}, bf16[4,2,1,1,128,1024]{5,4,3,2,1,0:T(8,128)(2,1)}, u32[]{:S(2)}, u32[]{:S(2)}) collective-permute-start(bf16[4,2,1,1,128,1024]{5,4,3,2,1,0:T(8,128)(2,1)} %constant_dynamic-slice_fusion.5), channel_id=1, source_target_pairs={{0,2},{1,3},{2,0},{3,1},{4,6},{5,7},{6,4},{7,5},{8,10},{9,11},{10,... | collective-permute-start | bytes 6291464 | tf_op jit(solution)/shard_map/ppermute | solution.py:220
  730.7 47.5 %collective-permute-start.16 = (bf16[4,1,2,1,32,4096]{5,4,3,2,1,0:T(8,128)(2,1)}, bf16[4,1,2,1,32,4096]{5,4,3,2,1,0:T(8,128)(2,1)}, u32[]{:S(2)}, u32[]{:S(2)}) collective-permute-start(bf16[4,1,2,1,32,4096]{5,4,3,2,1,0:T(8,128)(2,1)} %constant_dynamic-slice_fusion.4), channel_id=1, source_target_pairs={{0,4},{1,5},{2,6},{3,7},{4,0},{5,1},{6,2},{7,3},{8,12},{9,13},{10,... | collective-permute-start | bytes 6291464 | tf_op jit(solution)/shard_map/ppermute | solution.py:220
  734.0 85.9 %collective-permute-start.34 = (bf16[1024,1024]{1,0:T(8,128)(2,1)}, bf16[1024,1024]{1,0:T(8,128)(2,1)}, u32[]{:S(2)}, u32[]{:S(2)}) collective-permute-start(bf16[1024,1024]{1,0:T(8,128)(2,1)} %fusion.53), channel_id=1, source_target_pairs={{0,8},{8,0},{16,24},{24,16},{1,9},{9,1},{17,25},{25,17},{2,10},{10... | collective-permute-start | bytes 6291464 | tf_op jit(solution)/shard_map/ppermute | solution.py:69
  740.1 114.2 %collective-permute-start.35 = (bf16[1024,1024]{1,0:T(8,128)(2,1)}, bf16[1024,1024]{1,0:T(8,128)(2,1)}, u32[]{:S(2)}, u32[]{:S(2)}) collective-permute-start(bf16[1024,1024]{1,0:T(8,128)(2,1)} %fusion.56), channel_id=1, source_target_pairs={{0,8},{8,0},{16,24},{24,16},{1,9},{9,1},{17,25},{25,17},{2,10},{10... | collective-permute-start | bytes 6291464 | tf_op jit(solution)/shard_map/ppermute | solution.py:69
  793.8 121.1 %collective-permute-start.19 = (bf16[512,1024]{1,0:T(8,128)(2,1)}, bf16[512,1024]{1,0:T(8,128)(2,1)}, u32[]{:S(2)}, u32[]{:S(2)}) collective-permute-start(bf16[512,1024]{1,0:T(8,128)(2,1)} %get-tuple-element.102), channel_id=1, source_target_pairs={{0,24},{8,0},{16,8},{24,16},{1,25},{9,1},{17,9},{25,17},{2,26},{10... | collective-permute-start | bytes 3145736 | tf_op jit(solution)/shard_map/ppermute | solution.py:64
  797.2 117.9 %collective-permute-start.18 = (bf16[512,1024]{1,0:T(8,128)(2,1)}, bf16[512,1024]{1,0:T(8,128)(2,1)}, u32[]{:S(2)}, u32[]{:S(2)}) collective-permute-start(bf16[512,1024]{1,0:T(8,128)(2,1)} %get-tuple-element.103), channel_id=1, source_target_pairs={{0,16},{8,24},{16,0},{24,8},{1,17},{9,25},{17,1},{25,9},{2,18},{10... | collective-permute-start | bytes 3145736 | tf_op jit(solution)/shard_map/ppermute | solution.py:64
  815.2 47.3 %collective-permute-start.26 = (bf16[4,1,1,1,32,4096]{5,4,3,2,1,0:T(8,128)(2,1)}, bf16[4,1,1,1,32,4096]{5,4,3,2,1,0:T(8,128)(2,1)}, u32[]{:S(2)}, u32[]{:S(2)}) collective-permute-start(bf16[4,1,1,1,32,4096]{5,4,3,2,1,0:T(8,128)(2,1)} %constant_dynamic-slice_fusion.1), channel_id=1, source_target_pairs={{0,2},{1,3},{2,0},{3,1},{4,6},{5,7},{6,4},{7,5},{8,10},{9,11},{10,... | collective-permute-start | bytes 3145736 | tf_op jit(solution)/shard_map/ppermute | solution.py:220
  819.9 95.7 %collective-permute-start.17 = (bf16[512,1024]{1,0:T(8,128)(2,1)}, bf16[512,1024]{1,0:T(8,128)(2,1)}, u32[]{:S(2)}, u32[]{:S(2)}) collective-permute-start(bf16[512,1024]{1,0:T(8,128)(2,1)} %get-tuple-element.101), channel_id=1, source_target_pairs={{0,8},{8,16},{16,24},{24,0},{1,9},{9,17},{17,25},{25,1},{2,10},{10... | collective-permute-start | bytes 3145736 | tf_op jit(solution)/shard_map/ppermute | solution.py:64
  854.3 57.3 %collective-permute-start.20 = (bf16[4,2,2,1,40,1792]{5,4,3,2,1,0:T(8,128)(2,1)}, bf16[4,2,2,1,40,1792]{5,4,3,2,1,0:T(8,128)(2,1)}, u32[]{:S(2)}, u32[]{:S(2)}) collective-permute-start(bf16[4,2,2,1,40,1792]{5,4,3,2,1,0:T(8,128)(2,1)} %fusion.39), channel_id=1, source_target_pairs={{0,1},{1,0},{2,3},{3,2},{4,5},{5,4},{6,7},{7,6},{8,9},{9,8},{10,11... | collective-permute-start | bytes 6881288 | tf_op jit(solution)/shard_map/ppermute | solution.py:220
  888.2 53.1 %collective-permute-start.29 = (bf16[32,4096]{1,0:T(8,128)(2,1)S(1)}, bf16[32,4096]{1,0:T(8,128)(2,1)S(1)}, u32[]{:S(2)}, u32[]{:S(2)}) collective-permute-start(bf16[32,4096]{1,0:T(8,128)(2,1)S(1)} %get-tuple-element.118), channel_id=1, source_target_pairs={{0,24},{8,0},{16,8},{24,16},{1,25},{9,1},{17,9},{25,17},{2,26},{10... | collective-permute-start | bytes 786440 | tf_op jit(solution)/shard_map/ppermute | solution.py:64
  915.1 27.8 %collective-permute-start.27 = (bf16[32,4096]{1,0:T(8,128)(2,1)S(1)}, bf16[32,4096]{1,0:T(8,128)(2,1)S(1)}, u32[]{:S(2)}, u32[]{:S(2)}) collective-permute-start(bf16[32,4096]{1,0:T(8,128)(2,1)S(1)} %get-tuple-element.117), channel_id=1, source_target_pairs={{0,8},{8,16},{16,24},{24,0},{1,9},{9,17},{17,25},{25,1},{2,10},{10... | collective-permute-start | bytes 786440 | tf_op jit(solution)/shard_map/ppermute | solution.py:64
  915.6 42.8 %collective-permute-start.33 = (bf16[128,1024]{1,0:T(8,128)(2,1)S(1)}, bf16[128,1024]{1,0:T(8,128)(2,1)S(1)}, u32[]{:S(2)}, u32[]{:S(2)}) collective-permute-start(bf16[128,1024]{1,0:T(8,128)(2,1)S(1)} %get-tuple-element.115), channel_id=1, source_target_pairs={{0,24},{8,0},{16,8},{24,16},{1,25},{9,1},{17,9},{25,17},{2,26},{10... | collective-permute-start | bytes 786440 | tf_op jit(solution)/shard_map/ppermute | solution.py:64
  (98 other events, 1209.2 us)

commit v2 on v1

--- a/solution.py
+++ b/solution.py
@@ -194,7 +194,7 @@
         ],
         scratch_shapes=[pltpu.VMEM((length, LANES), F32)],
         compiler_params=pltpu.CompilerParams(vmem_limit_bytes=40 * 2**20),
-        cost_estimate=pl.CostEstimate(flops=3 * 10**9, bytes_accessed=8 * 2**20, transcendentals=10**7),
+        cost_estimate=pl.CostEstimate(flops=10**6, bytes_accessed=2**16, transcendentals=0),
     )(projected, projected, projected, id_rows, id_cols)
 
 
@@ -211,7 +211,7 @@
         out_shape=[shape] * 3,
         scratch_shapes=[pltpu.VMEM((length, LANES), F32)] * 3,
         compiler_params=pltpu.CompilerParams(vmem_limit_bytes=48 * 2**20),
-        cost_estimate=pl.CostEstimate(flops=8 * 10**9, bytes_accessed=12 * 2**20, transcendentals=10**7),
+        cost_estimate=pl.CostEstimate(flops=10**6, bytes_accessed=2**16, transcendentals=0),
     )(projected, projected, projected, grads, lse_rows, id_rows, id_cols)
 
 
@@ -248,7 +248,28 @@
 
 def by_device(term):
     seq_size, fsdp_size = lax.axis_size("seq"), lax.axis_size("fsdp")
-    return term.astype(BF).reshape(seq_size, fsdp_size, -1, term.shape[-1])
+    depth = term.shape[0] // (seq_size * fsdp_size)
+    tile = (depth, term.shape[1]) if depth % 16 == 0 else (16, depth * term.shape[1] // 16)
+    return term.astype(BF).reshape(seq_size, fsdp_size, *tile)
+
+
+def gather_plan(seq_size, count):
+    plan = [("send", 0), ("send", 1), ("own",)]
+    for hop in range(1, seq_size):
+        plan += [("proj", hop), ("arrive", 0, hop), ("arrive", 1, hop)]
+        if hop == 1:
+            plan += [("send", 2)]
+        if hop < seq_size - 1:
+            plan += [("go", hop - 1, 0)]
+    last = seq_size - 1
+    rest = [("go", 0, 1), ("go", last - 1, 0), ("go", 1, 1), ("go", last, 0)]
+    rest += [("go", hop, step) for step in range(1, count - 1) for hop in range(2 if step == 1 else 0, seq_size)]
+    plan += [("arrive", 2, 1), *rest[:4]]
+    rest = rest[4:]
+    share = -(-len(rest) // max(1, seq_size - 2))
+    for hop in range(2, seq_size):
+        plan += [("arrive", 2, hop), *rest[(hop - 2) * share : (hop - 1) * share]]
+    return plan + [("go", hop, count - 1) for hop in range(seq_size)]
 
 
 def gather_kernel(seq_size, bits, proj_ref, in_ref, out_ref, x_ref, proj_all, in_all, out_all, x_all, *sems):
@@ -369,48 +390,48 @@
         copy.start()
     for step in range(1, seq_size):
         proj(step).start()
-    for index in range(3):
+    def send_own(index):
         for side in (0, 1):
 
             @pl.when(has_next(side))
-            def _(index=index, side=side):
+            def _(side=side):
                 line(index, side, 1).start()
 
-    for copy in owns:
-        copy.wait()
-    each_block(0, lambda index, s, turn: cube(index, s, turn, 0).start())
-
-    def advance(hop):
-        for step in range(1, count):
-
-            def act(index, s, turn, step=step):
-                cube(index, s, turn, step - 1).wait()
-                cube(index, s, turn, step).start()
-
-            each_block(hop, act)
-
-    for hop in range(1, seq_size):
-        advance(hop - 1)
+    def arrive(index, hop):
+        for side in (0, 1):
+
+            @pl.when(has_block(side, hop))
+            def _(side=side):
+                line_wait(index, side, hop)
+                if hop < seq_size - 1:
+
+                    @pl.when(has_next(side))
+                    def _():
+                        line(index, side, hop + 1).start()
+
+                if index < 2:
+                    cube(index + 1, z - (1 - 2 * side) * hop, turn_of(side, hop), 0).start()
+
+    def go_on(hop, step):
+        def act(index, s, turn):
+            cube(index, s, turn, step).wait()
+            if step + 1 < count:
+                cube(index, s, turn, step + 1).start()
+
+        each_block(hop, act)
+
+    def proj_arrive(hop):
         proj_wait(hop)
         cube(0, lax.rem(z + seq_size - hop, seq_size), turn_of(0, hop), 0).start()
-        for index in range(3):
-            for side in (0, 1):
-
-                @pl.when(has_block(side, hop))
-                def _(index=index, side=side, hop=hop):
-                    line_wait(index, side, hop)
-                    if hop < seq_size - 1:
-
-                        @pl.when(has_next(side))
-                        def _():
-                            line(index, side, hop + 1).start()
-
-                    if index < 2:
-                        cube(index + 1, z - (1 - 2 * side) * hop, turn_of(side, hop), 0).start()
-
-    advance(seq_size - 1)
-    for hop in range(seq_size):
-        each_block(hop, lambda index, s, turn: cube(index, s, turn, count - 1).wait())
+
+    def own_cubes():
+        for copy in owns:
+            copy.wait()
+        each_block(0, lambda index, s, turn: cube(index, s, turn, 0).start())
+
+    acts = {"send": send_own, "own": own_cubes, "proj": proj_arrive, "arrive": arrive, "go": go_on}
+    for name, *values in gather_plan(seq_size, count):
+        acts[name](*values)
     for step in range(1, seq_size):
         proj(step).wait_send()
     for index in range(3):
@@ -435,7 +456,7 @@
     anywhere = pl.BlockSpec(memory_space=pl.ANY)
     outs = pl.pallas_call(
         functools.partial(gather_kernel, seq_size, bits),
-        in_specs=[anywhere] * 4,
+        in_specs=[pl.BlockSpec(memory_space=pltpu.VMEM)] * 4,
         out_specs=[anywhere] * 4,
         out_shape=[
             whole(proj.shape[1:]),
@@ -465,6 +486,264 @@
     )
 
 
+def add_into(target, index, term, rows=64):
+    depth = target.shape[-2]
+    rows = next(n for n in (rows, 48, 32, 16, depth) if depth % n == 0)
+    lead = target.shape[len(index) : -2]
+    count = 1
+    for size in lead:
+        count *= size
+
+    def step(i, carry):
+        block, place = i // (depth // rows), pl.multiple_of((i % (depth // rows)) * rows, rows)
+        where = []
+        for size in reversed(lead):
+            where.insert(0, block % size)
+            block = block // size
+        at = (*where, pl.ds(place, rows), slice(None))
+        left = target[(*index, *at)].astype(F32)
+        target[(*index, *at)] = (left + term(at).astype(F32)).astype(target.dtype)
+        return carry
+
+    lax.fori_loop(0, count * (depth // rows), step, 0)
+
+
+def finish_kernel(seq_size, bits, da_ref, in_ref, out_ref, proj_ref, *refs):
+    count = len(bits)
+    da_out, in_out, out_out, proj_out = refs[:4]
+    da_line, in_line, out_line, in_half, out_half = refs[4:9]
+    proj_parts = refs[9 : 9 + count]
+    own_sem, line_send, line_recv, half_send, half_recv, cube_send, cube_recv, proj_send, proj_recv = refs[9 + count :]
+    z = lax.axis_index("seq")
+    f = lax.axis_index("fsdp")
+    bit_of = {bit: (f // bit) % 2 for bit in bits}
+    mesh_id = pl.DeviceIdType.MESH
+    last = seq_size - 1
+
+    def flipped(bit):
+        return {"fsdp": f + bit * (1 - 2 * bit_of[bit])}
+
+    barrier = pltpu.get_barrier_semaphore()
+    for step in range(1, seq_size):
+        pl.semaphore_signal(barrier, inc=1, device_id={"seq": lax.rem(z + step, seq_size)}, device_id_type=mesh_id)
+    for bit in bits:
+        pl.semaphore_signal(barrier, inc=1, device_id=flipped(bit), device_id_type=mesh_id)
+    pl.semaphore_wait(barrier, seq_size - 1 + count)
+
+    lines = ((da_ref, da_line, da_out), (in_half, in_line, in_out), (out_half, out_line, out_out))
+
+    def line(index, side, hop, own):
+        terms, sums, _ = lines[index]
+        if own:
+            source = terms.at[seq_size - hop if side == 0 else hop - 1]
+        else:
+            source = sums.at[side, hop - 2]
+        return pltpu.make_async_remote_copy(
+            src_ref=source,
+            dst_ref=sums.at[side, hop - 1],
+            send_sem=line_send.at[index, side, hop - 1],
+            recv_sem=line_recv.at[index, side, hop - 1],
+            device_id={"seq": z + 1 - 2 * side},
+            device_id_type=mesh_id,
+        )
+
+    def at_end(side):
+        return z == 0 if side == 0 else z == last
+
+    def from_end(side):
+        return z if side == 0 else last - z
+
+    def send_own(index):
+        for side in (0, 1):
+
+            @pl.when(at_end(side))
+            def _(side=side):
+                for hop in range(1, seq_size):
+                    line(index, side, hop, True).start()
+
+    def arrive(index, hop):
+        terms, sums, _ = lines[index]
+        for side in (0, 1):
+
+            @pl.when((from_end(side) >= 1) & (from_end(side) <= hop))
+            def _(side=side):
+                pltpu.make_async_remote_copy(
+                    src_ref=sums.at[side, hop - 1],
+                    dst_ref=sums.at[side, hop - 1],
+                    send_sem=line_send.at[index, side, hop - 1],
+                    recv_sem=line_recv.at[index, side, hop - 1],
+                    device_id={"seq": z - 1 + 2 * side},
+                    device_id_type=mesh_id,
+                ).wait_recv()
+                if hop < last:
+                    target = z - 1 + seq_size - hop if side == 0 else hop - last + z
+                    add_into(sums, (side, hop - 1), lambda at: terms[(target, *at)])
+                    line(index, side, hop + 1, False).start()
+
+    def total(index):
+        terms, sums, result = lines[index]
+        add_first(result, lambda at: terms[(z, *at)])
+        for side in (0, 1):
+
+            @pl.when(from_end(side) >= 1)
+            def _(side=side):
+                add_into(result, (), lambda at: sums[(side, last - 1, *at)])
+
+    def add_first(result, term):
+        depth = result.shape[0]
+        rows = next(n for n in (64, 32, 16, depth) if depth % n == 0)
+
+        def step(i, carry):
+            at = (pl.ds(pl.multiple_of(i * rows, rows), rows), slice(None))
+            result[at] = term(at).astype(F32)
+            return carry
+
+        lax.fori_loop(0, depth // rows, step, 0)
+
+    halves = ((in_ref, in_half, bits[0]), (out_ref, out_half, bits[-2] if count > 1 else bits[0]))
+
+    def half(index):
+        source, target, bit = halves[index]
+        return pltpu.make_async_remote_copy(
+            src_ref=source.at[:, 1 - bit_of[bit]],
+            dst_ref=target,
+            send_sem=half_send.at[index],
+            recv_sem=half_recv.at[index],
+            device_id=flipped(bit),
+            device_id_type=mesh_id,
+        )
+
+    def half_add(index):
+        source, target, bit = halves[index]
+        half(index).wait()
+        add_into(target, (), lambda at: source[(at[0], bit_of[bit], *at[1:])])
+
+    order = bits[::-1]
+
+    def cube(step):
+        source = proj_ref if step == 0 else proj_parts[step - 1]
+        left = sorted(order[step:], reverse=True)
+        where = left.index(order[step])
+        view = source.at[(slice(None),) * (1 + where) + (1 - bit_of[order[step]],)]
+        return pltpu.make_async_remote_copy(
+            src_ref=view,
+            dst_ref=proj_parts[step],
+            send_sem=cube_send.at[step],
+            recv_sem=cube_recv.at[step],
+            device_id=flipped(order[step]),
+            device_id_type=mesh_id,
+        )
+
+    def cube_add(step):
+        source = proj_ref if step == 0 else proj_parts[step - 1]
+        left = sorted(order[step:], reverse=True)
+        where = 1 + left.index(order[step])
+        cube(step).wait()
+        add_into(proj_parts[step], (), lambda at: source[(*at[:where], bit_of[order[step]], *at[where:])])
+
+    def proj(step):
+        to = lax.rem(z + step, seq_size)
+        return pltpu.make_async_remote_copy(
+            src_ref=proj_parts[-1].at[to],
+            dst_ref=proj_out.at[z],
+            send_sem=proj_send.at[step - 1],
+            recv_sem=proj_recv.at[step - 1],
+            device_id={"seq": to},
+            device_id_type=mesh_id,
+        )
+
+    def proj_wait(step):
+        view = proj_out.at[lax.rem(z + seq_size - step, seq_size)]
+        copy = pltpu.make_async_remote_copy(
+            src_ref=view,
+            dst_ref=view,
+            send_sem=proj_send.at[step - 1],
+            recv_sem=proj_recv.at[step - 1],
+            device_id={"seq": lax.rem(z + step, seq_size)},
+            device_id_type=mesh_id,
+        )
+        copy.wait_recv()
+
+    send_own(0)
+    half(0).start()
+    half(1).start()
+    cube(0).start()
+    cube_add(0)
+    cube(1).start() if count > 1 else None
+    half_add(0)
+    half_add(1)
+    send_own(1)
+    send_own(2)
+    for hop in range(1, seq_size):
+        arrive(0, hop)
+        if hop < count:
+            cube_add(hop)
+            if hop + 1 < count:
+                cube(hop + 1).start()
+        if hop == min(count, last) - 1 or (count == 1 and hop == 1):
+            own = pltpu.make_async_copy(proj_parts[-1].at[z], proj_out.at[z], own_sem)
+            own.start()
+            for step in range(1, seq_size):
+                proj(step).start()
+    total(0)
+    for hop in range(1, seq_size):
+        arrive(1, hop)
+        arrive(2, hop)
+    total(1)
+    total(2)
+    pltpu.make_async_copy(proj_parts[-1].at[z], proj_out.at[z], own_sem).wait()
+    for step in range(1, seq_size):
+        proj_wait(step)
+        proj(step).wait_send()
+    for index in range(3):
+        for side in (0, 1):
+            for hop in range(1, seq_size):
+
+                @pl.when(at_end(side) | ((from_end(side) >= 1) & (from_end(side) <= hop - 1)))
+                def _(index=index, side=side, hop=hop):
+                    line(index, side, hop, True).wait_send()
+
+
+def finish_sums(da, ffin, ffout, proj):
+    seq_size = lax.axis_size("seq")
+    bits = fsdp_bits(False)
+    count = len(bits)
+    dma = pltpu.SemaphoreType.DMA
+    inside = pl.BlockSpec(memory_space=pltpu.VMEM)
+
+    def line_of(shape):
+        return pltpu.VMEM((2, seq_size - 1, *shape), BF)
+
+    order = bits[::-1]
+    parts = [pltpu.VMEM((seq_size, *[2] * (count - 1 - step), *proj.shape[-2:]), BF) for step in range(count)]
+    shapes = [v.shape[-2:] for v in (da, ffin, ffout)]
+    return pl.pallas_call(
+        functools.partial(finish_kernel, seq_size, bits),
+        in_specs=[inside] * 4,
+        out_specs=[inside] * 4,
+        out_shape=[jax.ShapeDtypeStruct(shape, F32) for shape in shapes]
+        + [jax.ShapeDtypeStruct((seq_size, *proj.shape[-2:]), BF)],
+        scratch_shapes=[
+            *[line_of(shape) for shape in shapes],
+            *[pltpu.VMEM((seq_size, *shape), BF) for shape in shapes[1:]],
+            *parts,
+            dma,
+            dma((3, 2, seq_size - 1)),
+            dma((3, 2, seq_size - 1)),
+            dma((2,)),
+            dma((2,)),
+            dma((len(order),)),
+            dma((len(order),)),
+            dma((seq_size - 1,)),
+            dma((seq_size - 1,)),
+        ],
+        compiler_params=pltpu.CompilerParams(
+            collective_id=1, has_side_effects=True, vmem_limit_bytes=56 * 2**20
+        ),
+        cost_estimate=pl.CostEstimate(flops=0, bytes_accessed=100 * 2**20, transcendentals=0),
+    )(da, ffin, ffout, proj)
+
+
 def whole_tiles(shard, rows=16):
     return shard if shard.shape[0] % rows == 0 else shard.reshape(rows, -1)
 
@@ -508,7 +787,8 @@
     slices = jnp.concatenate([slices, jnp.broadcast_to(out_proj[None], (seq_size, depth, width))], axis=2)
     small = jnp.concatenate([norm_gains.reshape(-1), norm_biases.reshape(-1), centroids[0]])
     spare = 32 - depth % 16 if depth % 16 else 16
-    extra = jnp.pad(small, (0, spare * wide - small.shape[0])).reshape(1, spare, wide)
+    extra = jnp.stack([jnp.pad(v, (0, wide - v.shape[0])) for v in (small, routes.reshape(tokens).astype(BF))])
+    extra = jnp.pad(extra, ((0, spare - 2), (0, 0)))[None]
     extra = jnp.broadcast_to(extra, (seq_size, spare, wide))
     bits = fsdp_bits(False)
     crossed = fsdp_bits(True)
@@ -531,20 +811,26 @@
     projected = mm(normed_flat, qkv_mine).astype(BF).reshape(seq_size, rows, span, 3 * cols)
 
     attended_mine, lse_rows = attend(projected, id_rows, id_cols)
+    win_half, wout_half = win_mine.shape[0] // 2, wout_mine.shape[0] // 2
+    pair_in_low = seq_pair(win_mine[:win_half])
+    pair_in_high = seq_pair(win_mine[win_half:])
+    attended_mine, pair_in_low, pair_in_high = lax.optimization_barrier((attended_mine, pair_in_low, pair_in_high))
     attended = seq_exchange(attended_mine).transpose(1, 2, 0, 3).reshape(tokens, width)
-
-    route = routes.reshape(tokens)
+    pair_out_low = seq_pair(after(wout_mine[:wout_half], attended))
+
+    fsdp_here = lax.axis_index("fsdp")
+    routes_all = lax.dynamic_index_in_dim(proj_all[:, :, depth + 1, :tokens], fsdp_here, 1, keepdims=False)
     later = (jnp.arange(tokens)[:, None] > jnp.arange(tokens)[None, :]).astype(BF)
-    choose = route[:, None] == jnp.arange(fsdp_size, dtype=jnp.int32)[None, :]
-    before = mm(later, choose.astype(BF))
-    slot_rank = jnp.sum(jnp.where(choose, before, 0.0), axis=1).astype(jnp.int32)
-    target = route * capacity + slot_rank
-    grad_tokens = out_grad.reshape(tokens, width)
     placings = []
     for group in range(groups):
-        slot_of = target if group == 0 else seq_shift(target, 2 * group)
-        placing = (slot_of[:, None] == jnp.arange(fsdp_size * capacity, dtype=jnp.int32)[None, :]).astype(BF)
-        placings.append(placing)
+        route = pick(routes_all, (here + seq_size - 2 * group) % seq_size).astype(jnp.int32)
+        choose = route[:, None] == jnp.arange(fsdp_size, dtype=jnp.int32)[None, :]
+        before = mm(later, choose.astype(BF))
+        slot_rank = jnp.sum(jnp.where(choose, before, 0.0), axis=1).astype(jnp.int32)
+        target = route * capacity + slot_rank
+        slots = jnp.arange(fsdp_size * capacity, dtype=jnp.int32)
+        placings.append((target[:, None] == slots[None, :]).astype(BF))
+    grad_tokens = out_grad.reshape(tokens, width)
 
     def slots_of(placing, values):
         return mm_tn(placing, values).astype(BF).reshape(fsdp_size, capacity, width)
@@ -555,13 +841,8 @@
     def tokens_of(placing, values):
         return mm(placing, values.reshape(fsdp_size * capacity, width))
 
-    grad_arrived = []
-    for group in range(groups):
-        values = grad_tokens if group == 0 else seq_shift(dr_mine, 2 * group)
-        grad_arrived.append(swap_slots(slots_of(placings[group], values)).reshape(-1, width))
-
-    win = jnp.concatenate([win_mine, seq_pair(win_mine)], axis=1)
-    wout = jnp.concatenate([wout_mine, seq_pair(wout_mine)], axis=0)
+    grad_own = swap_slots(slots_of(placings[0], grad_tokens)).reshape(-1, width)
+
 
     resid_in = tokens_in.astype(F32)
     middle = resid_in + mm(attended, out_all)
@@ -573,26 +854,42 @@
     parts_three = norm_parts(block_out)
     routed = ((block_out - parts_three[0]) * parts_three[1] * gain_rows[2] + bias_rows[2]).astype(BF)
 
-    arrived_all, dz_all, du_all, act_all, back_terms, gated_all = [], [], [], [], [], []
+    routed, pair_out_low = lax.optimization_barrier((routed, pair_out_low))
+    slots_own = slots_of(placings[0], routed)
+    pair_out_high = seq_pair(after(wout_mine[wout_half:], slots_own))
+    win = jnp.concatenate([win_mine, jnp.concatenate([pair_in_low, pair_in_high], axis=0)], axis=1)
+
+    arrived_all, dz_all, du_all, act_all, back_terms, back_slots, gated_all = [], [], [], [], [], [], []
     centroid_term = jnp.zeros((width,), F32)
     for group in range(groups):
-        values = routed if group == 0 else seq_shift(routed, 2 * group)
-        arrived = swap_slots(slots_of(placings[group], values)).reshape(-1, width)
-        gated = grad_arrived[group].astype(F32)
+        if group == 0:
+            arrived, grad_arrived = swap_slots(slots_own).reshape(-1, width), grad_own
+        else:
+            slots_here = slots_of(placings[group], after(seq_shift(routed, 2 * group), act))
+            arrived = swap_slots(slots_here).reshape(-1, width)
+            grads_here = seq_shift(after(dr_mine, slots_own), 2 * group)
+            grads_here = slots_of(placings[group], after(grads_here, slots_here))
+            grad_arrived = swap_slots(grads_here).reshape(-1, width)
         gate = jax.nn.sigmoid(mm(arrived, centroid))
-        dz = (gate[:, None] * gated).astype(BF)
         act, slope = gelu_pair(mm(arrived, win))
         act, slope = lax.optimization_barrier((act.astype(BF), slope.astype(BF)))
+        if group == 0:
+            wout = jnp.concatenate([wout_mine, pair_out_low, after(pair_out_high, act)], axis=0)
         result = mm(act, wout)
+        gated_low = (gate[:, None] * result).astype(BF).reshape(fsdp_size, capacity, width)
+        gated = grad_arrived.astype(F32)
+        dz = (gate[:, None] * gated).astype(BF)
         dl = jnp.sum(gated * result, axis=-1) * gate * (1.0 - gate)
         du = (slope.astype(F32) * mm_nt(dz, wout)).astype(BF)
         rows_grad = mm_nt(du, win) + dl[:, None] * centroid.astype(F32)
         centroid_term = centroid_term + jnp.sum(dl[:, None] * arrived.astype(F32), axis=0)
-        back = tokens_of(placings[group], swap_slots(rows_grad.astype(BF).reshape(fsdp_size, capacity, width)))
+        back = swap_slots(rows_grad.astype(BF).reshape(fsdp_size, capacity, width))
+        back_slots.append(back)
+        back = tokens_of(placings[group], back)
         if group:
             back = seq_shift(back.astype(BF), -2 * group).astype(F32)
         back_terms.append(back)
-        gated_all.append((gate[:, None] * result).astype(BF).reshape(fsdp_size, capacity, width))
+        gated_all.append(gated_low)
         arrived_all.append(arrived)
         dz_all.append(dz)
         du_all.append(du)
@@ -604,9 +901,13 @@
     out_sent = mm_tn(act[:, half:], dz).astype(BF)
     in_kept = mm_tn(arrived, du[:, :half])
     out_kept = mm_tn(act[:, :half], dz)
-    in_pair, out_pair = seq_pair(in_sent), seq_pair(out_sent)
-    back_sum, in_sent, out_sent, in_kept, out_kept = lax.optimization_barrier(
-        (sum(back_terms), in_sent, out_sent, in_kept, out_kept)
+    in_pair = seq_pair(after(in_sent, in_kept, out_kept))
+
+    gated_back = swap_slots(after(jnp.concatenate(gated_all, axis=1), *back_slots))
+    gated_back = gated_back.reshape(fsdp_size, groups, capacity, width)
+    out_terms = [tokens_of(placings[group], gated_back[:, group]) for group in range(groups)]
+    back_sum, in_sent, out_sent, in_kept, out_kept, *out_terms = lax.optimization_barrier(
+        (sum(back_terms), in_sent, out_sent, in_kept, out_kept, out_terms[0], *(v.astype(BF) for v in out_terms[1:]))
     )
 
     block_norm_grad, gain_three, bias_three = norm_back(block_out, parts_three, gain_rows[2], back_sum)
@@ -619,58 +920,58 @@
     branch = middle_grad.astype(BF)
     attended_grad = mm_nt(branch, out_all).astype(BF)
     attended_grad = attended_grad.reshape(rows, span, seq_size, cols).transpose(2, 0, 1, 3)
+    attended_grad, in_pair = lax.optimization_barrier((attended_grad, in_pair))
+    active_low, hidden_low = after((active_low, hidden_low), attended_grad)
     attended_grad = seq_exchange(attended_grad)
-
-    gated_back = swap_slots(jnp.concatenate(gated_all, axis=1)).reshape(fsdp_size, groups, capacity, width)
-    outputs = block_out
-    for group in range(groups):
-        out = tokens_of(placings[group], gated_back[:, group])
-        if group:
-            out = seq_shift(out.astype(BF), -2 * group).astype(F32)
-        outputs = outputs + out
-    outputs = outputs.astype(BF).reshape(rows, span, width)
 
     ffout_terms = hyper_split(by_device(mm_tn(active_low, block_low)))
     ffin_terms = hyper_split(by_device(mm_tn(hidden_low, hidden_grad)))
-    out_terms = mm_tn(attended, branch)
+    out_proj_term = mm_tn(attended, branch)
     ffout_terms = hyper_scatter_step(ffout_terms, crossed[-1])
     ffin_terms = hyper_scatter_step(ffin_terms, bits[-1])
     attended_grad, ffout_terms, ffin_terms = lax.optimization_barrier((attended_grad, ffout_terms, ffin_terms))
+    out_pair = seq_pair(after(out_sent, attended_grad))
+    out_terms = out_terms[:1] + [
+        seq_shift(after(out_terms[group], attended_grad), -2 * group) for group in range(1, groups)
+    ]
     ffout_terms = hyper_scatter(ffout_terms, crossed[-2:0:-1])
     ffin_terms = hyper_scatter(ffin_terms, bits[-2:0:-1])
 
     dq, dk, dv = attend_back(projected, attended_grad, lse_rows, id_rows, id_cols)
     projected_grad = jnp.concatenate([dq, dk, dv], axis=-1).reshape(seq_size * tokens, 3 * cols)
-    projected_grad, ffout_terms, ffin_terms = lax.optimization_barrier((projected_grad, ffout_terms, ffin_terms))
+    projected_grad, out_pair = lax.optimization_barrier((projected_grad, out_pair))
     normed_low_terms = mm_nt(projected_grad, qkv_mine).astype(BF)
-    normed_one_grad = seq_sum_scatter(normed_low_terms.reshape(seq_size, tokens, width))
     unit_all = (inputs_all.astype(F32) - parts_all[0]) * parts_all[1]
     terms_wide = normed_low_terms.astype(F32)
     gain_one, bias_one = jnp.sum(terms_wide * unit_all, axis=0), jnp.sum(terms_wide, axis=0)
     small_terms = jnp.stack([gain_one, gain_two, gain_three, bias_one, bias_two, bias_three])
 
-    ffout_terms = hyper_scatter_step(ffout_terms, crossed[0])
-    ffin_terms = hyper_scatter_step(ffin_terms, bits[0])
-    ffn_out_grad = seq_sum_scatter(ffout_terms.reshape(seq_size, *ffn_out.shape))
-    ffn_in_grad = seq_sum_scatter(ffin_terms.reshape(seq_size, *ffn_in.shape))
-
-    proj_terms = jnp.concatenate([mm_tn(normed_flat, projected_grad).astype(BF), out_terms.astype(BF)], axis=1)
+    proj_terms = jnp.concatenate([mm_tn(normed_flat, projected_grad).astype(BF), out_proj_term.astype(BF)], axis=1)
     proj_terms = proj_terms.reshape(seq_size, fsdp_size, depth, wide)
     small_rows = small_terms.astype(BF).reshape(6, seq_size, fsdp_size, depth).transpose(1, 2, 0, 3)
     small_rows = small_rows.reshape(seq_size, fsdp_size, 1, 6 * depth)
-    small_rows = jnp.pad(small_rows, ((0, 0), (0, 0), (0, 7), (0, wide - 6 * depth)))
+    small_rows = jnp.pad(small_rows, ((0, 0), (0, 0), (0, spare - 1), (0, wide - 6 * depth)))
+    centroid_rows = jnp.where(
+        (jnp.arange(fsdp_size) == fsdp_here)[None, :, None], centroid_term.reshape(seq_size, 1, cols), 0.0
+    )
+    small_rows = lax.dynamic_update_slice(small_rows, centroid_rows.astype(BF)[:, :, None], (0, 0, 1, 0))
     proj_terms = hyper_split(jnp.concatenate([proj_terms, small_rows], axis=2))
-    proj_terms = hyper_scatter(proj_terms, bits[::-1]).reshape(seq_size, depth + 8, wide)
-    centroid_rows = centroid_term.astype(BF).reshape(seq_size, 1, cols)
-    proj_terms = lax.dynamic_update_slice(proj_terms, centroid_rows, (0, depth + 1, 0))
-    proj_sums = seq_exchange(proj_terms).astype(F32)
+    proj_terms, *out_terms = lax.optimization_barrier((proj_terms, *out_terms))
+    outputs = block_out + sum(v.astype(F32) for v in out_terms)
+    outputs = outputs.astype(BF).reshape(rows, span, width)
+    last_in = ffin_terms.reshape(seq_size, 2, *ffin_terms.shape[-2:])
+    last_out = ffout_terms.reshape(seq_size, 2, *ffout_terms.shape[-2:])
+    normed_one_grad, ffn_in_grad, ffn_out_grad, proj_sums = finish_sums(
+        normed_low_terms.reshape(seq_size, tokens, width), last_in, last_out, proj_terms
+    )
+    ffn_in_grad, ffn_out_grad = ffn_in_grad.reshape(ffn_in.shape), ffn_out_grad.reshape(ffn_out.shape)
+    proj_sums = proj_sums.astype(F32)
     qkv_grad = proj_sums[:, :depth, : 3 * cols].reshape(seq_size, depth, 3, cols)
     qkv_grad = qkv_grad.transpose(2, 1, 0, 3).reshape(qkv_proj.shape)
     out_proj_grad = jnp.sum(proj_sums[:, :depth, 3 * cols :], axis=0)
     small_grad = jnp.sum(proj_sums[:, depth, : 6 * depth], axis=0).reshape(6, depth)
     centroids_grad = jnp.sum(proj_sums[:, depth + 1, :cols], axis=0)[None]
 
-    in_pair, out_pair = lax.optimization_barrier((in_pair, out_pair, normed_low_terms))[:2]
     expert_in_grad = (in_kept + in_pair.astype(F32))[None]
     expert_out_grad = (out_kept + out_pair.astype(F32))[None]
 

time: 984 us -> 911 us (0.926)
  waiting for transfers between devices: 303 us -> 196 us
  Pallas kernels: 222 us -> 289 us
  starting transfers between devices: 104 us -> 58.7 us
    pallas_call x0 -> x1, Pallas kernels: none -> 121 us  [finish_sums(): pl.pallas_call(functools.partial(finish_kernel, seq_size, bits), in_specs...]
    ppermute x23 -> x10, waiting for transfers between devices: 194 us -> 119 us  [seq_shift(): lax.ppermute(values, 'seq', [(i, (i + step) % size) for i in range(size)])]
    ppermute x9 -> x4, waiting for transfers between devices: 60.7 us -> 0.01 us  [fsdp_flip(): return lax.ppermute(values, 'fsdp', [(i, i ^ bit) for i in range(size)])]
    pallas_call x1, Pallas kernels: 181 us -> 127 us  [start_gathers(): pl.pallas_call(functools.partial(gather_kernel, seq_size, bits), in_specs...]
    ppermute x23 -> x10, starting transfers between devices: 58 us -> 13.4 us  [seq_shift(): lax.ppermute(values, 'seq', [(i, (i + step) % size) for i in range(size)])]
    ppermute x4 -> x6, waiting for transfers between devices: 34.4 us -> 52.5 us  [seq_pair(): return lax.ppermute(values, 'seq', [(i, i ^ 1) for i in range(size)])]
    all_to_all x7, waiting for transfers between devices: 13.7 us -> 24.6 us  [swap_slots(): lax.all_to_all(values, 'fsdp', split_axis=0, concat_axis=0, tiled=True)]
    convert_element_type x8 -> x2, other arithmetic: 22.2 us -> 13.7 us  [hyper_scatter_step(): return (kept.astype(F32) + arrived.astype(F32)).astype(BF)]
  transfers between devices with their start and end apart: 43 -> 27, of which waited for: 18 -> 13; matrix products, arithmetic and copies ran while one was open for 27% -> 30% of each run, Pallas kernels for 2% -> 5%
where the time goes in v2:
time: 911 us; the launch traced here: 898 us
  Pallas kernels  289 us (32%)
  waiting for transfers between devices  196 us (22%)
  matrix products  188 us (21%)
  local copies, waits for them, and re-layouts  89 us (10%)
  other arithmetic  75.4 us (8%)
  starting transfers between devices  58.7 us (6%)
    pallas_call x1, Pallas kernels, start_gathers(): pl.pallas_call(functools.partial(gather_kernel, seq_size, bits), in_specs...  127 us
    pallas_call x1, Pallas kernels, finish_sums(): pl.pallas_call(functools.partial(finish_kernel, seq_size, bits), in_specs...  121 us
    ppermute x10, waiting for transfers between devices, seq_shift(): lax.ppermute(values, 'seq', [(i, (i + step) % size) for i in range(size)])  119 us
    dot_general x12, matrix products, mm_tn(): lax.dot_general(left, right, (((0,), (0,)), ((), ())), preferred_element_...  69 us
    dot_general x16, matrix products, mm(): return jnp.dot(left, right, preferred_element_type=F32)  67.4 us
    ppermute x6, waiting for transfers between devices, seq_pair(): return lax.ppermute(values, 'seq', [(i, i ^ 1) for i in range(size)])  52.5 us
    dot_general x8, matrix products, mm_nt(): lax.dot_general(left, right, (((1,), (1,)), ((), ())), preferred_element_...  51.3 us
    all_to_all x7, starting transfers between devices, swap_slots(): lax.all_to_all(values, 'fsdp', split_axis=0, concat_axis=0, tiled=True)  31.1 us
  transfers between devices with their start and end apart: 27, of which 13 were waited for; matrix products, arithmetic and copies ran while one was open for 30% of the time, Pallas kernels for 5%

profile of v2, /device:TPU:0, one launch (start us, length us, event | category | flops | bytes accessed | tf_op | source)
XLA Modules:
  0.0 898.1 jit_solution(17894716745234150184)
XLA Ops:
  7.2 127.1 %shard_map.212 = (bf16[4,2,2,2,48,1792]{5,4,3,2,1,0:T(8,128)(2,1)}, bf16[4,2,2,2,32,4096]{5,4,3,2,1,0:T(8,128)(2,1)}, bf16[4,2,2,2,128,1024]{5,4,3,2,1,0:T(8,128)(2,1)}, bf16[4,512,1024]{2,1,0:T(8,128)(2,1)}) custom-call(bf16[4,48,1792]{2,1,0:T(8,128)(2,1)} %pad_maximum_fusion.16.proj_ref, bf16[32,4096]{1,0:T(8,128)(2,1)} %in_ref.1, ...), custom_call_target="tpu_custom_call" | custom-call | bytes 104857600 | tf_op jit(solution)/shard_map/pallas_call | solution.py:457
  155.9 20.0 %shard_map.213 = (bf16[4,2,256,256]{3,2,1,0:T(8,128)(2,1)S(1)}, f32[2,2,2,1024]{3,2,1,0:T(2,128)S(1)}) custom-call(bf16[4,2,256,768]{3,2,1,0:T(8,128)(2,1)S(1)} %bitcast.158, bf16[4,2,256,768]{3,2,1,0:T(8,128)(2,1)S(1)} %bitcast.159, bf16[4,2,256,768]{3,2,1,0:T(8,128)(2,1)S(1)} %bitcast.160, s32[2,1,1024]{2,1,0:T(1,128)S(1)} %fusion.86.id_row_ref, ...), custom_call_target="tpu_custom_call" | custom-call | flops 1000000 | bytes 65536 | tf_op jit(solution)/shard_map/pallas_call | solution.py:186
  218.0 8.5 fusion.10
  233.8 17.8 %collective-permute-done.5 = bf16[512,1024]{1,0:T(8,128)(2,1)S(1)} collective-permute-done((bf16[512,1024]{1,0:T(8,128)(2,1)S(1)}, bf16[512,1024]{1,0:T(8,128)(2,1)S(1)}, u32[]{:S(2)}, u32[]{:S(2)}) %collective-permute-start.5) | collective-permute-done | bytes 1048608 | tf_op jit(solution)/shard_map/ppermute | solution.py:69
  271.6 9.1 %all-to-all-done = bf16[8,96,1024]{2,1,0:T(8,128)(2,1)S(1)} async-done(((bf16[8,96,1024]{2,1,0:T(8,128)(2,1)}), bf16[8,96,1024]{2,1,0:T(8,128)(2,1)S(1)}, u32[]{:S(2)}, u32[]{:S(2)}) %all-to-all-start) | async-done | bytes 1572896 | tf_op jit(solution)/shard_map/all_to_all | solution.py:839
  285.0 9.7 %fusion.15 = (bf16[768,2048]{1,0:T(8,128)(2,1)}, bf16[768,2048]{1,0:T(8,128)(2,1)}) fusion(bf16[768,1024]{1,0:T(8,128)(2,1)S(1)} %bitcast.169, bf16[512,1024]{1,0:T(8,128)(2,1)} %collective-permute-done.1, bf16[512,1024]{1,0:T(8,128)(2,1)} %collective-permute-done, bf16[1024,1024]{1,0:T(8,128)(2,1)} %bitcast.189), kind=kOutput, calls=%fused_computation.30 | convolution fusion | flops 3251109888 | bytes 12058624 | tf_op jit(solution)/shard_map/dot_general | solution.py:31
  294.7 44.1 %collective-permute-done.7 = bf16[512,1024]{1,0:T(8,128)(2,1)} collective-permute-done((bf16[512,1024]{1,0:T(8,128)(2,1)}, bf16[512,1024]{1,0:T(8,128)(2,1)}, u32[]{:S(2)}, u32[]{:S(2)}) %collective-permute-start.7) | collective-permute-done | bytes 1048608 | tf_op jit(solution)/shard_map/ppermute | solution.py:64
  342.3 18.6 %collective-permute-done.8 = bf16[512,1024]{1,0:T(8,128)(2,1)} collective-permute-done((bf16[512,1024]{1,0:T(8,128)(2,1)}, bf16[512,1024]{1,0:T(8,128)(2,1)}, u32[]{:S(2)}, u32[]{:S(2)}) %collective-permute-start.8) | collective-permute-done | bytes 1048608 | tf_op jit(solution)/shard_map/ppermute | solution.py:64
  371.7 8.5 multiply_convert_fusion.7
  399.0 10.2 %fusion.20 = (bf16[768,2048]{1,0:T(8,128)(2,1)}, bf16[768,2048]{1,0:T(8,128)(2,1)}) fusion(bf16[768,1024]{1,0:T(8,128)(2,1)} %bitcast.32, bf16[512,1024]{1,0:T(8,128)(2,1)} %collective-permute-done.1, bf16[512,1024]{1,0:T(8,128)(2,1)} %collective-permute-done, bf16[1024,1024]{1,0:T(8,128)(2,1)} %bitcast.190), kind=kOutput, calls=%fused_computation.35 | convolution fusion | flops 3251109888 | bytes 12058624 | tf_op jit(solution)/shard_map/dot_general | solution.py:31
  411.1 8.9 all-to-all-done.4
  424.6 8.5 multiply_convert_fusion.6
  482.0 7.2 fusion.33
  491.9 11.0 %fusion.35 = f32[1024,1024]{1,0:T(8,128)} fusion(bf16[768,2048]{1,0:T(8,128)(2,1)S(1)} %copy-done.78, bf16[768,2048]{1,0:T(8,128)(2,1)S(1)} %copy-done.75, bf16[768,1024]{1,0:T(8,128)(2,1)} %bitcast.32, bf16[768,1024]{1,0:T(8,128)(2,1)S(1)} %bitcast.172), kind=kOutput, calls=%fused_computation.71 | convolution fusion | flops 3233808384 | bytes 13631488 | tf_op jit(solution)/shard_map/dot_general | solution.py:39
  509.9 30.0 %collective-permute-done.9 = bf16[512,1024]{1,0:T(8,128)(2,1)S(1)} collective-permute-done((bf16[512,1024]{1,0:T(8,128)(2,1)S(1)}, bf16[512,1024]{1,0:T(8,128)(2,1)S(1)}, u32[]{:S(2)}, u32[]{:S(2)}) %collective-permute-start.9) | collective-permute-done | bytes 1048608 | tf_op jit(solution)/shard_map/ppermute | solution.py:64
  552.0 9.6 %multiply_convert_fusion = bf16[512,4096]{1,0:T(8,128)(2,1)S(1)} fusion(bf16[512,4096]{1,0:T(8,128)(2,1)} %get-tuple-element.92, bf16[4096,1024]{1,0:T(8,128)(2,1)} %bitcast.242, f32[512,1024]{1,0:T(8,128)S(1)} %multiply_add_fusion.1), kind=kOutput, calls=%fused_computation.19 | convolution fusion | flops 4301783040 | bytes 18874368 | tf_op jit(solution)/shard_map/dot_general | solution.py:35
  561.7 9.1 %multiply_reduce_fusion.4 = (bf16[1024]{0:T(1024)(128)(2,1)S(1)}, f32[512]{0:T(512)S(1)}, f32[512]{0:T(512)S(1)}, bf16[1024]{0:T(1024)(128)(2,1)S(1)}, f32[512,1024]{1,0:T(8,128)S(1)}) fusion(f32[512,1024]{1,0:T(8,128)S(1)} %copy-done.12, f32[512]{0:T(512)S(1)} %copy-done.60, f32[512]{0:T(512)S(1)} %copy-done.58, f32[1024]{0:T(1024)S(1)} %copy-done.54, ...), kind=kOutput, calls=%fused_computation.102 | convolution fusion | flops 4299682816 | bytes 16793600 | tf_op jit(solution)/shard_map/dot_general | solution.py:35
  576.3 7.4 convolution_convert_fusion.1
  613.6 10.3 %collective-permute-done.12 = bf16[2,256,256]{2,1,0:T(8,128)(2,1)S(1)} collective-permute-done((bf16[2,256,256]{2,1,0:T(8,128)(2,1)S(1)}, bf16[2,256,256]{2,1,0:T(8,128)(2,1)S(1)}, u32[]{:S(2)}, u32[]{:S(2)}) %collective-permute-start.12) | collective-permute-done | bytes 262176 | tf_op jit(solution)/shard_map/ppermute | solution.py:64
  624.0 7.9 add_convert_fusion.1
  660.5 21.1 %shard_map.214 = (bf16[4,2,256,256]{3,2,1,0:T(8,128)(2,1)S(1)}, bf16[4,2,256,256]{3,2,1,0:T(8,128)(2,1)S(1)}, bf16[4,2,256,256]{3,2,1,0:T(8,128)(2,1)S(1)}) custom-call(bf16[4,2,256,768]{3,2,1,0:T(8,128)(2,1)} %bitcast.161, bf16[4,2,256,768]{3,2,1,0:T(8,128)(2,1)} %bitcast.162, bf16[4,2,256,768]{3,2,1,0:T(8,128)(2,1)} %bitcast.163, ...), custom_call_target="tpu_custom_call" | custom-call | flops 1000000 | bytes 65536 | tf_op jit(solution)/shard_map/pallas_call | solution.py:206
  681.9 28.8 %collective-permute-done.16 = bf16[1024,1024]{1,0:T(8,128)(2,1)} collective-permute-done((bf16[1024,1024]{1,0:T(8,128)(2,1)}, bf16[1024,1024]{1,0:T(8,128)(2,1)}, u32[]{:S(2)}, u32[]{:S(2)}) %collective-permute-start.16) | collective-permute-done | bytes 2097184 | tf_op jit(solution)/shard_map/ppermute | solution.py:69
  719.4 8.6 fusion.56
  752.1 120.5 %shard_map.215 = (f32[512,1024]{1,0:T(8,128)}, f32[32,4096]{1,0:T(8,128)}, f32[128,1024]{1,0:T(8,128)}, bf16[4,48,1792]{2,1,0:T(8,128)(2,1)}) custom-call(bf16[4,512,1024]{2,1,0:T(8,128)(2,1)} %bitcast.167, bf16[4,2,32,4096]{3,2,1,0:T(8,128)(2,1)} %fusion.48.in_ref, bf16[4,2,128,1024]{3,2,1,0:T(8,128)(2,1)} %fusion.49.out_ref, ...), custom_call_target="tpu_custom_call" | custom-call | bytes 104857600 | tf_op jit(solution)/shard_map/pallas_call | solution.py:720
  (402 shorter events, 333.3 us)
Async XLA Ops:
  135.8 42.2 %collective-permute-start = (bf16[512,1024]{1,0:T(8,128)(2,1)}, bf16[512,1024]{1,0:T(8,128)(2,1)}, u32[]{:S(2)}, u32[]{:S(2)}) collective-permute-start(bf16[512,1024]{1,0:T(8,128)(2,1)} %get-tuple-element.165), channel_id=1, source_target_pairs={{0,8},{8,0},{16,24},{24,16},{1,9},{9,1},{17,25},{25,17},{2,10},{10... | collective-permute-start | bytes 3145736 | tf_op jit(solution)/shard_map/ppermute | solution.py:69
  135.8 48.2 %collective-permute-start.1 = (bf16[512,1024]{1,0:T(8,128)(2,1)}, bf16[512,1024]{1,0:T(8,128)(2,1)}, u32[]{:S(2)}, u32[]{:S(2)}) collective-permute-start(bf16[512,1024]{1,0:T(8,128)(2,1)} %get-tuple-element.164), channel_id=1, source_target_pairs={{0,8},{8,0},{16,24},{24,16},{1,9},{9,1},{17,25},{25,17},{2,10},{10... | collective-permute-start | bytes 3145736 | tf_op jit(solution)/shard_map/ppermute | solution.py:69
  185.8 21.2 %collective-permute-start.3 = (bf16[2,256,256]{2,1,0:T(8,128)(2,1)}, bf16[2,256,256]{2,1,0:T(8,128)(2,1)}, u32[]{:S(2)}, u32[]{:S(2)}) collective-permute-start(bf16[2,256,256]{2,1,0:T(8,128)(2,1)} %get-tuple-element.173), channel_id=1, source_target_pairs={{0,16},{8,24},{16,0},{24,8},{1,17},{9,25},{17,1},{25,9},{2,18},{10... | collective-permute-start | bytes 786440 | tf_op jit(solution)/shard_map/ppermute | solution.py:64
  226.6 25.0 %collective-permute-start.5 = (bf16[512,1024]{1,0:T(8,128)(2,1)S(1)}, bf16[512,1024]{1,0:T(8,128)(2,1)S(1)}, u32[]{:S(2)}, u32[]{:S(2)}) collective-permute-start(bf16[512,1024]{1,0:T(8,128)(2,1)S(1)} %copy-done.46), channel_id=1, source_target_pairs={{0,8},{8,0},{16,24},{24,16},{1,9},{9,1},{17,25},{25,17},{2,10},{10... | collective-permute-start | bytes 3145736 | tf_op jit(solution)/shard_map/ppermute | solution.py:69
  255.4 25.2 %all-to-all-start = ((bf16[8,96,1024]{2,1,0:T(8,128)(2,1)}), bf16[8,96,1024]{2,1,0:T(8,128)(2,1)S(1)}, u32[]{:S(2)}, u32[]{:S(2)}) async-start(bf16[8,96,1024]{2,1,0:T(8,128)(2,1)} %bitcast.205), calls=%async_computation | async-start | bytes 3145728 | tf_op jit(solution)/shard_map/all_to_all | solution.py:839
  266.7 72.0 %collective-permute-start.7 = (bf16[512,1024]{1,0:T(8,128)(2,1)}, bf16[512,1024]{1,0:T(8,128)(2,1)}, u32[]{:S(2)}, u32[]{:S(2)}) collective-permute-start(bf16[512,1024]{1,0:T(8,128)(2,1)} %add_convert_fusion.9), channel_id=1, source_target_pairs={{0,16},{8,24},{16,0},{24,8},{1,17},{9,25},{17,1},{25,9},{2,18},{10... | collective-permute-start | bytes 3145736 | tf_op jit(solution)/shard_map/ppermute | solution.py:64
  267.5 93.3 %collective-permute-start.8 = (bf16[512,1024]{1,0:T(8,128)(2,1)}, bf16[512,1024]{1,0:T(8,128)(2,1)}, u32[]{:S(2)}, u32[]{:S(2)}) collective-permute-start(bf16[512,1024]{1,0:T(8,128)(2,1)} %bitcast.10), channel_id=1, source_target_pairs={{0,16},{8,24},{16,0},{24,8},{1,17},{9,25},{17,1},{25,9},{2,18},{10... | collective-permute-start | bytes 3145736 | tf_op jit(solution)/shard_map/ppermute | solution.py:64
  269.7 91.2 %collective-permute-start.6 = (bf16[512,1024]{1,0:T(8,128)(2,1)}, bf16[512,1024]{1,0:T(8,128)(2,1)}, u32[]{:S(2)}, u32[]{:S(2)}) collective-permute-start(bf16[512,1024]{1,0:T(8,128)(2,1)} %get-tuple-element.81), channel_id=1, source_target_pairs={{0,8},{8,0},{16,24},{24,16},{1,9},{9,1},{17,25},{25,17},{2,10},{10... | collective-permute-start | bytes 3145736 | tf_op jit(solution)/shard_map/ppermute | solution.py:69
  280.7 86.5 %all-to-all-start.1 = ((bf16[8,96,1024]{2,1,0:T(8,128)(2,1)}), bf16[8,96,1024]{2,1,0:T(8,128)(2,1)}, u32[]{:S(2)}, u32[]{:S(2)}) async-start(bf16[8,96,1024]{2,1,0:T(8,128)(2,1)} %bitcast.201), calls=%async_computation.1 | async-start | bytes 3145728 | tf_op jit(solution)/shard_map/all_to_all | solution.py:839
  367.2 27.5 %all-to-all-start.3 = ((bf16[8,96,1024]{2,1,0:T(8,128)(2,1)}), bf16[8,96,1024]{2,1,0:T(8,128)(2,1)}, u32[]{:S(2)}, u32[]{:S(2)}) async-start(bf16[8,96,1024]{2,1,0:T(8,128)(2,1)} %bitcast.206), calls=%async_computation.3 | async-start | bytes 3145728 | tf_op jit(solution)/shard_map/all_to_all | solution.py:839
  394.7 25.4 %all-to-all-start.4 = ((bf16[8,96,1024]{2,1,0:T(8,128)(2,1)}), bf16[8,96,1024]{2,1,0:T(8,128)(2,1)}, u32[]{:S(2)}, u32[]{:S(2)}) async-start(bf16[8,96,1024]{2,1,0:T(8,128)(2,1)} %bitcast.204), calls=%async_computation.4 | async-start | bytes 3145728 | tf_op jit(solution)/shard_map/all_to_all | solution.py:839
  420.0 27.5 %all-to-all-start.2 = ((bf16[8,96,1024]{2,1,0:T(8,128)(2,1)}), bf16[8,96,1024]{2,1,0:T(8,128)(2,1)}, u32[]{:S(2)}, u32[]{:S(2)}) async-start(bf16[8,96,1024]{2,1,0:T(8,128)(2,1)} %bitcast.203), calls=%async_computation.2 | async-start | bytes 3145728 | tf_op jit(solution)/shard_map/all_to_all | solution.py:839
  447.6 25.4 %all-to-all-start.5 = ((bf16[8,96,1024]{2,1,0:T(8,128)(2,1)}), bf16[8,96,1024]{2,1,0:T(8,128)(2,1)}, u32[]{:S(2)}, u32[]{:S(2)}) async-start(bf16[8,96,1024]{2,1,0:T(8,128)(2,1)} %bitcast.202), calls=%async_computation.5 | async-start | bytes 3145728 | tf_op jit(solution)/shard_map/all_to_all | solution.py:839
  472.9 69.4 %all-to-all-start.6 = ((bf16[8,192,1024]{2,1,0:T(8,128)(2,1)}), bf16[8,192,1024]{2,1,0:T(8,128)(2,1)}, u32[]{:S(2)}, u32[]{:S(2)}) async-start(bf16[8,192,1024]{2,1,0:T(8,128)(2,1)} %pad_maximum_fusion.6), calls=%async_computation.6 | async-start | bytes 6291456 | tf_op jit(solution)/shard_map/all_to_all | solution.py:839
  491.8 48.1 %collective-permute-start.9 = (bf16[512,1024]{1,0:T(8,128)(2,1)S(1)}, bf16[512,1024]{1,0:T(8,128)(2,1)S(1)}, u32[]{:S(2)}, u32[]{:S(2)}) collective-permute-start(bf16[512,1024]{1,0:T(8,128)(2,1)S(1)} %fusion.61), channel_id=1, source_target_pairs={{0,16},{8,24},{16,0},{24,8},{1,17},{9,25},{17,1},{25,9},{2,18},{10... | collective-permute-start | bytes 3145736 | tf_op jit(solution)/shard_map/ppermute | solution.py:64
  502.9 73.4 %collective-permute-start.10 = (bf16[1024,1024]{1,0:T(8,128)(2,1)}, bf16[1024,1024]{1,0:T(8,128)(2,1)}, u32[]{:S(2)}, u32[]{:S(2)}) collective-permute-start(bf16[1024,1024]{1,0:T(8,128)(2,1)} %fusion.50), channel_id=1, source_target_pairs={{0,8},{8,0},{16,24},{24,16},{1,9},{9,1},{17,25},{25,17},{2,10},{10... | collective-permute-start | bytes 6291464 | tf_op jit(solution)/shard_map/ppermute | solution.py:69
  590.0 34.0 %collective-permute-start.14 = (bf16[4,2,2,1,128,1024]{5,4,1,0,3,2:T(8,128)(2,1)}, bf16[4,2,2,1,128,1024]{5,4,1,0,3,2:T(8,128)(2,1)}, u32[]{:S(2)}, u32[]{:S(2)}) collective-permute-start(bf16[4,2,2,1,128,1024]{5,4,1,0,3,2:T(8,128)(2,1)} %copy.65), channel_id=1, source_target_pairs={{0,1},{1,0},{2,3},{3,2},{4,5},{5,4},{6,7},{7,6},{8,9},{9,8},{10,11... | collective-permute-start | bytes 12582920 | tf_op jit(solution)/shard_map/ppermute | solution.py:220
  601.1 30.7 %collective-permute-start.15 = (bf16[4,2,2,1,32,4096]{5,4,2,0,3,1:T(8,128)(2,1)}, bf16[4,2,2,1,32,4096]{5,4,2,0,3,1:T(8,128)(2,1)}, u32[]{:S(2)}, u32[]{:S(2)}) collective-permute-start(bf16[4,2,2,1,32,4096]{5,4,2,0,3,1:T(8,128)(2,1)} %copy.67), channel_id=1, source_target_pairs={{0,1},{1,0},{2,3},{3,2},{4,5},{5,4},{6,7},{7,6},{8,9},{9,8},{10,11... | collective-permute-start | bytes 12582920 | tf_op jit(solution)/shard_map/ppermute | solution.py:220
  602.5 21.4 %collective-permute-start.12 = (bf16[2,256,256]{2,1,0:T(8,128)(2,1)S(1)}, bf16[2,256,256]{2,1,0:T(8,128)(2,1)S(1)}, u32[]{:S(2)}, u32[]{:S(2)}) collective-permute-start(bf16[2,256,256]{2,1,0:T(8,128)(2,1)S(1)} %get-tuple-element.169), channel_id=1, source_target_pairs={{0,16},{8,24},{16,0},{24,8},{1,17},{9,25},{17,1},{25,9},{2,18},{10... | collective-permute-start | bytes 786440 | tf_op jit(solution)/shard_map/ppermute | solution.py:64
  605.4 18.5 %collective-permute-start.13 = (bf16[2,256,256]{2,1,0:T(8,128)(2,1)S(1)}, bf16[2,256,256]{2,1,0:T(8,128)(2,1)S(1)}, u32[]{:S(2)}, u32[]{:S(2)}) collective-permute-start(bf16[2,256,256]{2,1,0:T(8,128)(2,1)S(1)} %get-tuple-element.168), channel_id=1, source_target_pairs={{0,24},{8,0},{16,8},{24,16},{1,25},{9,1},{17,9},{25,17},{2,26},{10... | collective-permute-start | bytes 786440 | tf_op jit(solution)/shard_map/ppermute | solution.py:64
  637.6 73.0 %collective-permute-start.16 = (bf16[1024,1024]{1,0:T(8,128)(2,1)}, bf16[1024,1024]{1,0:T(8,128)(2,1)}, u32[]{:S(2)}, u32[]{:S(2)}) collective-permute-start(bf16[1024,1024]{1,0:T(8,128)(2,1)} %fusion.53), channel_id=1, source_target_pairs={{0,8},{8,0},{16,24},{24,16},{1,9},{9,1},{17,25},{25,17},{2,10},{10... | collective-permute-start | bytes 6291464 | tf_op jit(solution)/shard_map/ppermute | solution.py:69
  654.4 90.0 %collective-permute-start.17 = (bf16[512,1024]{1,0:T(8,128)(2,1)}, bf16[512,1024]{1,0:T(8,128)(2,1)}, u32[]{:S(2)}, u32[]{:S(2)}) collective-permute-start(bf16[512,1024]{1,0:T(8,128)(2,1)} %fusion.62), channel_id=1, source_target_pairs={{0,16},{8,24},{16,0},{24,8},{1,17},{9,25},{17,1},{25,9},{2,18},{10... | collective-permute-start | bytes 3145736 | tf_op jit(solution)/shard_map/ppermute | solution.py:64
  655.8 88.5 %collective-permute-start.18 = (bf16[4,1,2,1,32,4096]{5,4,2,0,3,1:T(8,128)(2,1)}, bf16[4,1,2,1,32,4096]{5,4,2,0,3,1:T(8,128)(2,1)}, u32[]{:S(2)}, u32[]{:S(2)}) collective-permute-start(bf16[4,1,2,1,32,4096]{5,4,2,0,3,1:T(8,128)(2,1)} %constant_dynamic-slice_fusion.1), channel_id=1, source_target_pairs={{0,4},{1,5},{2,6},{3,7},{4,0},{5,1},{6,2},{7,3},{8,12},{9,13},{10,... | collective-permute-start | bytes 6291464 | tf_op jit(solution)/shard_map/ppermute | solution.py:220
  659.0 89.2 %collective-permute-start.19 = (bf16[4,2,1,1,128,1024]{5,4,1,0,3,2:T(8,128)(2,1)}, bf16[4,2,1,1,128,1024]{5,4,1,0,3,2:T(8,128)(2,1)}, u32[]{:S(2)}, u32[]{:S(2)}) collective-permute-start(bf16[4,2,1,1,128,1024]{5,4,1,0,3,2:T(8,128)(2,1)} %constant_dynamic-slice_fusion), channel_id=1, source_target_pairs={{0,2},{1,3},{2,0},{3,1},{4,6},{5,7},{6,4},{7,5},{8,10},{9,11},{10,... | collective-permute-start | bytes 6291464 | tf_op jit(solution)/shard_map/ppermute | solution.py:220
  (91 other events, 1046.6 us)

commit v3 on v2

--- a/solution.py
+++ b/solution.py
@@ -55,8 +55,8 @@
     return scale * (unit_grad - first - unit * second), jnp.sum(grads * unit, axis=0), jnp.sum(grads, axis=0)
 
 
-def after(values, *earlier):
-    return lax.optimization_barrier((values, *earlier))[0]
+def tie(*values):
+    return lax.optimization_barrier(values)
 
 
 def seq_shift(values, step):
@@ -77,14 +77,19 @@
     return lax.dynamic_index_in_dim(values, place, 0, keepdims=False)
 
 
-def seq_exchange(values):
+def seq_exchange(values, chained=False):
     size = lax.axis_size("seq")
     here = lax.axis_index("seq")
     result = put(jnp.zeros_like(values), pick(values, here), here)
+    arrived = None
     for step in range(1, size):
-        arrived = seq_shift(pick(values, (here + step) % size), step)
-        result = put(result, arrived, (here - step) % size)
-    return result
+        sent = pick(values, (here + step) % size)
+        if chained and arrived is not None:
+            sent, arrived = tie(sent, arrived)
+        if arrived is not None:
+            result = put(result, arrived, (here - step + 1) % size)
+        arrived = seq_shift(sent, step)
+    return put(result, arrived, (here - size + 1) % size)
 
 
 def seq_sum_scatter(values):
@@ -123,9 +128,10 @@
         for head, query in enumerate(masked_pair(queries[start:end])):
             scores = jnp.where(mask, mm_nt(keys[:end], query), -1e30)
             top = jnp.max(scores, axis=0, keepdims=True)
-            lse = top + jnp.log(jnp.sum(jnp.exp(scores - top), axis=0, keepdims=True))
-            weights = jnp.exp(scores - lse).astype(BF)
-            lse_ref[0, 0, pl.ds(head, 1), pl.ds(start, size)] = lse
+            powers = jnp.exp(scores - top)
+            whole = jnp.sum(powers, axis=0, keepdims=True)
+            weights = (powers * (1.0 / whole)).astype(BF)
+            lse_ref[0, 0, pl.ds(head, 1), pl.ds(start, size)] = top + jnp.log(whole)
             part = values_t[head * HEAD_DIM : (head + 1) * HEAD_DIM, :end]
             parts.append(mm(part, weights))
         o_all[pl.ds(start, size), :] = jnp.concatenate(parts, axis=0).T
@@ -230,27 +236,199 @@
     return parts.reshape(parts.shape[0], *[2] * count, *parts.shape[2:])
 
 
-def hyper_scatter_step(held, bit):
-    count = lax.axis_size("fsdp").bit_length() - 1
-    axis = count + 1 - bit.bit_length()
-    bit_here = (lax.axis_index("fsdp") // bit) % 2
-    sent = lax.dynamic_slice_in_dim(held, 1 - bit_here, 1, axis)
-    kept = lax.dynamic_slice_in_dim(held, bit_here, 1, axis)
-    arrived = fsdp_flip(sent, bit)
-    return (kept.astype(F32) + arrived.astype(F32)).astype(BF)
-
-
-def hyper_scatter(held, bits):
-    for bit in bits:
-        held = hyper_scatter_step(held, bit)
-    return held
-
-
 def by_device(term):
     seq_size, fsdp_size = lax.axis_size("seq"), lax.axis_size("fsdp")
     depth = term.shape[0] // (seq_size * fsdp_size)
     tile = (depth, term.shape[1]) if depth % 16 == 0 else (16, depth * term.shape[1] // 16)
     return term.astype(BF).reshape(seq_size, fsdp_size, *tile)
+
+
+def ffn_kernel(middle_ref, gains_ref, biases_ref, win_ref, wout_ref, normed_ref, act_ref, slope_ref, block_ref, routed_ref):
+    chunk = pl.program_id(0)
+
+    def norm(values, row):
+        average, scale = norm_parts(values)
+        return ((values - average) * scale * gains_ref[row : row + 1] + biases_ref[row : row + 1]).astype(BF)
+
+    @pl.when(chunk == 0)
+    def _():
+        normed_ref[...] = norm(middle_ref[...], 1)
+        block_ref[...] = middle_ref[...]
+
+    act, slope = gelu_pair(mm(normed_ref[...], win_ref[...]))
+    act = act.astype(BF)
+    act_ref[...] = act
+    slope_ref[...] = slope.astype(BF)
+    block_ref[...] += mm(act, wout_ref[...])
+
+    @pl.when(chunk == pl.num_programs(0) - 1)
+    def _():
+        routed_ref[...] = norm(block_ref[...], 2)
+
+
+def ffn_specs(tokens, width, hidden):
+    size = min(512, hidden)
+    whole = pl.BlockSpec((tokens, width), lambda j: (0, 0))
+    piece = pl.BlockSpec((tokens, size), lambda j: (0, j))
+    row = pl.BlockSpec((8, width), lambda j: (0, 0))
+    return size, whole, piece, row, [
+        pl.BlockSpec((width, size), lambda j: (0, j)),
+        pl.BlockSpec((size, width), lambda j: (j, 0)),
+    ]
+
+
+def ffn_forward(middle, gains, biases, win, wout):
+    tokens, width = middle.shape
+    hidden = win.shape[1]
+    size, whole, piece, row, weights = ffn_specs(tokens, width, hidden)
+    low, wide = jax.ShapeDtypeStruct((tokens, width), BF), jax.ShapeDtypeStruct((tokens, hidden), BF)
+    return pl.pallas_call(
+        ffn_kernel,
+        grid=(hidden // size,),
+        in_specs=[whole, row, row, *weights],
+        out_specs=[whole, piece, piece, whole, whole],
+        out_shape=[low, wide, wide, jax.ShapeDtypeStruct((tokens, width), F32), low],
+        compiler_params=pltpu.CompilerParams(vmem_limit_bytes=48 * 2**20),
+        cost_estimate=pl.CostEstimate(flops=10**6, bytes_accessed=2**16, transcendentals=0),
+    )(middle, gains, biases, win, wout)
+
+
+def ffn_back_kernel(
+    back_ref, block_ref, grad_ref, middle_ref, gains_ref, slope_ref, win_ref, wout_ref,
+    low_ref, du_ref, dh_ref, branch_ref, terms_ref, total,
+):
+    chunk = pl.program_id(0)
+
+    def norm_grad(values, row, grads):
+        moved, gain, bias = norm_back(values, norm_parts(values), gains_ref[row : row + 1], grads)
+        return moved, gain[None], bias[None]
+
+    @pl.when(chunk == 0)
+    def _():
+        moved, gain, bias = norm_grad(block_ref[...], 2, back_ref[...])
+        grads = grad_ref[...].astype(F32) + moved
+        dh_ref[...] = grads
+        low_ref[...] = grads.astype(BF)
+        terms_ref[0:1] = gain
+        terms_ref[1:2] = bias
+        total[...] = jnp.zeros_like(total)
+
+    du = (slope_ref[...].astype(F32) * mm_nt(low_ref[...], wout_ref[...])).astype(BF)
+    du_ref[...] = du
+    total[...] += mm_nt(du, win_ref[...])
+
+    @pl.when(chunk == pl.num_programs(0) - 1)
+    def _():
+        moved, gain, bias = norm_grad(middle_ref[...], 1, total[...])
+        grads = dh_ref[...] + moved
+        dh_ref[...] = grads
+        branch_ref[...] = grads.astype(BF)
+        terms_ref[2:3] = gain
+        terms_ref[3:4] = bias
+
+
+def ffn_backward(back, block_out, grads, middle, gains, slope, win, wout):
+    tokens, width = middle.shape
+    hidden = win.shape[1]
+    size, whole, piece, row, weights = ffn_specs(tokens, width, hidden)
+    low, wide = jax.ShapeDtypeStruct((tokens, width), BF), jax.ShapeDtypeStruct((tokens, hidden), BF)
+    f32 = jax.ShapeDtypeStruct((tokens, width), F32)
+    return pl.pallas_call(
+        ffn_back_kernel,
+        grid=(hidden // size,),
+        in_specs=[whole, whole, whole, whole, row, piece, *weights],
+        out_specs=[whole, piece, whole, whole, row],
+        out_shape=[low, wide, f32, low, jax.ShapeDtypeStruct((8, width), F32)],
+        scratch_shapes=[pltpu.VMEM((tokens, width), F32)],
+        compiler_params=pltpu.CompilerParams(vmem_limit_bytes=48 * 2**20),
+        cost_estimate=pl.CostEstimate(flops=10**6, bytes_accessed=2**16, transcendentals=0),
+    )(back, block_out, grads, middle, gains, slope, win, wout)
+
+
+def expert_kernel(x_ref, dr_ref, centroid_ref, win_own, wout_own, win_low, win_high, wout_low, wout_high, *refs):
+    act_ref, du_ref, dz_ref, all_ref, gated_ref, dx_ref, term_ref, total, back, win_ref, wout_ref = refs[-11:]
+    chunk = pl.program_id(0)
+    own = pl.num_programs(0) - 2
+    for here, win_part, wout_part in (
+        (chunk < own, win_own, wout_own),
+        (chunk == own, win_low, wout_low),
+        (chunk == own + 1, win_high, wout_high),
+    ):
+
+        @pl.when(here)
+        def _(win_part=win_part, wout_part=wout_part):
+            win_ref[...] = win_part[...]
+            wout_ref[...] = wout_part[...]
+
+    x = x_ref[...]
+
+    def gate_of():
+        logits = mm_nt(x, centroid_ref[...])[:, :1]
+        return 1.0 / (1.0 + jnp.exp(-logits))
+
+    @pl.when(chunk == 0)
+    def _():
+        dz_ref[...] = (gate_of() * dr_ref[...].astype(F32)).astype(BF)
+        all_ref[...] = x
+        total[...] = jnp.zeros_like(total)
+        back[...] = jnp.zeros_like(back)
+
+    act, slope = gelu_pair(mm(x, win_ref[...]))
+    act = act.astype(BF)
+    act_ref[...] = act
+    total[...] += mm(act, wout_ref[...])
+    du = (slope * mm_nt(dz_ref[...], wout_ref[...])).astype(BF)
+    du_ref[...] = du
+    back[...] += mm_nt(du, win_ref[...])
+
+    @pl.when(chunk == pl.num_programs(0) - 1)
+    def _():
+        gate = gate_of()
+        result = total[...]
+        gated_ref[...] = (gate * result).astype(BF)
+        dl = jnp.sum(dr_ref[...].astype(F32) * result, axis=1, keepdims=True) * gate * (1.0 - gate)
+        dx_ref[...] = (back[...] + dl * centroid_ref[:1].astype(F32)).astype(BF)
+        term_ref[...] = jnp.broadcast_to(jnp.sum(dl * x.astype(F32), axis=0, keepdims=True), term_ref.shape)
+
+
+def expert_block(group, groups, arrived, grads, centroid, weights, earlier):
+    slots, width = arrived.shape
+    size = weights[2].shape[1]
+    own = weights[0].shape[1] // size
+    hidden = (own + 2) * size
+    whole = pl.BlockSpec((slots, width), lambda j: (0, 0))
+    shared = pl.BlockSpec((slots, width), lambda j: (group, 0))
+    piece = pl.BlockSpec((slots, size), lambda j: (group, j))
+    row = pl.BlockSpec((LANES, width), lambda j: (0, 0))
+    term = pl.BlockSpec((8, width), lambda j: (0, 0))
+    win_piece = pl.BlockSpec((width, size), lambda j: (0, 0))
+    wout_piece = pl.BlockSpec((size, width), lambda j: (0, 0))
+    return pl.pallas_call(
+        expert_kernel,
+        grid=(own + 2,),
+        in_specs=[
+            whole,
+            whole,
+            row,
+            pl.BlockSpec((width, size), lambda j: (0, jnp.minimum(j, own - 1))),
+            pl.BlockSpec((size, width), lambda j: (jnp.minimum(j, own - 1), 0)),
+            win_piece,
+            win_piece,
+            wout_piece,
+            wout_piece,
+            *[pl.BlockSpec(memory_space=pl.ANY)] * len(earlier),
+        ],
+        out_specs=[piece, piece, shared, shared, whole, whole, term],
+        out_shape=[jax.ShapeDtypeStruct((groups * slots, hidden), BF)] * 2
+        + [jax.ShapeDtypeStruct((groups * slots, width), BF)] * 2
+        + [jax.ShapeDtypeStruct((slots, width), BF)] * 2
+        + [jax.ShapeDtypeStruct((8, width), F32)],
+        scratch_shapes=[pltpu.VMEM((slots, width), F32)] * 2
+        + [pltpu.VMEM((width, size), BF), pltpu.VMEM((size, width), BF)],
+        input_output_aliases={9 + i: i for i in range(len(earlier))},
+        compiler_params=pltpu.CompilerParams(vmem_limit_bytes=48 * 2**20),
+        cost_estimate=pl.CostEstimate(flops=10**6, bytes_accessed=2**16, transcendentals=0),
+    )(arrived, grads, jnp.broadcast_to(centroid[None], (LANES, width)), *weights, *earlier)
 
 
 def gather_plan(seq_size, count):
@@ -486,7 +664,7 @@
     )
 
 
-def add_into(target, index, term, rows=64):
+def copy_into(target, index, term, rows=64, add=False):
     depth = target.shape[-2]
     rows = next(n for n in (rows, 48, 32, 16, depth) if depth % n == 0)
     lead = target.shape[len(index) : -2]
@@ -501,19 +679,46 @@
             where.insert(0, block % size)
             block = block // size
         at = (*where, pl.ds(place, rows), slice(None))
-        left = target[(*index, *at)].astype(F32)
-        target[(*index, *at)] = (left + term(at).astype(F32)).astype(target.dtype)
+        value = term(at).astype(target.dtype)
+        target[(*index, *at)] = target[(*index, *at)] + value if add else value
         return carry
 
     lax.fori_loop(0, count * (depth // rows), step, 0)
 
 
-def finish_kernel(seq_size, bits, da_ref, in_ref, out_ref, proj_ref, *refs):
+def add_into(target, index, term):
+    copy_into(target, index, term, add=True)
+
+
+def finish_plan(seq_size, count):
+    last = count - 1
+    plan = [("send", 0), ("open",), ("arrive", 0, 1)]
+    ffn = [("add", index, step) for step in range(1, count) for index in (0, 1)]
+    for hop in range(2, seq_size):
+        plan += [("arrive", 0, hop)]
+        share = len(ffn) - 2 if hop == seq_size - 2 else 0
+        plan += ffn[:share]
+        ffn = ffn[share:]
+        if hop == seq_size - 2:
+            plan += [("add", 2, 0), ("add", 3, 0)]
+    if seq_size == 2:
+        plan += [("add", 2, 0), ("add", 3, 0)]
+    for item in ffn:
+        plan += [item] + ([("send", 1 + item[1])] if item[2] == last else [])
+    rest = [("add", index, step) for step in range(1, count) for index in (2, 3)] + [("proj",)]
+    for hop in range(1, seq_size):
+        share = -(-len(rest) // (seq_size - hop))
+        plan += [("arrive", 1, hop), ("arrive", 2, hop), *rest[:share]]
+        rest = rest[share:]
+    return plan + [("total", 0), ("total", 1), ("total", 2)]
+
+
+def finish_kernel(seq_size, bits, da_ref, in_ref, in_added, out_ref, out_added, proj_ref, *refs):
     count = len(bits)
     da_out, in_out, out_out, proj_out = refs[:4]
-    da_line, in_line, out_line, in_half, out_half = refs[4:9]
-    proj_parts = refs[9 : 9 + count]
-    own_sem, line_send, line_recv, half_send, half_recv, cube_send, cube_recv, proj_send, proj_recv = refs[9 + count :]
+    da_line, in_line, out_line = refs[4:7]
+    in_parts, out_parts, proj_parts = (refs[7 + i * count : 7 + (i + 1) * count] for i in range(3))
+    own_sem, keep_sem, line_send, line_recv, cube_send, cube_recv, proj_send, proj_recv = refs[7 + 3 * count :]
     z = lax.axis_index("seq")
     f = lax.axis_index("fsdp")
     bit_of = {bit: (f // bit) % 2 for bit in bits}
@@ -530,7 +735,7 @@
         pl.semaphore_signal(barrier, inc=1, device_id=flipped(bit), device_id_type=mesh_id)
     pl.semaphore_wait(barrier, seq_size - 1 + count)
 
-    lines = ((da_ref, da_line, da_out), (in_half, in_line, in_out), (out_half, out_line, out_out))
+    lines = ((da_ref, da_line, da_out), (in_parts[-1], in_line, in_out), (out_parts[-1], out_line, out_out))
 
     def line(index, side, hop, own):
         terms, sums, _ = lines[index]
@@ -600,46 +805,63 @@
 
         lax.fori_loop(0, depth // rows, step, 0)
 
-    halves = ((in_ref, in_half, bits[0]), (out_ref, out_half, bits[-2] if count > 1 else bits[0]))
-
-    def half(index):
-        source, target, bit = halves[index]
+    plain = bits[::-1]
+    turned = plain[:1] + plain[:0:-1]
+    some = seq_size // 2
+    cubes = (
+        ([in_ref, *in_parts], plain, None),
+        ([out_ref, *out_parts], turned, None),
+        ([proj_ref, *proj_parts], plain, 0),
+        ([proj_ref, *proj_parts], turned, some),
+    )
+
+    def half_of(index, step, kept):
+        states, order, _ = cubes[index]
+        where = 1 + sorted(order[step:], reverse=True).index(order[step])
+        return states[step], where, bit_of[order[step]] if kept else 1 - bit_of[order[step]]
+
+    def rows_of(index):
+        offset = cubes[index][2]
+        return slice(None) if offset is None else pl.ds(offset, some)
+
+    def cube(index, step):
+        source, where, bit = half_of(index, step, False)
+        states, order, _ = cubes[index]
         return pltpu.make_async_remote_copy(
-            src_ref=source.at[:, 1 - bit_of[bit]],
-            dst_ref=target,
-            send_sem=half_send.at[index],
-            recv_sem=half_recv.at[index],
-            device_id=flipped(bit),
-            device_id_type=mesh_id,
-        )
-
-    def half_add(index):
-        source, target, bit = halves[index]
-        half(index).wait()
-        add_into(target, (), lambda at: source[(at[0], bit_of[bit], *at[1:])])
-
-    order = bits[::-1]
-
-    def cube(step):
-        source = proj_ref if step == 0 else proj_parts[step - 1]
-        left = sorted(order[step:], reverse=True)
-        where = left.index(order[step])
-        view = source.at[(slice(None),) * (1 + where) + (1 - bit_of[order[step]],)]
-        return pltpu.make_async_remote_copy(
-            src_ref=view,
-            dst_ref=proj_parts[step],
-            send_sem=cube_send.at[step],
-            recv_sem=cube_recv.at[step],
+            src_ref=source.at[(rows_of(index),) + (slice(None),) * (where - 1) + (bit,)],
+            dst_ref=states[step + 1].at[rows_of(index)],
+            send_sem=cube_send.at[index, step],
+            recv_sem=cube_recv.at[index, step],
             device_id=flipped(order[step]),
             device_id_type=mesh_id,
         )
 
-    def cube_add(step):
-        source = proj_ref if step == 0 else proj_parts[step - 1]
-        left = sorted(order[step:], reverse=True)
-        where = 1 + left.index(order[step])
-        cube(step).wait()
-        add_into(proj_parts[step], (), lambda at: source[(*at[:where], bit_of[order[step]], *at[where:])])
+    def cube_add(index, step):
+        source, where, bit = half_of(index, step, True)
+        states, _, offset = cubes[index]
+        cube(index, step).wait()
+        for i in range(seq_size if offset is None else some):
+            row = i + (offset or 0)
+            add_into(states[step + 1], (row,), lambda at, row=row: source[(row, *at[: where - 1], bit, *at[where - 1 :])])
+        if step + 1 < count:
+            cube(index, step + 1).start()
+
+    def keep(index):
+        source, where, bit = half_of(index, 0, True)
+        return pltpu.make_async_copy(
+            source.at[(slice(None),) * where + (bit,)], cubes[index][0][1], keep_sem.at[index]
+        )
+
+    def open_cubes():
+        for index in (2, 3):
+            cube(index, 0).start()
+        for index in (0, 1):
+            keep(index).start()
+        for index, added in ((0, in_added), (1, out_added)):
+            keep(index).wait()
+            for row in range(seq_size):
+                add_into(cubes[index][0][1], (row,), lambda at, row=row: added[(row, *at)])
+            cube(index, 1).start()
 
     def proj(step):
         to = lax.rem(z + step, seq_size)
@@ -664,33 +886,14 @@
         )
         copy.wait_recv()
 
-    send_own(0)
-    half(0).start()
-    half(1).start()
-    cube(0).start()
-    cube_add(0)
-    cube(1).start() if count > 1 else None
-    half_add(0)
-    half_add(1)
-    send_own(1)
-    send_own(2)
-    for hop in range(1, seq_size):
-        arrive(0, hop)
-        if hop < count:
-            cube_add(hop)
-            if hop + 1 < count:
-                cube(hop + 1).start()
-        if hop == min(count, last) - 1 or (count == 1 and hop == 1):
-            own = pltpu.make_async_copy(proj_parts[-1].at[z], proj_out.at[z], own_sem)
-            own.start()
-            for step in range(1, seq_size):
-                proj(step).start()
-    total(0)
-    for hop in range(1, seq_size):
-        arrive(1, hop)
-        arrive(2, hop)
-    total(1)
-    total(2)
+    def proj_start():
+        pltpu.make_async_copy(proj_parts[-1].at[z], proj_out.at[z], own_sem).start()
+        for step in range(1, seq_size):
+            proj(step).start()
+
+    acts = {"send": send_own, "open": open_cubes, "add": cube_add, "arrive": arrive, "proj": proj_start, "total": total}
+    for name, *values in finish_plan(seq_size, count):
+        acts[name](*values)
     pltpu.make_async_copy(proj_parts[-1].at[z], proj_out.at[z], own_sem).wait()
     for step in range(1, seq_size):
         proj_wait(step)
@@ -709,31 +912,29 @@
     bits = fsdp_bits(False)
     count = len(bits)
     dma = pltpu.SemaphoreType.DMA
-    inside = pl.BlockSpec(memory_space=pltpu.VMEM)
-
-    def line_of(shape):
-        return pltpu.VMEM((2, seq_size - 1, *shape), BF)
-
-    order = bits[::-1]
-    parts = [pltpu.VMEM((seq_size, *[2] * (count - 1 - step), *proj.shape[-2:]), BF) for step in range(count)]
-    shapes = [v.shape[-2:] for v in (da, ffin, ffout)]
+    inside, anywhere = pl.BlockSpec(memory_space=pltpu.VMEM), pl.BlockSpec(memory_space=pl.ANY)
+    shapes = [v.shape[-2:] for v in (da, ffin[0], ffout[0])]
+
+    def parts_of(shape, first):
+        return [pltpu.VMEM((seq_size, *[2] * (count - step), *shape), BF) for step in range(first, count + 1)]
+
     return pl.pallas_call(
         functools.partial(finish_kernel, seq_size, bits),
-        in_specs=[inside] * 4,
+        in_specs=[inside, anywhere, inside, anywhere, inside, inside],
         out_specs=[inside] * 4,
         out_shape=[jax.ShapeDtypeStruct(shape, F32) for shape in shapes]
         + [jax.ShapeDtypeStruct((seq_size, *proj.shape[-2:]), BF)],
         scratch_shapes=[
-            *[line_of(shape) for shape in shapes],
-            *[pltpu.VMEM((seq_size, *shape), BF) for shape in shapes[1:]],
-            *parts,
+            *[pltpu.VMEM((2, seq_size - 1, *shape), BF) for shape in shapes],
+            *parts_of(shapes[1], 1),
+            *parts_of(shapes[2], 1),
+            *parts_of(proj.shape[-2:], 1),
             dma,
+            dma((2,)),
             dma((3, 2, seq_size - 1)),
             dma((3, 2, seq_size - 1)),
-            dma((2,)),
-            dma((2,)),
-            dma((len(order),)),
-            dma((len(order),)),
+            dma((4, count)),
+            dma((4, count)),
             dma((seq_size - 1,)),
             dma((seq_size - 1,)),
         ],
@@ -741,7 +942,7 @@
             collective_id=1, has_side_effects=True, vmem_limit_bytes=56 * 2**20
         ),
         cost_estimate=pl.CostEstimate(flops=0, bytes_accessed=100 * 2**20, transcendentals=0),
-    )(da, ffin, ffout, proj)
+    )(da, *ffin, *ffout, proj)
 
 
 def whole_tiles(shard, rows=16):
@@ -786,7 +987,7 @@
     slices = qkv_proj.reshape(3, depth, seq_size, cols).transpose(2, 1, 0, 3).reshape(seq_size, depth, 3 * cols)
     slices = jnp.concatenate([slices, jnp.broadcast_to(out_proj[None], (seq_size, depth, width))], axis=2)
     small = jnp.concatenate([norm_gains.reshape(-1), norm_biases.reshape(-1), centroids[0]])
-    spare = 32 - depth % 16 if depth % 16 else 16
+    spare = 16 - depth % 16
     extra = jnp.stack([jnp.pad(v, (0, wide - v.shape[0])) for v in (small, routes.reshape(tokens).astype(BF))])
     extra = jnp.pad(extra, ((0, spare - 2), (0, 0)))[None]
     extra = jnp.broadcast_to(extra, (seq_size, spare, wide))
@@ -805,18 +1006,23 @@
     gain_rows, bias_rows = rows_of[:3], rows_of[3:]
     mine = small[:, :, 6 * depth : 6 * depth + cols]
     centroid = lax.dynamic_index_in_dim(mine, lax.axis_index("fsdp"), 1, keepdims=False).reshape(width)
-    win_mine, wout_mine, dr_mine = after((expert_in[0], expert_out[0], out_grad.reshape(tokens, width)), inputs_all)
+    inputs_all, win_mine, wout_mine, dr_mine = tie(
+        inputs_all, expert_in[0], expert_out[0], out_grad.reshape(tokens, width)
+    )
     parts_all = norm_parts(inputs_all.astype(F32))
     normed_flat = ((inputs_all.astype(F32) - parts_all[0]) * parts_all[1] * gain_rows[0] + bias_rows[0]).astype(BF)
     projected = mm(normed_flat, qkv_mine).astype(BF).reshape(seq_size, rows, span, 3 * cols)
 
     attended_mine, lse_rows = attend(projected, id_rows, id_cols)
-    win_half, wout_half = win_mine.shape[0] // 2, wout_mine.shape[0] // 2
-    pair_in_low = seq_pair(win_mine[:win_half])
-    pair_in_high = seq_pair(win_mine[win_half:])
-    attended_mine, pair_in_low, pair_in_high = lax.optimization_barrier((attended_mine, pair_in_low, pair_in_high))
+    win_half, wout_half = win_mine.shape[1] // 2, wout_mine.shape[0] // 2
+    pair_in_low = seq_pair(win_mine[:, :win_half])
+    grad_moved = [seq_shift(dr_mine, 2 * group) for group in range(1, groups)]
+    attended_mine, pair_in_low, *grad_moved = tie(attended_mine, pair_in_low, *grad_moved)
     attended = seq_exchange(attended_mine).transpose(1, 2, 0, 3).reshape(tokens, width)
-    pair_out_low = seq_pair(after(wout_mine[:wout_half], attended))
+    attended, pair_in_high, pair_out_low, wout_high = tie(
+        attended, win_mine[:, win_half:], wout_mine[:wout_half], wout_mine[wout_half:]
+    )
+    pair_in_high, pair_out_low = seq_pair(pair_in_high), seq_pair(pair_out_low)
 
     fsdp_here = lax.axis_index("fsdp")
     routes_all = lax.dynamic_index_in_dim(proj_all[:, :, depth + 1, :tokens], fsdp_here, 1, keepdims=False)
@@ -841,113 +1047,112 @@
     def tokens_of(placing, values):
         return mm(placing, values.reshape(fsdp_size * capacity, width))
 
-    grad_own = swap_slots(slots_of(placings[0], grad_tokens)).reshape(-1, width)
+    grad_slots = [slots_of(placings[group], ([grad_tokens] + grad_moved)[group]) for group in range(groups)]
+    grad_slots = swap_slots(jnp.concatenate(grad_slots, axis=1)).reshape(fsdp_size, groups, capacity, width)
+    grad_slots = [grad_slots[:, group].reshape(-1, width) for group in range(groups)]
 
 
     resid_in = tokens_in.astype(F32)
     middle = resid_in + mm(attended, out_all)
-    parts_two = norm_parts(middle)
-    hidden_low = ((middle - parts_two[0]) * parts_two[1] * gain_rows[1] + bias_rows[1]).astype(BF)
-    active, active_slope = gelu_pair(mm(hidden_low, ffin_all))
-    active_low, active_slope = lax.optimization_barrier((active.astype(BF), active_slope.astype(BF)))
-    block_out = middle + mm(active_low, ffout_all)
-    parts_three = norm_parts(block_out)
-    routed = ((block_out - parts_three[0]) * parts_three[1] * gain_rows[2] + bias_rows[2]).astype(BF)
-
-    routed, pair_out_low = lax.optimization_barrier((routed, pair_out_low))
+    gains_pad, biases_pad = jnp.pad(gain_rows, ((0, 5), (0, 0))), jnp.pad(bias_rows, ((0, 5), (0, 0)))
+    hidden_low, active_low, active_slope, block_out, routed = ffn_forward(
+        middle, gains_pad, biases_pad, ffin_all, ffout_all
+    )
+    routed, wout_high, pair_in_high, pair_out_low, *grad_slots = tie(
+        routed, wout_high, pair_in_high, pair_out_low, *grad_slots
+    )
     slots_own = slots_of(placings[0], routed)
-    pair_out_high = seq_pair(after(wout_mine[wout_half:], slots_own))
-    win = jnp.concatenate([win_mine, jnp.concatenate([pair_in_low, pair_in_high], axis=0)], axis=1)
-
-    arrived_all, dz_all, du_all, act_all, back_terms, back_slots, gated_all = [], [], [], [], [], [], []
-    centroid_term = jnp.zeros((width,), F32)
+    pair_out_high = seq_pair(wout_high)
+
+    arrived = [swap_slots(slots_own).reshape(-1, width)]
+    for group in range(1, groups):
+        routed_here = seq_shift(routed, 2 * group)
+        routed_here, pair_out_high = tie(routed_here, pair_out_high)
+        slots_here = slots_of(placings[group], routed_here)
+        slots_here, pair_out_high, *arrived = tie(slots_here, pair_out_high, *arrived)
+        arrived.append(swap_slots(slots_here).reshape(-1, width))
+    weights = (win_mine, wout_mine, pair_in_low, pair_in_high, pair_out_low, pair_out_high)
+    shared, gateds, rows_grads, terms = (), [], [], []
     for group in range(groups):
-        if group == 0:
-            arrived, grad_arrived = swap_slots(slots_own).reshape(-1, width), grad_own
-        else:
-            slots_here = slots_of(placings[group], after(seq_shift(routed, 2 * group), act))
-            arrived = swap_slots(slots_here).reshape(-1, width)
-            grads_here = seq_shift(after(dr_mine, slots_own), 2 * group)
-            grads_here = slots_of(placings[group], after(grads_here, slots_here))
-            grad_arrived = swap_slots(grads_here).reshape(-1, width)
-        gate = jax.nn.sigmoid(mm(arrived, centroid))
-        act, slope = gelu_pair(mm(arrived, win))
-        act, slope = lax.optimization_barrier((act.astype(BF), slope.astype(BF)))
-        if group == 0:
-            wout = jnp.concatenate([wout_mine, pair_out_low, after(pair_out_high, act)], axis=0)
-        result = mm(act, wout)
-        gated_low = (gate[:, None] * result).astype(BF).reshape(fsdp_size, capacity, width)
-        gated = grad_arrived.astype(F32)
-        dz = (gate[:, None] * gated).astype(BF)
-        dl = jnp.sum(gated * result, axis=-1) * gate * (1.0 - gate)
-        du = (slope.astype(F32) * mm_nt(dz, wout)).astype(BF)
-        rows_grad = mm_nt(du, win) + dl[:, None] * centroid.astype(F32)
-        centroid_term = centroid_term + jnp.sum(dl[:, None] * arrived.astype(F32), axis=0)
-        back = swap_slots(rows_grad.astype(BF).reshape(fsdp_size, capacity, width))
-        back_slots.append(back)
-        back = tokens_of(placings[group], back)
+        *shared, gated, rows_grad, term = expert_block(
+            group, groups, arrived[group], grad_slots[group], centroid, weights, shared
+        )
+        gateds.append(gated)
+        rows_grads.append(rows_grad)
+        terms.append(term)
+    act, du, dz, arrived = shared
+
+    half = expert_in.shape[2]
+    in_sent = mm_tn(arrived, du[:, half:]).astype(BF)
+    back_low = [None] * groups
+    for group in reversed(range(groups)):
+        rows_grad = rows_grads[group].reshape(fsdp_size, capacity, width)
+        if group + 1 < groups:
+            rows_grad, back_low[group + 1] = tie(rows_grad, back_low[group + 1])
+        back_slots = swap_slots(rows_grad)
+        if group + 1 == groups:
+            back_slots, in_sent = tie(back_slots, in_sent)
+        back_low[group] = tokens_of(placings[group], back_slots)
         if group:
-            back = seq_shift(back.astype(BF), -2 * group).astype(F32)
-        back_terms.append(back)
-        gated_all.append(gated_low)
-        arrived_all.append(arrived)
-        dz_all.append(dz)
-        du_all.append(du)
-        act_all.append(act)
-
-    half = expert_in.shape[2]
-    arrived, dz, du, act = (jnp.concatenate(v, axis=0) for v in (arrived_all, dz_all, du_all, act_all))
-    in_sent = mm_tn(arrived, du[:, half:]).astype(BF)
+            back_low[group] = back_low[group].astype(BF)
+    in_pair = seq_pair(in_sent)
+    gated_all = jnp.concatenate([gated.reshape(fsdp_size, capacity, width) for gated in gateds], axis=1)
+    if groups > 1:
+        gated_all, arrived, act, du, back_low[-1] = tie(gated_all, arrived, act, du, back_low[-1])
+    back_sum = back_low[0]
+    for group in range(1, groups):
+        back_sum = back_sum + seq_shift(back_low[group], -2 * group).astype(F32)
+    centroid_term = sum(term[0] for term in terms)
     out_sent = mm_tn(act[:, half:], dz).astype(BF)
     in_kept = mm_tn(arrived, du[:, :half])
     out_kept = mm_tn(act[:, :half], dz)
-    in_pair = seq_pair(after(in_sent, in_kept, out_kept))
-
-    gated_back = swap_slots(after(jnp.concatenate(gated_all, axis=1), *back_slots))
-    gated_back = gated_back.reshape(fsdp_size, groups, capacity, width)
+
+    gated_back = swap_slots(gated_all).reshape(fsdp_size, groups, capacity, width)
     out_terms = [tokens_of(placings[group], gated_back[:, group]) for group in range(groups)]
-    back_sum, in_sent, out_sent, in_kept, out_kept, *out_terms = lax.optimization_barrier(
-        (sum(back_terms), in_sent, out_sent, in_kept, out_kept, out_terms[0], *(v.astype(BF) for v in out_terms[1:]))
-    )
-
-    block_norm_grad, gain_three, bias_three = norm_back(block_out, parts_three, gain_rows[2], back_sum)
-    block_grad = grad_tokens.astype(F32) + block_norm_grad
-    block_low = block_grad.astype(BF)
-    hidden_grad = (active_slope.astype(F32) * mm_nt(block_low, ffout_all)).astype(BF)
-    normed_two_grad = mm_nt(hidden_grad, ffin_all)
-    middle_norm_grad, gain_two, bias_two = norm_back(middle, parts_two, gain_rows[1], normed_two_grad)
-    middle_grad = block_grad + middle_norm_grad
-    branch = middle_grad.astype(BF)
+    back_sum, out_sent, in_kept, out_kept, *out_terms = tie(
+        back_sum, out_sent, in_kept, out_kept, out_terms[0], *(v.astype(BF) for v in out_terms[1:])
+    )
+
+    block_low, hidden_grad, middle_grad, branch, dense_rows = ffn_backward(
+        back_sum, block_out, grad_tokens, middle, gains_pad, active_slope, ffin_all, ffout_all
+    )
+    gain_three, bias_three, gain_two, bias_two = (dense_rows[i] for i in range(4))
     attended_grad = mm_nt(branch, out_all).astype(BF)
     attended_grad = attended_grad.reshape(rows, span, seq_size, cols).transpose(2, 0, 1, 3)
-    attended_grad, in_pair = lax.optimization_barrier((attended_grad, in_pair))
-    active_low, hidden_low = after((active_low, hidden_low), attended_grad)
-    attended_grad = seq_exchange(attended_grad)
-
-    ffout_terms = hyper_split(by_device(mm_tn(active_low, block_low)))
-    ffin_terms = hyper_split(by_device(mm_tn(hidden_low, hidden_grad)))
-    out_proj_term = mm_tn(attended, branch)
-    ffout_terms = hyper_scatter_step(ffout_terms, crossed[-1])
-    ffin_terms = hyper_scatter_step(ffin_terms, bits[-1])
-    attended_grad, ffout_terms, ffin_terms = lax.optimization_barrier((attended_grad, ffout_terms, ffin_terms))
-    out_pair = seq_pair(after(out_sent, attended_grad))
-    out_terms = out_terms[:1] + [
-        seq_shift(after(out_terms[group], attended_grad), -2 * group) for group in range(1, groups)
-    ]
-    ffout_terms = hyper_scatter(ffout_terms, crossed[-2:0:-1])
-    ffin_terms = hyper_scatter(ffin_terms, bits[-2:0:-1])
+    attended_grad, in_pair, active_low, hidden_low, attended = tie(
+        attended_grad, in_pair, active_low, hidden_low, attended
+    )
+    attended_grad = seq_exchange(attended_grad, True)
+
+    def halved(term):
+        terms = hyper_split(by_device(term))
+        sent = lax.dynamic_index_in_dim(terms, 1 - fsdp_here % 2, terms.ndim - 3, keepdims=False)
+        return terms, fsdp_flip(sent, 1)
+
+    ffout_terms = halved(mm_tn(active_low, block_low))
+    ffin_terms = halved(mm_tn(hidden_low, hidden_grad))
+    proj_terms = mm_tn(attended, branch).astype(BF).reshape(seq_size, fsdp_size, depth, width)
+    proj_terms = jnp.pad(proj_terms, ((0, 0), (0, 0), (0, spare), (3 * cols, 0)))
+    def halves(values):
+        return values[: values.shape[0] // 2], values[values.shape[0] // 2 :]
+
+    out_halves = [halves(values) for values in [out_sent, *out_terms[1:]]]
+    attended_grad, *out_first = tie(attended_grad, *[first for first, _ in out_halves])
+    out_first = [seq_pair(out_first[0])] + [seq_shift(out_first[group], -2 * group) for group in range(1, groups)]
 
     dq, dk, dv = attend_back(projected, attended_grad, lse_rows, id_rows, id_cols)
     projected_grad = jnp.concatenate([dq, dk, dv], axis=-1).reshape(seq_size * tokens, 3 * cols)
-    projected_grad, out_pair = lax.optimization_barrier((projected_grad, out_pair))
+    sizes = len(out_first)
+    projected_grad, *moved = tie(projected_grad, *out_first, *[second for _, second in out_halves])
+    out_first, out_second = moved[:sizes], moved[sizes:]
+    out_second = [seq_pair(out_second[0])] + [seq_shift(out_second[group], -2 * group) for group in range(1, groups)]
     normed_low_terms = mm_nt(projected_grad, qkv_mine).astype(BF)
     unit_all = (inputs_all.astype(F32) - parts_all[0]) * parts_all[1]
     terms_wide = normed_low_terms.astype(F32)
     gain_one, bias_one = jnp.sum(terms_wide * unit_all, axis=0), jnp.sum(terms_wide, axis=0)
     small_terms = jnp.stack([gain_one, gain_two, gain_three, bias_one, bias_two, bias_three])
 
-    proj_terms = jnp.concatenate([mm_tn(normed_flat, projected_grad).astype(BF), out_proj_term.astype(BF)], axis=1)
-    proj_terms = proj_terms.reshape(seq_size, fsdp_size, depth, wide)
+    qkv_term = mm_tn(normed_flat, projected_grad).astype(BF).reshape(seq_size, fsdp_size, depth, 3 * cols)
     small_rows = small_terms.astype(BF).reshape(6, seq_size, fsdp_size, depth).transpose(1, 2, 0, 3)
     small_rows = small_rows.reshape(seq_size, fsdp_size, 1, 6 * depth)
     small_rows = jnp.pad(small_rows, ((0, 0), (0, 0), (0, spare - 1), (0, wide - 6 * depth)))
@@ -955,14 +1160,14 @@
         (jnp.arange(fsdp_size) == fsdp_here)[None, :, None], centroid_term.reshape(seq_size, 1, cols), 0.0
     )
     small_rows = lax.dynamic_update_slice(small_rows, centroid_rows.astype(BF)[:, :, None], (0, 0, 1, 0))
-    proj_terms = hyper_split(jnp.concatenate([proj_terms, small_rows], axis=2))
-    proj_terms, *out_terms = lax.optimization_barrier((proj_terms, *out_terms))
-    outputs = block_out + sum(v.astype(F32) for v in out_terms)
+    proj_terms = lax.dynamic_update_slice(proj_terms, qkv_term, (0, 0, 0, 0))
+    proj_terms = hyper_split(lax.dynamic_update_slice(proj_terms, small_rows, (0, 0, depth, 0)))
+    proj_terms, *out_second = tie(proj_terms, *out_second)
+    out_pair, *out_moved = [jnp.concatenate(v, axis=0) for v in zip(out_first, out_second, strict=True)]
+    outputs = block_out + out_terms[0] + sum(v.astype(F32) for v in out_moved)
     outputs = outputs.astype(BF).reshape(rows, span, width)
-    last_in = ffin_terms.reshape(seq_size, 2, *ffin_terms.shape[-2:])
-    last_out = ffout_terms.reshape(seq_size, 2, *ffout_terms.shape[-2:])
     normed_one_grad, ffn_in_grad, ffn_out_grad, proj_sums = finish_sums(
-        normed_low_terms.reshape(seq_size, tokens, width), last_in, last_out, proj_terms
+        normed_low_terms.reshape(seq_size, tokens, width), ffin_terms, ffout_terms, proj_terms
     )
     ffn_in_grad, ffn_out_grad = ffn_in_grad.reshape(ffn_in.shape), ffn_out_grad.reshape(ffn_out.shape)
     proj_sums = proj_sums.astype(F32)

time: 911 us -> 817 us (0.90)
  Pallas kernels: 289 us -> 392 us
  matrix products: 188 us -> 90.3 us
  other arithmetic: 75.4 us -> 38.7 us
  waiting for transfers between devices: 196 us -> 161 us
  local copies, waits for them, and re-layouts: 89 us -> 70.5 us
    pallas_call x0 -> x4, Pallas kernels: none -> 86.1 us  [the longest x2 46.5 us: expert_block(): pl.pallas_call(expert_kernel, grid=(own + 2,), in_specs=[whole, whole, ro...]
    dot_general x16 -> x8, matrix products: 67.4 us -> 23.8 us  [mm(): return jnp.dot(left, right, preferred_element_type=F32)]
    dot_general x8 -> x2, matrix products: 51.3 us -> 7.72 us  [mm_nt(): lax.dot_general(left, right, (((1,), (1,)), ((), ())), preferred_element_...]
    ppermute x6 -> x7, waiting for transfers between devices: 52.5 us -> 21 us  [seq_pair(): return lax.ppermute(values, 'seq', [(i, i ^ 1) for i in range(size)])]
    convert_element_type x6 -> x0, other arithmetic: 18.7 us -> none  [the longest x2 13.7 us: hyper_scatter_step(): return (kept.astype(F32) + arrived.astype(F32)).astype(BF)]
    pallas_call x1, Pallas kernels: 121 us -> 138 us  [finish_sums(): pl.pallas_call(functools.partial(finish_kernel, seq_size, bits), in_specs...]
    concatenate x3 -> x0, local copies, waits for them, and re-layouts: 12.3 us -> none  [the longest x1 5.89 us: on_device(): jnp.concatenate([mm_tn(normed_flat, projected_grad).astype(BF), out_proj_...]
    ppermute x10 -> x11, starting transfers between devices: 13.4 us -> 24.5 us  [seq_shift(): lax.ppermute(values, 'seq', [(i, (i + step) % size) for i in range(size)])]
  transfers between devices with their start and end apart: 27 -> 26, of which waited for: 13 -> 15; matrix products, arithmetic and copies ran while one was open for 30% -> 18% of each run, Pallas kernels for 5% -> 13%
where the time goes in v3:
time: 817 us; the launch traced here: 812 us
  Pallas kernels  392 us (48%)
  waiting for transfers between devices  161 us (20%)
  matrix products  90.3 us (11%)
  local copies, waits for them, and re-layouts  70.5 us (9%)
  starting transfers between devices  57.8 us (7%)
  other arithmetic  38.7 us (5%)
    pallas_call x1, Pallas kernels, finish_sums(): pl.pallas_call(functools.partial(finish_kernel, seq_size, bits), in_specs...  138 us
    pallas_call x1, Pallas kernels, start_gathers(): pl.pallas_call(functools.partial(gather_kernel, seq_size, bits), in_specs...  127 us
    ppermute x11, waiting for transfers between devices, seq_shift(): lax.ppermute(values, 'seq', [(i, (i + step) % size) for i in range(size)])  110 us
    dot_general x12, matrix products, mm_tn(): lax.dot_general(left, right, (((0,), (0,)), ((), ())), preferred_element_...  58.8 us
    pallas_call x2, Pallas kernels, expert_block(): pl.pallas_call(expert_kernel, grid=(own + 2,), in_specs=[whole, whole, ro...  46.5 us
    all_to_all x6, waiting for transfers between devices, swap_slots(): lax.all_to_all(values, 'fsdp', split_axis=0, concat_axis=0, tiled=True)  30.1 us
    all_to_all x6, starting transfers between devices, swap_slots(): lax.all_to_all(values, 'fsdp', split_axis=0, concat_axis=0, tiled=True)  26.5 us
    ppermute x11, starting transfers between devices, seq_shift(): lax.ppermute(values, 'seq', [(i, (i + step) % size) for i in range(size)])  24.5 us
  transfers between devices with their start and end apart: 26, of which 15 were waited for; matrix products, arithmetic and copies ran while one was open for 18% of the time, Pallas kernels for 13%

profile of v3, /device:TPU:0, one launch (start us, length us, event | category | flops | bytes accessed | tf_op | source)
XLA Modules:
  0.0 812.1 jit_solution(3666878159832588293)
XLA Ops:
  7.2 127.1 %shard_map.212 = (bf16[4,2,2,2,48,1792]{5,4,3,2,1,0:T(8,128)(2,1)}, bf16[4,2,2,2,32,4096]{5,4,3,2,1,0:T(8,128)(2,1)}, bf16[4,2,2,2,128,1024]{5,4,3,2,1,0:T(8,128)(2,1)}, bf16[4,512,1024]{2,1,0:T(8,128)(2,1)}) custom-call(bf16[4,48,1792]{2,1,0:T(8,128)(2,1)} %pad_maximum_fusion.3.proj_ref, bf16[32,4096]{1,0:T(8,128)(2,1)} %in_ref.1, ...), custom_call_target="tpu_custom_call" | custom-call | bytes 104857600 | tf_op jit(solution)/shard_map/pallas_call | solution.py:635
  153.3 6.9 convolution_convert_fusion.3
  160.3 19.7 %shard_map.213 = (bf16[4,2,256,256]{3,2,1,0:T(8,128)(2,1)S(1)}, f32[2,2,2,1024]{3,2,1,0:T(2,128)S(1)}) custom-call(bf16[4,2,256,768]{3,2,1,0:T(8,128)(2,1)S(1)} %bitcast.127, bf16[4,2,256,768]{3,2,1,0:T(8,128)(2,1)S(1)} %bitcast.128, bf16[4,2,256,768]{3,2,1,0:T(8,128)(2,1)S(1)} %bitcast.129, s32[2,1,1024]{2,1,0:T(1,128)S(1)} %fusion.56.id_row_ref, ...), custom_call_target="tpu_custom_call" | custom-call | flops 1000000 | bytes 65536 | tf_op jit(solution)/shard_map/pallas_call | solution.py:192
  203.3 6.0 collective-permute-done.2
  210.3 9.6 %collective-permute-done.3 = bf16[2,256,256]{2,1,0:T(8,128)(2,1)} collective-permute-done((bf16[2,256,256]{2,1,0:T(8,128)(2,1)}, bf16[2,256,256]{2,1,0:T(8,128)(2,1)}, u32[]{:S(2)}, u32[]{:S(2)}) %collective-permute-start.3) | collective-permute-done | bytes 262176 | tf_op jit(solution)/shard_map/ppermute | solution.py:64
  235.2 18.6 %shard_map.214 = (bf16[512,1024]{1,0:T(8,128)(2,1)S(1)}, bf16[512,4096]{1,0:T(8,128)(2,1)}, bf16[512,4096]{1,0:T(8,128)(2,1)}, f32[512,1024]{1,0:T(8,128)S(1)}, bf16[512,1024]{1,0:T(8,128)(2,1)}) custom-call(f32[512,1024]{1,0:T(8,128)} %convert_add_fusion.middle_ref, f32[8,1024]{1,0:T(8,128)S(1)} %pad.30.gains_ref, f32[8,1024]{1,0:T(8,128)S(1)} %pad.31.biases_ref, ...), custom_call_target="tpu_custom_call" | custom-call | flops 1000000 | bytes 65536 | tf_op jit(solution)/shard_map/pallas_call | solution.py:285
  260.1 12.4 %collective-permute-done.6.wout_low = bf16[512,1024]{1,0:T(8,128)(2,1)S(1)} collective-permute-done((bf16[512,1024]{1,0:T(8,128)(2,1)}, bf16[512,1024]{1,0:T(8,128)(2,1)S(1)}, u32[]{:S(2)}, u32[]{:S(2)}) %collective-permute-start.6) | collective-permute-done | bytes 1048608 | tf_op jit(solution)/shard_map/ppermute | solution.py:69
  283.7 45.7 %collective-permute-done.7 = bf16[512,1024]{1,0:T(8,128)(2,1)S(1)} collective-permute-done((bf16[512,1024]{1,0:T(8,128)(2,1)}, bf16[512,1024]{1,0:T(8,128)(2,1)S(1)}, u32[]{:S(2)}, u32[]{:S(2)}) %collective-permute-start.7) | collective-permute-done | bytes 1048608 | tf_op jit(solution)/shard_map/ppermute | solution.py:64
  337.0 23.2 %shard_map.215 = (bf16[1536,2048]{1,0:T(8,128)(2,1)}, bf16[1536,2048]{1,0:T(8,128)(2,1)}, bf16[1536,1024]{1,0:T(8,128)(2,1)}, bf16[1536,1024]{1,0:T(8,128)(2,1)}...) custom-call(bf16[768,1024]{1,0:T(8,128)(2,1)} %bitcast.30.x_ref, ...), custom_call_target="tpu_custom_call" | custom-call | flops 1000000 | bytes 65536 | tf_op jit(solution)/shard_map/pallas_call | solution.py:406
  361.4 23.3 %shard_map.216 = (bf16[1536,2048]{1,0:T(8,128)(2,1)}, bf16[1536,2048]{1,0:T(8,128)(2,1)}, bf16[1536,1024]{1,0:T(8,128)(2,1)}, bf16[1536,1024]{1,0:T(8,128)(2,1)}...) custom-call(bf16[768,1024]{1,0:T(8,128)(2,1)} %bitcast.32.x_ref, ...), custom_call_target="tpu_custom_call", output_to_operand_aliasing={{0}: (9, {}), {1}: (10, {}), {2}: (11, {}), {3}: (12, {})} | custom-call | flops 1000000 | bytes 65536 | tf_op jit(solution)/shard_map/pallas_call | solution.py:406
  390.8 6.6 fusion.25
  397.4 14.5 %all-to-all-done.3 = bf16[8,96,1024]{2,1,0:T(8,128)(2,1)} async-done(((bf16[8,96,1024]{2,1,0:T(8,128)(2,1)}), bf16[8,96,1024]{2,1,0:T(8,128)(2,1)}, u32[]{:S(2)}, u32[]{:S(2)}) %all-to-all-start.3) | async-done | bytes 1572896 | tf_op jit(solution)/shard_map/all_to_all | solution.py:1045
  428.1 12.8 %all-to-all-done.4 = bf16[8,96,1024]{2,1,0:T(8,128)(2,1)} async-done(((bf16[8,96,1024]{2,1,0:T(8,128)(2,1)}), bf16[8,96,1024]{2,1,0:T(8,128)(2,1)}, u32[]{:S(2)}, u32[]{:S(2)}) %all-to-all-start.4) | async-done | bytes 1572896 | tf_op jit(solution)/shard_map/all_to_all | solution.py:1045
  444.6 8.4 %fusion.8 = f32[1024,1024]{1,0:T(8,128)} fusion(bf16[1536,1024]{1,0:T(8,128)(2,1)} %get-tuple-element.150, bf16[1536,2048]{1,0:T(8,128)(2,1)} %get-tuple-element.149), kind=kOutput, calls=%fused_computation.21 | convolution fusion | flops 3221225472 | bytes 10485760 | tf_op jit(solution)/shard_map/dot_general | solution.py:39
  453.0 6.8 fusion.28
  465.6 9.9 %collective-permute-done.9 = bf16[512,1024]{1,0:T(8,128)(2,1)} collective-permute-done((bf16[512,1024]{1,0:T(8,128)(2,1)}, bf16[512,1024]{1,0:T(8,128)(2,1)}, u32[]{:S(2)}, u32[]{:S(2)}) %collective-permute-start.9) | collective-permute-done | bytes 1048608 | tf_op jit(solution)/shard_map/ppermute | solution.py:64
  487.5 21.1 %shard_map.217 = (bf16[512,1024]{1,0:T(8,128)(2,1)S(1)}, bf16[512,4096]{1,0:T(8,128)(2,1)}, f32[512,1024]{1,0:T(8,128)S(1)}, bf16[512,1024]{1,0:T(8,128)(2,1)S(1)}, f32[8,1024]{1,0:T(8,128)S(1)}) custom-call(f32[512,1024]{1,0:T(8,128)} %convert_add_fusion.1.back_ref, f32[512,1024]{1,0:T(8,128)} %copy-done.3, bf16[512,1024]{1,0:T(8,128)(2,1)} %bitcast.5.grad_ref, ...), custom_call_target="tpu_custom_call" | custom-call | flops 1000000 | bytes 65536 | tf_op jit(solution)/shard_map/pallas_call | solution.py:336
  514.8 5.6 collective-permute-done.10
  521.7 7.1 convolution_convert_fusion
  545.9 11.2 %collective-permute-done.12 = bf16[2,256,256]{2,1,0:T(8,128)(2,1)S(1)} collective-permute-done((bf16[2,256,256]{2,1,0:T(8,128)(2,1)S(1)}, bf16[2,256,256]{2,1,0:T(8,128)(2,1)S(1)}, u32[]{:S(2)}, u32[]{:S(2)}) %collective-permute-start.12) | collective-permute-done | bytes 262176 | tf_op jit(solution)/shard_map/ppermute | solution.py:64
  582.7 21.1 %shard_map.218 = (bf16[4,2,256,256]{3,2,1,0:T(8,128)(2,1)S(1)}, bf16[4,2,256,256]{3,2,1,0:T(8,128)(2,1)S(1)}, bf16[4,2,256,256]{3,2,1,0:T(8,128)(2,1)S(1)}) custom-call(bf16[4,2,256,768]{3,2,1,0:T(8,128)(2,1)} %bitcast.130, bf16[4,2,256,768]{3,2,1,0:T(8,128)(2,1)} %bitcast.131, bf16[4,2,256,768]{3,2,1,0:T(8,128)(2,1)} %bitcast.132, ...), custom_call_target="tpu_custom_call" | custom-call | flops 1000000 | bytes 65536 | tf_op jit(solution)/shard_map/pallas_call | solution.py:212
  616.2 8.3 %convolution_convert_fusion.9 = bf16[1024,768]{1,0:T(8,128)(2,1)} fusion(bf16[2048,768]{1,0:T(8,128)(2,1)} %bitcast.167, bf16[2048,1024]{1,0:T(8,128)(2,1)} %bitcast.155, f32[1024]{0:T(1024)S(1)} %copy-done.50, f32[1024]{0:T(1024)S(1)} %mul.82, f32[2048]{0:T(1024)S(1)} %copy-done.48, f32[2048]{0:T(1024)S(1)} %copy-done.45), kind=kOutput, calls=%fused_computation.53 | convolution fusion | flops 3234594816 | bytes 8937472 | tf_op jit(solution)/shard_map/dot_general | solution.py:39
  631.0 19.6 %collective-permute-done.17 = bf16[256,1024]{1,0:T(8,128)(2,1)S(1)} collective-permute-done((bf16[256,1024]{1,0:T(8,128)(2,1)}, bf16[256,1024]{1,0:T(8,128)(2,1)S(1)}, u32[]{:S(2)}, u32[]{:S(2)}) %collective-permute-start.17) | collective-permute-done | bytes 524320 | tf_op jit(solution)/shard_map/ppermute | solution.py:64
  659.6 137.6 %shard_map.219 = (f32[512,1024]{1,0:T(8,128)}, f32[32,4096]{1,0:T(8,128)}, f32[128,1024]{1,0:T(8,128)}, bf16[4,48,1792]{2,1,0:T(8,128)(2,1)}) custom-call(bf16[4,512,1024]{2,1,0:T(8,128)(2,1)} %bitcast.152, bf16[4,2,2,2,32,4096]{5,4,3,2,1,0:T(8,128)(2,1)} %bitcast.145, bf16[4,2,2,32,4096]{4,3,2,1,0:T(8,128)(2,1)} %collective-permute-done.18.in_added, ...), custom_call_target="tpu_custom_call" | custom-call | bytes 104857600 | tf_op jit(solution)/shard_map/pallas_call | solution.py:921
  (299 shorter events, 226.8 us)
Async XLA Ops:
  135.8 48.0 %collective-permute-start = (bf16[1024,512]{1,0:T(8,128)(2,1)}, bf16[1024,512]{1,0:T(8,128)(2,1)}, u32[]{:S(2)}, u32[]{:S(2)}) collective-permute-start(bf16[1024,512]{1,0:T(8,128)(2,1)} %get-tuple-element.223), channel_id=1, source_target_pairs={{0,8},{8,0},{16,24},{24,16},{1,9},{9,1},{17,25},{25,17},{2,10},{10... | collective-permute-start | bytes 3145736 | tf_op jit(solution)/shard_map/ppermute | solution.py:69
  135.8 50.8 %collective-permute-start.1 = (bf16[512,1024]{1,0:T(8,128)(2,1)}, bf16[512,1024]{1,0:T(8,128)(2,1)}, u32[]{:S(2)}, u32[]{:S(2)}) collective-permute-start(bf16[512,1024]{1,0:T(8,128)(2,1)} %bitcast.5.grad_ref), channel_id=1, source_target_pairs={{0,16},{8,24},{16,0},{24,8},{1,17},{9,25},{17,1},{25,9},{2,18},{10... | collective-permute-start | bytes 3145736 | tf_op jit(solution)/shard_map/ppermute | solution.py:64
  191.0 65.2 %all-to-all-start = ((bf16[8,192,1024]{2,1,0:T(8,128)(2,1)}), bf16[8,192,1024]{2,1,0:T(8,128)(2,1)}, u32[]{:S(2)}, u32[]{:S(2)}) async-start(bf16[8,192,1024]{2,1,0:T(8,128)(2,1)} %pad_maximum_fusion), calls=%async_computation | async-start | bytes 6291456 | tf_op jit(solution)/shard_map/all_to_all | solution.py:1045
  198.3 21.6 %collective-permute-start.3 = (bf16[2,256,256]{2,1,0:T(8,128)(2,1)}, bf16[2,256,256]{2,1,0:T(8,128)(2,1)}, u32[]{:S(2)}, u32[]{:S(2)}) collective-permute-start(bf16[2,256,256]{2,1,0:T(8,128)(2,1)} %get-tuple-element.231), channel_id=1, source_target_pairs={{0,16},{8,24},{16,0},{24,8},{1,17},{9,25},{17,1},{25,9},{2,18},{10... | collective-permute-start | bytes 786440 | tf_op jit(solution)/shard_map/ppermute | solution.py:64
  202.4 18.5 %collective-permute-start.4 = (bf16[2,256,256]{2,1,0:T(8,128)(2,1)}, bf16[2,256,256]{2,1,0:T(8,128)(2,1)S(1)}, u32[]{:S(2)}, u32[]{:S(2)}) collective-permute-start(bf16[2,256,256]{2,1,0:T(8,128)(2,1)} %get-tuple-element.230), channel_id=1, source_target_pairs={{0,24},{8,0},{16,8},{24,16},{1,25},{9,1},{17,9},{25,17},{2,26},{10... | collective-permute-start | bytes 786440 | tf_op jit(solution)/shard_map/ppermute | solution.py:64
  223.0 37.2 %collective-permute-start.5 = (bf16[1024,512]{1,0:T(8,128)(2,1)}, bf16[1024,512]{1,0:T(8,128)(2,1)S(1)}, u32[]{:S(2)}, u32[]{:S(2)}) collective-permute-start(bf16[1024,512]{1,0:T(8,128)(2,1)} %get-tuple-element.119), channel_id=1, source_target_pairs={{0,8},{8,0},{16,24},{24,16},{1,9},{9,1},{17,25},{25,17},{2,10},{10... | collective-permute-start | bytes 3145736 | tf_op jit(solution)/shard_map/ppermute | solution.py:69
  227.2 45.4 %collective-permute-start.6 = (bf16[512,1024]{1,0:T(8,128)(2,1)}, bf16[512,1024]{1,0:T(8,128)(2,1)S(1)}, u32[]{:S(2)}, u32[]{:S(2)}) collective-permute-start(bf16[512,1024]{1,0:T(8,128)(2,1)} %get-tuple-element.120), channel_id=1, source_target_pairs={{0,8},{8,0},{16,24},{24,16},{1,9},{9,1},{17,25},{25,17},{2,10},{10... | collective-permute-start | bytes 3145736 | tf_op jit(solution)/shard_map/ppermute | solution.py:69
  276.0 55.6 %all-to-all-start.1 = ((bf16[8,96,1024]{2,1,0:T(8,128)(2,1)}), bf16[8,96,1024]{2,1,0:T(8,128)(2,1)}, u32[]{:S(2)}, u32[]{:S(2)}) async-start(bf16[8,96,1024]{2,1,0:T(8,128)(2,1)} %bitcast.183), calls=%async_computation.1 | async-start | bytes 3145728 | tf_op jit(solution)/shard_map/all_to_all | solution.py:1045
  280.3 49.0 %collective-permute-start.7 = (bf16[512,1024]{1,0:T(8,128)(2,1)}, bf16[512,1024]{1,0:T(8,128)(2,1)S(1)}, u32[]{:S(2)}, u32[]{:S(2)}) collective-permute-start(bf16[512,1024]{1,0:T(8,128)(2,1)} %get-tuple-element.122), channel_id=1, source_target_pairs={{0,16},{8,24},{16,0},{24,8},{1,17},{9,25},{17,1},{25,9},{2,18},{10... | collective-permute-start | bytes 3145736 | tf_op jit(solution)/shard_map/ppermute | solution.py:64
  281.9 47.4 %collective-permute-start.8 = (bf16[512,1024]{1,0:T(8,128)(2,1)}, bf16[512,1024]{1,0:T(8,128)(2,1)S(1)}, u32[]{:S(2)}, u32[]{:S(2)}) collective-permute-start(bf16[512,1024]{1,0:T(8,128)(2,1)} %get-tuple-element.123), channel_id=1, source_target_pairs={{0,8},{8,0},{16,24},{24,16},{1,9},{9,1},{17,25},{25,17},{2,10},{10... | collective-permute-start | bytes 3145736 | tf_op jit(solution)/shard_map/ppermute | solution.py:69
  331.6 29.8 %all-to-all-start.2 = ((bf16[8,96,1024]{2,1,0:T(8,128)(2,1)}), bf16[8,96,1024]{2,1,0:T(8,128)(2,1)}, u32[]{:S(2)}, u32[]{:S(2)}) async-start(bf16[8,96,1024]{2,1,0:T(8,128)(2,1)} %bitcast.180), calls=%async_computation.2 | async-start | bytes 3145728 | tf_op jit(solution)/shard_map/all_to_all | solution.py:1045
  385.9 26.0 %all-to-all-start.3 = ((bf16[8,96,1024]{2,1,0:T(8,128)(2,1)}), bf16[8,96,1024]{2,1,0:T(8,128)(2,1)}, u32[]{:S(2)}, u32[]{:S(2)}) async-start(bf16[8,96,1024]{2,1,0:T(8,128)(2,1)} %bitcast.181), calls=%async_computation.3 | async-start | bytes 3145728 | tf_op jit(solution)/shard_map/all_to_all | solution.py:1045
  415.3 25.6 %all-to-all-start.4 = ((bf16[8,96,1024]{2,1,0:T(8,128)(2,1)}), bf16[8,96,1024]{2,1,0:T(8,128)(2,1)}, u32[]{:S(2)}, u32[]{:S(2)}) async-start(bf16[8,96,1024]{2,1,0:T(8,128)(2,1)} %bitcast.179), calls=%async_computation.4 | async-start | bytes 3145728 | tf_op jit(solution)/shard_map/all_to_all | solution.py:1045
  426.3 49.2 %collective-permute-start.9 = (bf16[512,1024]{1,0:T(8,128)(2,1)}, bf16[512,1024]{1,0:T(8,128)(2,1)}, u32[]{:S(2)}, u32[]{:S(2)}) collective-permute-start(bf16[512,1024]{1,0:T(8,128)(2,1)} %fusion.35), channel_id=1, source_target_pairs={{0,16},{8,24},{16,0},{24,8},{1,17},{9,25},{17,1},{25,9},{2,18},{10... | collective-permute-start | bytes 3145736 | tf_op jit(solution)/shard_map/ppermute | solution.py:64
  440.9 41.5 %all-to-all-start.5 = ((bf16[8,192,1024]{2,1,0:T(8,128)(2,1)}), bf16[8,192,1024]{2,1,0:T(8,128)(2,1)S(1)}, u32[]{:S(2)}, u32[]{:S(2)}) async-start(bf16[8,192,1024]{2,1,0:T(8,128)(2,1)} %pad_maximum_fusion.1), calls=%async_computation.5 | async-start | bytes 6291456 | tf_op jit(solution)/shard_map/all_to_all | solution.py:1045
  459.8 60.6 %collective-permute-start.10 = (bf16[1024,1024]{1,0:T(8,128)(2,1)}, bf16[1024,1024]{1,0:T(8,128)(2,1)}, u32[]{:S(2)}, u32[]{:S(2)}) collective-permute-start(bf16[1024,1024]{1,0:T(8,128)(2,1)} %fusion.25), channel_id=1, source_target_pairs={{0,8},{8,0},{16,24},{24,16},{1,9},{9,1},{17,25},{25,17},{2,10},{10... | collective-permute-start | bytes 6291464 | tf_op jit(solution)/shard_map/ppermute | solution.py:69
  521.3 20.2 %collective-permute-start.11 = (bf16[2,256,256]{2,1,0:T(8,128)(2,1)}, bf16[2,256,256]{2,1,0:T(8,128)(2,1)}, u32[]{:S(2)}, u32[]{:S(2)}) collective-permute-start(bf16[2,256,256]{2,1,0:T(8,128)(2,1)} %get-tuple-element.227), channel_id=1, source_target_pairs={{0,8},{8,16},{16,24},{24,0},{1,9},{9,17},{17,25},{25,1},{2,10},{10... | collective-permute-start | bytes 786440 | tf_op jit(solution)/shard_map/ppermute | solution.py:64
  534.7 124.9 %collective-permute-start.19 = (bf16[4,2,2,128,1024]{4,3,2,1,0:T(8,128)(2,1)}, bf16[4,2,2,128,1024]{4,3,2,1,0:T(8,128)(2,1)}, u32[]{:S(2)}, u32[]{:S(2)}) collective-permute-start(bf16[4,2,2,128,1024]{4,3,2,1,0:T(8,128)(2,1)} %dynamic-slice_bitcast_fusion), channel_id=1, source_target_pairs={{0,1},{1,0},{2,3},{3,2},{4,5},{5,4},{6,7},{7,6},{8,9},{9,8},{10,11... | collective-permute-start | bytes 12582920 | tf_op jit(solution)/shard_map/ppermute | solution.py:226
  541.6 15.5 %collective-permute-start.12 = (bf16[2,256,256]{2,1,0:T(8,128)(2,1)S(1)}, bf16[2,256,256]{2,1,0:T(8,128)(2,1)S(1)}, u32[]{:S(2)}, u32[]{:S(2)}) collective-permute-start(bf16[2,256,256]{2,1,0:T(8,128)(2,1)S(1)} %copy-done.41), channel_id=1, source_target_pairs={{0,16},{8,24},{16,0},{24,8},{1,17},{9,25},{17,1},{25,9},{2,18},{10... | collective-permute-start | bytes 786440 | tf_op jit(solution)/shard_map/ppermute | solution.py:64
  566.1 38.0 %collective-permute-start.14 = (bf16[512,1024]{1,0:T(8,128)(2,1)}, bf16[512,1024]{1,0:T(8,128)(2,1)}, u32[]{:S(2)}, u32[]{:S(2)}) collective-permute-start(bf16[512,1024]{1,0:T(8,128)(2,1)} %get-tuple-element.173), channel_id=1, source_target_pairs={{0,8},{8,0},{16,24},{24,16},{1,9},{9,1},{17,25},{25,17},{2,10},{10... | collective-permute-start | bytes 3145736 | tf_op jit(solution)/shard_map/ppermute | solution.py:69
  568.5 91.1 %collective-permute-start.18 = (bf16[4,2,2,32,4096]{4,3,2,1,0:T(8,128)(2,1)}, bf16[4,2,2,32,4096]{4,3,2,1,0:T(8,128)(2,1)}, u32[]{:S(2)}, u32[]{:S(2)}) collective-permute-start(bf16[4,2,2,32,4096]{4,3,2,1,0:T(8,128)(2,1)} %dynamic-slice_bitcast_fusion.1), channel_id=1, source_target_pairs={{0,1},{1,0},{2,3},{3,2},{4,5},{5,4},{6,7},{7,6},{8,9},{9,8},{10,11... | collective-permute-start | bytes 12582920 | tf_op jit(solution)/shard_map/ppermute | solution.py:226
  573.1 31.0 %collective-permute-start.15 = (bf16[256,1024]{1,0:T(8,128)(2,1)}, bf16[256,1024]{1,0:T(8,128)(2,1)}, u32[]{:S(2)}, u32[]{:S(2)}) collective-permute-start(bf16[256,1024]{1,0:T(8,128)(2,1)} %get-tuple-element.174), channel_id=1, source_target_pairs={{0,16},{8,24},{16,0},{24,8},{1,17},{9,25},{17,1},{25,9},{2,18},{10... | collective-permute-start | bytes 1572872 | tf_op jit(solution)/shard_map/ppermute | solution.py:64
  616.2 36.6 %collective-permute-start.16 = (bf16[512,1024]{1,0:T(8,128)(2,1)}, bf16[512,1024]{1,0:T(8,128)(2,1)S(1)}, u32[]{:S(2)}, u32[]{:S(2)}) collective-permute-start(bf16[512,1024]{1,0:T(8,128)(2,1)} %get-tuple-element.181), channel_id=1, source_target_pairs={{0,8},{8,0},{16,24},{24,16},{1,9},{9,1},{17,25},{25,17},{2,10},{10... | collective-permute-start | bytes 3145736 | tf_op jit(solution)/shard_map/ppermute | solution.py:69
  624.7 26.0 %collective-permute-start.17 = (bf16[256,1024]{1,0:T(8,128)(2,1)}, bf16[256,1024]{1,0:T(8,128)(2,1)S(1)}, u32[]{:S(2)}, u32[]{:S(2)}) collective-permute-start(bf16[256,1024]{1,0:T(8,128)(2,1)} %get-tuple-element.182), channel_id=1, source_target_pairs={{0,16},{8,24},{16,0},{24,8},{1,17},{9,25},{17,1},{25,9},{2,18},{10... | collective-permute-start | bytes 1572872 | tf_op jit(solution)/shard_map/ppermute | solution.py:64
  (61 other events, 879.3 us)

commit v4 on v3

--- a/solution.py
+++ b/solution.py
@@ -243,6 +243,36 @@
     return term.astype(BF).reshape(seq_size, fsdp_size, *tile)
 
 
+def project_kernel(x_ref, gains_ref, biases_ref, w_ref, normed_ref, out_ref):
+    x = x_ref[...].astype(F32)
+    average, scale = norm_parts(x)
+    normed = ((x - average) * scale * gains_ref[0:1] + biases_ref[0:1]).astype(BF)
+    normed_ref[...] = normed
+    out_ref[...] = mm(normed, w_ref[...].reshape(x.shape[1], w_ref.shape[-1])).astype(BF)
+
+
+def project(inputs_all, gains, biases, weights, columns, tokens):
+    width = inputs_all.shape[1]
+    row = pl.BlockSpec((8, width), lambda i: (0, 0))
+    return pl.pallas_call(
+        project_kernel,
+        grid=(inputs_all.shape[0] // tokens,),
+        in_specs=[
+            pl.BlockSpec((tokens, width), lambda i: (i, 0)),
+            row,
+            row,
+            pl.BlockSpec((*weights.shape[:3], columns), lambda i: (0, 0, 0, 0)),
+        ],
+        out_specs=[pl.BlockSpec((tokens, width), lambda i: (i, 0)), pl.BlockSpec((tokens, columns), lambda i: (i, 0))],
+        out_shape=[
+            jax.ShapeDtypeStruct(inputs_all.shape, BF),
+            jax.ShapeDtypeStruct((inputs_all.shape[0], columns), BF),
+        ],
+        compiler_params=pltpu.CompilerParams(vmem_limit_bytes=40 * 2**20),
+        cost_estimate=pl.CostEstimate(flops=10**6, bytes_accessed=2**16, transcendentals=0),
+    )(inputs_all, gains, biases, weights)
+
+
 def ffn_kernel(middle_ref, gains_ref, biases_ref, win_ref, wout_ref, normed_ref, act_ref, slope_ref, block_ref, routed_ref):
     chunk = pl.program_id(0)
 
@@ -347,6 +377,7 @@
 
 def expert_kernel(x_ref, dr_ref, centroid_ref, win_own, wout_own, win_low, win_high, wout_low, wout_high, *refs):
     act_ref, du_ref, dz_ref, all_ref, gated_ref, dx_ref, term_ref, total, back, win_ref, wout_ref = refs[-11:]
+    groups_of = gated_ref.shape
     chunk = pl.program_id(0)
     own = pl.num_programs(0) - 2
     for here, win_part, wout_part in (
@@ -385,13 +416,13 @@
     def _():
         gate = gate_of()
         result = total[...]
-        gated_ref[...] = (gate * result).astype(BF)
+        gated_ref[...] = (gate * result).astype(BF).reshape(groups_of)
         dl = jnp.sum(dr_ref[...].astype(F32) * result, axis=1, keepdims=True) * gate * (1.0 - gate)
         dx_ref[...] = (back[...] + dl * centroid_ref[:1].astype(F32)).astype(BF)
         term_ref[...] = jnp.broadcast_to(jnp.sum(dl * x.astype(F32), axis=0, keepdims=True), term_ref.shape)
 
 
-def expert_block(group, groups, arrived, grads, centroid, weights, earlier):
+def expert_block(group, groups, blocks, arrived, grads, centroid, weights, earlier):
     slots, width = arrived.shape
     size = weights[2].shape[1]
     own = weights[0].shape[1] // size
@@ -418,10 +449,19 @@
             wout_piece,
             *[pl.BlockSpec(memory_space=pl.ANY)] * len(earlier),
         ],
-        out_specs=[piece, piece, shared, shared, whole, whole, term],
+        out_specs=[
+            piece,
+            piece,
+            shared,
+            shared,
+            pl.BlockSpec((blocks, slots // blocks, width), lambda j: (0, group, 0)),
+            whole,
+            term,
+        ],
         out_shape=[jax.ShapeDtypeStruct((groups * slots, hidden), BF)] * 2
         + [jax.ShapeDtypeStruct((groups * slots, width), BF)] * 2
-        + [jax.ShapeDtypeStruct((slots, width), BF)] * 2
+        + [jax.ShapeDtypeStruct((blocks, groups * slots // blocks, width), BF)]
+        + [jax.ShapeDtypeStruct((slots, width), BF)]
         + [jax.ShapeDtypeStruct((8, width), F32)],
         scratch_shapes=[pltpu.VMEM((slots, width), F32)] * 2
         + [pltpu.VMEM((width, size), BF), pltpu.VMEM((size, width), BF)],
@@ -692,24 +732,25 @@
 
 def finish_plan(seq_size, count):
     last = count - 1
-    plan = [("send", 0), ("open",), ("arrive", 0, 1)]
-    ffn = [("add", index, step) for step in range(1, count) for index in (0, 1)]
-    for hop in range(2, seq_size):
-        plan += [("arrive", 0, hop)]
-        share = len(ffn) - 2 if hop == seq_size - 2 else 0
-        plan += ffn[:share]
-        ffn = ffn[share:]
-        if hop == seq_size - 2:
-            plan += [("add", 2, 0), ("add", 3, 0)]
-    if seq_size == 2:
-        plan += [("add", 2, 0), ("add", 3, 0)]
-    for item in ffn:
-        plan += [item] + ([("send", 1 + item[1])] if item[2] == last else [])
-    rest = [("add", index, step) for step in range(1, count) for index in (2, 3)] + [("proj",)]
+    steps = [[("add", 2 * row + i, step) for i in (0, 1)] for row in range(seq_size) for step in range(1, count)]
+    steps.sort(key=lambda pair: (pair[0][1] // 2 + 1.2 * pair[0][2], pair[0][2]))
+    ffn = [item for pair in steps for item in pair]
+    halves = [2 * seq_size, 2 * seq_size + 1]
+    proj = [("add", k, step) for step in range(count) for k in halves]
+    plan = [("send", 0), ("open",)]
+    share = -(-len(ffn) // (seq_size - 1))
     for hop in range(1, seq_size):
-        share = -(-len(rest) // (seq_size - hop))
-        plan += [("arrive", 1, hop), ("arrive", 2, hop), *rest[:share]]
-        rest = rest[share:]
+        chunk, ffn = ffn[:share], ffn[share:]
+        if hop == seq_size - 1:
+            plan += proj[:2]
+            proj = proj[2:]
+        plan += chunk[: share // 3] + [("arrive", 0, hop)] + chunk[share // 3 :]
+    plan += [("send", 1), ("send", 2)]
+    proj += [("proj",)]
+    share = -(-len(proj) // (seq_size - 1))
+    for hop in range(1, seq_size):
+        plan += [*proj[:share], ("arrive", 1, hop), ("arrive", 2, hop)]
+        proj = proj[share:]
     return plan + [("total", 0), ("total", 1), ("total", 2)]
 
 
@@ -808,25 +849,22 @@
     plain = bits[::-1]
     turned = plain[:1] + plain[:0:-1]
     some = seq_size // 2
-    cubes = (
-        ([in_ref, *in_parts], plain, None),
-        ([out_ref, *out_parts], turned, None),
-        ([proj_ref, *proj_parts], plain, 0),
-        ([proj_ref, *proj_parts], turned, some),
-    )
+    cubes = []
+    for row in range(seq_size):
+        cubes += [([in_ref, *in_parts], plain, row, 1), ([out_ref, *out_parts], turned, row, 1)]
+    cubes += [([proj_ref, *proj_parts], plain, 0, some), ([proj_ref, *proj_parts], turned, some, seq_size - some)]
 
     def half_of(index, step, kept):
-        states, order, _ = cubes[index]
+        states, order = cubes[index][:2]
         where = 1 + sorted(order[step:], reverse=True).index(order[step])
         return states[step], where, bit_of[order[step]] if kept else 1 - bit_of[order[step]]
 
     def rows_of(index):
-        offset = cubes[index][2]
-        return slice(None) if offset is None else pl.ds(offset, some)
+        return pl.ds(cubes[index][2], cubes[index][3])
 
     def cube(index, step):
         source, where, bit = half_of(index, step, False)
-        states, order, _ = cubes[index]
+        states, order = cubes[index][:2]
         return pltpu.make_async_remote_copy(
             src_ref=source.at[(rows_of(index),) + (slice(None),) * (where - 1) + (bit,)],
             dst_ref=states[step + 1].at[rows_of(index)],
@@ -838,29 +876,27 @@
 
     def cube_add(index, step):
         source, where, bit = half_of(index, step, True)
-        states, _, offset = cubes[index]
+        states, _, offset, length = cubes[index]
         cube(index, step).wait()
-        for i in range(seq_size if offset is None else some):
-            row = i + (offset or 0)
+        for row in range(offset, offset + length):
             add_into(states[step + 1], (row,), lambda at, row=row: source[(row, *at[: where - 1], bit, *at[where - 1 :])])
         if step + 1 < count:
             cube(index, step + 1).start()
 
     def keep(index):
         source, where, bit = half_of(index, 0, True)
-        return pltpu.make_async_copy(
-            source.at[(slice(None),) * where + (bit,)], cubes[index][0][1], keep_sem.at[index]
-        )
+        view = source.at[(rows_of(index),) + (slice(None),) * (where - 1) + (bit,)]
+        return pltpu.make_async_copy(view, cubes[index][0][1].at[rows_of(index)], keep_sem.at[index])
 
     def open_cubes():
-        for index in (2, 3):
+        for index in range(2 * seq_size):
+            keep(index).start()
+        for index in (2 * seq_size, 2 * seq_size + 1):
             cube(index, 0).start()
-        for index in (0, 1):
-            keep(index).start()
-        for index, added in ((0, in_added), (1, out_added)):
+        for index in range(2 * seq_size):
+            row, added = index // 2, (in_added, out_added)[index % 2]
             keep(index).wait()
-            for row in range(seq_size):
-                add_into(cubes[index][0][1], (row,), lambda at, row=row: added[(row, *at)])
+            add_into(cubes[index][0][1], (row,), lambda at, row=row, added=added: added[(row, *at)])
             cube(index, 1).start()
 
     def proj(step):
@@ -930,11 +966,11 @@
             *parts_of(shapes[2], 1),
             *parts_of(proj.shape[-2:], 1),
             dma,
-            dma((2,)),
+            dma((2 * seq_size,)),
             dma((3, 2, seq_size - 1)),
             dma((3, 2, seq_size - 1)),
-            dma((4, count)),
-            dma((4, count)),
+            dma((2 * seq_size + 2, count)),
+            dma((2 * seq_size + 2, count)),
             dma((seq_size - 1,)),
             dma((seq_size - 1,)),
         ],
@@ -983,25 +1019,27 @@
     id_rows, id_cols = doc_ids[:, None, :], doc_ids[:, :, None]
 
     depth = out_proj.shape[0]
-    wide = 3 * cols + width
+    wide = 3 * cols + width + LANES
     slices = qkv_proj.reshape(3, depth, seq_size, cols).transpose(2, 1, 0, 3).reshape(seq_size, depth, 3 * cols)
-    slices = jnp.concatenate([slices, jnp.broadcast_to(out_proj[None], (seq_size, depth, width))], axis=2)
-    small = jnp.concatenate([norm_gains.reshape(-1), norm_biases.reshape(-1), centroids[0]])
-    spare = 16 - depth % 16
-    extra = jnp.stack([jnp.pad(v, (0, wide - v.shape[0])) for v in (small, routes.reshape(tokens).astype(BF))])
-    extra = jnp.pad(extra, ((0, spare - 2), (0, 0)))[None]
-    extra = jnp.broadcast_to(extra, (seq_size, spare, wide))
+    small = jnp.concatenate(
+        [norm_gains.reshape(-1), norm_biases.reshape(-1), centroids[0], routes.reshape(tokens).astype(BF)]
+    )
+    small = jnp.pad(small, (0, depth * LANES - small.shape[0])).reshape(depth, LANES)
+    slices = jnp.concatenate(
+        [slices, *[jnp.broadcast_to(v[None], (seq_size, *v.shape)) for v in (out_proj, small)]], axis=2
+    )
+    spare = -depth % 16
     bits = fsdp_bits(False)
     crossed = fsdp_bits(True)
     tokens_in = inputs.reshape(tokens, width)
     proj_all, ffin_all, ffout_all, inputs_all = start_gathers(
-        jnp.concatenate([slices, extra], axis=1), whole_tiles(ffn_in), whole_tiles(ffn_out), tokens_in
+        jnp.pad(slices, ((0, 0), (0, spare), (0, 0))), whole_tiles(ffn_in), whole_tiles(ffn_out), tokens_in
     )
     inputs_all = inputs_all.reshape(seq_size * tokens, width)
     ffin_all, ffout_all = ffin_all.reshape(width, -1), ffout_all.reshape(-1, width)
     qkv_mine = proj_all[:, :, :depth, : 3 * cols].reshape(width, 3 * cols)
-    out_all = proj_all[:, :, :depth, 3 * cols :].reshape(width, width)
-    small = proj_all[:, :, depth, :]
+    out_all = proj_all[:, :, :depth, 3 * cols : 3 * cols + width].reshape(width, width)
+    small = proj_all[:, :, :depth, 3 * cols + width :].reshape(seq_size, fsdp_size, -1)
     rows_of = small[:, :, : 6 * depth].astype(F32).reshape(-1, 6, depth).transpose(1, 0, 2).reshape(6, width)
     gain_rows, bias_rows = rows_of[:3], rows_of[3:]
     mine = small[:, :, 6 * depth : 6 * depth + cols]
@@ -1009,23 +1047,15 @@
     inputs_all, win_mine, wout_mine, dr_mine = tie(
         inputs_all, expert_in[0], expert_out[0], out_grad.reshape(tokens, width)
     )
-    parts_all = norm_parts(inputs_all.astype(F32))
-    normed_flat = ((inputs_all.astype(F32) - parts_all[0]) * parts_all[1] * gain_rows[0] + bias_rows[0]).astype(BF)
-    projected = mm(normed_flat, qkv_mine).astype(BF).reshape(seq_size, rows, span, 3 * cols)
+    gains_pad, biases_pad = jnp.pad(gain_rows, ((0, 5), (0, 0))), jnp.pad(bias_rows, ((0, 5), (0, 0)))
+    proj_used = proj_all if spare == 0 else proj_all[:, :, :depth, : 3 * cols]
+    normed_flat, projected = project(inputs_all, gains_pad, biases_pad, proj_used, 3 * cols, tokens)
+    projected = projected.reshape(seq_size, rows, span, 3 * cols)
 
     attended_mine, lse_rows = attend(projected, id_rows, id_cols)
-    win_half, wout_half = win_mine.shape[1] // 2, wout_mine.shape[0] // 2
-    pair_in_low = seq_pair(win_mine[:, :win_half])
-    grad_moved = [seq_shift(dr_mine, 2 * group) for group in range(1, groups)]
-    attended_mine, pair_in_low, *grad_moved = tie(attended_mine, pair_in_low, *grad_moved)
-    attended = seq_exchange(attended_mine).transpose(1, 2, 0, 3).reshape(tokens, width)
-    attended, pair_in_high, pair_out_low, wout_high = tie(
-        attended, win_mine[:, win_half:], wout_mine[:wout_half], wout_mine[wout_half:]
-    )
-    pair_in_high, pair_out_low = seq_pair(pair_in_high), seq_pair(pair_out_low)
-
     fsdp_here = lax.axis_index("fsdp")
-    routes_all = lax.dynamic_index_in_dim(proj_all[:, :, depth + 1, :tokens], fsdp_here, 1, keepdims=False)
+    routes_all = small[:, :, 6 * depth + cols : 6 * depth + cols + tokens]
+    routes_all = lax.dynamic_index_in_dim(routes_all, fsdp_here, 1, keepdims=False)
     later = (jnp.arange(tokens)[:, None] > jnp.arange(tokens)[None, :]).astype(BF)
     placings = []
     for group in range(groups):
@@ -1047,40 +1077,53 @@
     def tokens_of(placing, values):
         return mm(placing, values.reshape(fsdp_size * capacity, width))
 
+    win_half, wout_half = win_mine.shape[1] // 2, wout_mine.shape[0] // 2
+    pair_in_low = seq_pair(win_mine[:, :win_half])
+    grad_moved = [seq_shift(dr_mine, 2 * group) for group in range(1, groups)]
     grad_slots = [slots_of(placings[group], ([grad_tokens] + grad_moved)[group]) for group in range(groups)]
-    grad_slots = swap_slots(jnp.concatenate(grad_slots, axis=1)).reshape(fsdp_size, groups, capacity, width)
-    grad_slots = [grad_slots[:, group].reshape(-1, width) for group in range(groups)]
-
+    grad_slots = jnp.concatenate(grad_slots, axis=1)
+    attended_mine, pair_in_low, grad_slots = tie(attended_mine, pair_in_low, grad_slots)
+    grad_slots = swap_slots(grad_slots)
+    attended = seq_exchange(attended_mine)
+    attended = attended.transpose(1, 2, 0, 3).reshape(tokens, width)
+    attended, pair_in_high, pair_out_low, wout_high = tie(
+        attended, win_mine[:, win_half:], wout_mine[:wout_half], wout_mine[wout_half:]
+    )
+    pair_in_high, pair_out_low = seq_pair(pair_in_high), seq_pair(pair_out_low)
 
     resid_in = tokens_in.astype(F32)
     middle = resid_in + mm(attended, out_all)
-    gains_pad, biases_pad = jnp.pad(gain_rows, ((0, 5), (0, 0))), jnp.pad(bias_rows, ((0, 5), (0, 0)))
     hidden_low, active_low, active_slope, block_out, routed = ffn_forward(
         middle, gains_pad, biases_pad, ffin_all, ffout_all
     )
-    routed, wout_high, pair_in_high, pair_out_low, *grad_slots = tie(
-        routed, wout_high, pair_in_high, pair_out_low, *grad_slots
-    )
+    routed, wout_high, pair_in_high, pair_out_low, grad_slots = tie(
+        routed, wout_high, pair_in_high, pair_out_low, grad_slots
+    )
+    grad_slots = grad_slots.reshape(fsdp_size, groups, capacity, width)
+    grad_slots = [grad_slots[:, group].reshape(-1, width) for group in range(groups)]
     slots_own = slots_of(placings[0], routed)
     pair_out_high = seq_pair(wout_high)
+
+    own_mean, own_scale = norm_parts(resid_in)
 
     arrived = [swap_slots(slots_own).reshape(-1, width)]
     for group in range(1, groups):
         routed_here = seq_shift(routed, 2 * group)
-        routed_here, pair_out_high = tie(routed_here, pair_out_high)
+        routed_here, pair_out_high, qkv_mine, own_mean, own_scale, *grad_slots = tie(
+            routed_here, pair_out_high, qkv_mine, own_mean, own_scale, *grad_slots
+        )
         slots_here = slots_of(placings[group], routed_here)
         slots_here, pair_out_high, *arrived = tie(slots_here, pair_out_high, *arrived)
         arrived.append(swap_slots(slots_here).reshape(-1, width))
     weights = (win_mine, wout_mine, pair_in_low, pair_in_high, pair_out_low, pair_out_high)
-    shared, gateds, rows_grads, terms = (), [], [], []
+    shared, rows_grads, terms = (), [], []
     for group in range(groups):
-        *shared, gated, rows_grad, term = expert_block(
-            group, groups, arrived[group], grad_slots[group], centroid, weights, shared
+        *shared, rows_grad, term = expert_block(
+            group, groups, fsdp_size, arrived[group], grad_slots[group], centroid, weights, shared
         )
-        gateds.append(gated)
         rows_grads.append(rows_grad)
         terms.append(term)
-    act, du, dz, arrived = shared
+    act, du, dz, arrived, gated_all = shared
 
     half = expert_in.shape[2]
     in_sent = mm_tn(arrived, du[:, half:]).astype(BF)
@@ -1096,7 +1139,6 @@
         if group:
             back_low[group] = back_low[group].astype(BF)
     in_pair = seq_pair(in_sent)
-    gated_all = jnp.concatenate([gated.reshape(fsdp_size, capacity, width) for gated in gateds], axis=1)
     if groups > 1:
         gated_all, arrived, act, du, back_low[-1] = tie(gated_all, arrived, act, du, back_low[-1])
     back_sum = back_low[0]
@@ -1109,9 +1151,8 @@
 
     gated_back = swap_slots(gated_all).reshape(fsdp_size, groups, capacity, width)
     out_terms = [tokens_of(placings[group], gated_back[:, group]) for group in range(groups)]
-    back_sum, out_sent, in_kept, out_kept, *out_terms = tie(
-        back_sum, out_sent, in_kept, out_kept, out_terms[0], *(v.astype(BF) for v in out_terms[1:])
-    )
+    out_terms = out_terms[:1] + [v.astype(BF) for v in out_terms[1:]]
+    back_sum, out_sent, in_kept, out_kept = tie(back_sum, out_sent, in_kept, out_kept)
 
     block_low, hidden_grad, middle_grad, branch, dense_rows = ffn_backward(
         back_sum, block_out, grad_tokens, middle, gains_pad, active_slope, ffin_all, ffout_all
@@ -1130,40 +1171,56 @@
         return terms, fsdp_flip(sent, 1)
 
     ffout_terms = halved(mm_tn(active_low, block_low))
-    ffin_terms = halved(mm_tn(hidden_low, hidden_grad))
+    ffin_terms = mm_tn(hidden_low, hidden_grad).astype(BF)
     proj_terms = mm_tn(attended, branch).astype(BF).reshape(seq_size, fsdp_size, depth, width)
-    proj_terms = jnp.pad(proj_terms, ((0, 0), (0, 0), (0, spare), (3 * cols, 0)))
-    def halves(values):
-        return values[: values.shape[0] // 2], values[values.shape[0] // 2 :]
-
-    out_halves = [halves(values) for values in [out_sent, *out_terms[1:]]]
-    attended_grad, *out_first = tie(attended_grad, *[first for first, _ in out_halves])
-    out_first = [seq_pair(out_first[0])] + [seq_shift(out_first[group], -2 * group) for group in range(1, groups)]
+    def split(values):
+        size = values.shape[0] // 4
+        return values[: 2 * size], values[2 * size : 3 * size], values[3 * size :]
+
+    def send_pieces(pieces):
+        return [seq_pair(pieces[0])] + [seq_shift(pieces[group], -2 * group) for group in range(1, groups)]
+
+    out_pieces = [split(values) for values in [out_sent, *out_terms[1:]]]
+    sizes = len(out_pieces)
+    attended_grad, *out_first = tie(attended_grad, *[pieces[0] for pieces in out_pieces])
+    out_first = send_pieces(out_first)
 
     dq, dk, dv = attend_back(projected, attended_grad, lse_rows, id_rows, id_cols)
     projected_grad = jnp.concatenate([dq, dk, dv], axis=-1).reshape(seq_size * tokens, 3 * cols)
-    sizes = len(out_first)
-    projected_grad, *moved = tie(projected_grad, *out_first, *[second for _, second in out_halves])
-    out_first, out_second = moved[:sizes], moved[sizes:]
-    out_second = [seq_pair(out_second[0])] + [seq_shift(out_second[group], -2 * group) for group in range(1, groups)]
+    projected_grad, inputs_all, in_kept, out_kept, proj_terms, ffin_terms, *moved = tie(
+        projected_grad,
+        inputs_all,
+        in_kept,
+        out_kept,
+        proj_terms,
+        ffin_terms,
+        *out_first,
+        *[pieces[1] for pieces in out_pieces],
+    )
+    ffin_terms = halved(ffin_terms)
+    proj_terms = jnp.pad(proj_terms, ((0, 0), (0, 0), (0, spare), (3 * cols, LANES)))
+    out_first, out_second = moved[:sizes], send_pieces(moved[sizes:])
     normed_low_terms = mm_nt(projected_grad, qkv_mine).astype(BF)
+    parts_all = norm_parts(inputs_all.astype(F32))
     unit_all = (inputs_all.astype(F32) - parts_all[0]) * parts_all[1]
     terms_wide = normed_low_terms.astype(F32)
     gain_one, bias_one = jnp.sum(terms_wide * unit_all, axis=0), jnp.sum(terms_wide, axis=0)
     small_terms = jnp.stack([gain_one, gain_two, gain_three, bias_one, bias_two, bias_three])
 
     qkv_term = mm_tn(normed_flat, projected_grad).astype(BF).reshape(seq_size, fsdp_size, depth, 3 * cols)
+    qkv_term, *moved = tie(qkv_term, *out_second, *[pieces[2] for pieces in out_pieces])
+    out_second, out_third = moved[:sizes], send_pieces(moved[sizes:])
     small_rows = small_terms.astype(BF).reshape(6, seq_size, fsdp_size, depth).transpose(1, 2, 0, 3)
-    small_rows = small_rows.reshape(seq_size, fsdp_size, 1, 6 * depth)
-    small_rows = jnp.pad(small_rows, ((0, 0), (0, 0), (0, spare - 1), (0, wide - 6 * depth)))
     centroid_rows = jnp.where(
         (jnp.arange(fsdp_size) == fsdp_here)[None, :, None], centroid_term.reshape(seq_size, 1, cols), 0.0
     )
-    small_rows = lax.dynamic_update_slice(small_rows, centroid_rows.astype(BF)[:, :, None], (0, 0, 1, 0))
+    small_rows = jnp.concatenate([small_rows.reshape(seq_size, fsdp_size, 6 * depth), centroid_rows.astype(BF)], axis=2)
+    small_rows = jnp.pad(small_rows, ((0, 0), (0, 0), (0, depth * LANES - small_rows.shape[2])))
+    small_rows = small_rows.reshape(seq_size, fsdp_size, depth, LANES)
     proj_terms = lax.dynamic_update_slice(proj_terms, qkv_term, (0, 0, 0, 0))
-    proj_terms = hyper_split(lax.dynamic_update_slice(proj_terms, small_rows, (0, 0, depth, 0)))
-    proj_terms, *out_second = tie(proj_terms, *out_second)
-    out_pair, *out_moved = [jnp.concatenate(v, axis=0) for v in zip(out_first, out_second, strict=True)]
+    proj_terms = hyper_split(lax.dynamic_update_slice(proj_terms, small_rows, (0, 0, 0, 3 * cols + width)))
+    proj_terms, *out_third = tie(proj_terms, *out_third)
+    out_pair, *out_moved = [jnp.concatenate(v, axis=0) for v in zip(out_first, out_second, out_third, strict=True)]
     outputs = block_out + out_terms[0] + sum(v.astype(F32) for v in out_moved)
     outputs = outputs.astype(BF).reshape(rows, span, width)
     normed_one_grad, ffn_in_grad, ffn_out_grad, proj_sums = finish_sums(
@@ -1173,14 +1230,15 @@
     proj_sums = proj_sums.astype(F32)
     qkv_grad = proj_sums[:, :depth, : 3 * cols].reshape(seq_size, depth, 3, cols)
     qkv_grad = qkv_grad.transpose(2, 1, 0, 3).reshape(qkv_proj.shape)
-    out_proj_grad = jnp.sum(proj_sums[:, :depth, 3 * cols :], axis=0)
-    small_grad = jnp.sum(proj_sums[:, depth, : 6 * depth], axis=0).reshape(6, depth)
-    centroids_grad = jnp.sum(proj_sums[:, depth + 1, :cols], axis=0)[None]
+    out_proj_grad = jnp.sum(proj_sums[:, :depth, 3 * cols : 3 * cols + width], axis=0)
+    small = jnp.sum(proj_sums[:, :depth, 3 * cols + width :], axis=0).reshape(-1)
+    small_grad = small[: 6 * depth].reshape(6, depth)
+    centroids_grad = small[6 * depth : 6 * depth + cols][None]
 
     expert_in_grad = (in_kept + in_pair.astype(F32))[None]
     expert_out_grad = (out_kept + out_pair.astype(F32))[None]
 
-    input_norm_grad, _, _ = norm_back(resid_in, norm_parts(resid_in), gain_rows[0], normed_one_grad)
+    input_norm_grad, _, _ = norm_back(resid_in, (own_mean, own_scale), gain_rows[0], normed_one_grad)
     input_grad = (middle_grad + input_norm_grad).reshape(rows, span, width)
     return (
         outputs,

time: 817 us -> 789 us (0.966)
  waiting for transfers between devices: 161 us -> 136 us
  matrix products: 90.3 us -> 78.3 us
  other arithmetic: 38.7 us -> 28.6 us
  local copies, waits for them, and re-layouts: 70.5 us -> 80.3 us
    all_to_all x6, waiting for transfers between devices: 30.1 us -> 12.2 us  [swap_slots(): lax.all_to_all(values, 'fsdp', split_axis=0, concat_axis=0, tiled=True)]
    ppermute x11 -> x12, waiting for transfers between devices: 110 us -> 93.6 us  [seq_shift(): lax.ppermute(values, 'seq', [(i, (i + step) % size) for i in range(size)])]
    dot_general x8 -> x7, matrix products: 23.8 us -> 13.7 us  [mm(): return jnp.dot(left, right, preferred_element_type=F32)]
    ppermute x7 -> x8, waiting for transfers between devices: 21 us -> 30.1 us  [seq_pair(): return lax.ppermute(values, 'seq', [(i, i ^ 1) for i in range(size)])]
    ppermute x11 -> x12, starting transfers between devices: 24.5 us -> 18.9 us  [seq_shift(): lax.ppermute(values, 'seq', [(i, (i + step) % size) for i in range(size)])]
    unnamed x131 -> x152, local copies, waits for them, and re-layouts: 19.4 us -> 24.5 us
  transfers between devices with their start and end apart: 26 -> 28, of which waited for: 15 -> 17; matrix products, arithmetic and copies ran while one was open for 18% -> 17% of each run, Pallas kernels for 13% -> 14%
where the time goes in v4:
time: 789 us; the launch traced here: 778 us
  Pallas kernels  395 us (50%)
  waiting for transfers between devices  136 us (17%)
  local copies, waits for them, and re-layouts  80.3 us (10%)
  matrix products  78.3 us (10%)
  starting transfers between devices  57.7 us (7%)
  other arithmetic  28.6 us (4%)
    pallas_call x1, Pallas kernels, finish_sums(): pl.pallas_call(functools.partial(finish_kernel, seq_size, bits), in_specs...  138 us
    pallas_call x1, Pallas kernels, start_gathers(): pl.pallas_call(functools.partial(gather_kernel, seq_size, bits), in_specs...  123 us
    ppermute x12, waiting for transfers between devices, seq_shift(): lax.ppermute(values, 'seq', [(i, (i + step) % size) for i in range(size)])  93.6 us
    dot_general x12, matrix products, mm_tn(): lax.dot_general(left, right, (((0,), (0,)), ((), ())), preferred_element_...  56.9 us
    pallas_call x2, Pallas kernels, expert_block(): pl.pallas_call(expert_kernel, grid=(own + 2,), in_specs=[whole, whole, ro...  46.4 us
    ppermute x8, waiting for transfers between devices, seq_pair(): return lax.ppermute(values, 'seq', [(i, i ^ 1) for i in range(size)])  30.1 us
    all_to_all x6, starting transfers between devices, swap_slots(): lax.all_to_all(values, 'fsdp', split_axis=0, concat_axis=0, tiled=True)  27.2 us
    unnamed x152, local copies, waits for them, and re-layouts  24.5 us
  transfers between devices with their start and end apart: 28, of which 17 were waited for; matrix products, arithmetic and copies ran while one was open for 17% of the time, Pallas kernels for 14%

profile of v4, /device:TPU:0, one launch (start us, length us, event | category | flops | bytes accessed | tf_op | source)
XLA Modules:
  0.0 778.1 jit_solution(1863032210590012056)
XLA Ops:
  10.2 123.1 %shard_map.212 = (bf16[4,2,2,2,32,1920]{5,4,3,2,1,0:T(8,128)(2,1)}, bf16[4,2,2,2,32,4096]{5,4,3,2,1,0:T(8,128)(2,1)}, bf16[4,2,2,2,128,1024]{5,4,3,2,1,0:T(8,128)(2,1)}, bf16[4,512,1024]{2,1,0:T(8,128)(2,1)}) custom-call(bf16[4,32,1920]{2,1,0:T(8,128)(2,1)} %pad_maximum_fusion.2.proj_ref, bf16[32,4096]{1,0:T(8,128)(2,1)} %in_ref.1, ...), custom_call_target="tpu_custom_call" | custom-call | bytes 104857600 | tf_op jit(solution)/shard_map/pallas_call | solution.py:675
  145.8 7.3 shard_map.213
  155.1 19.7 %shard_map.214 = (bf16[4,2,256,256]{3,2,1,0:T(8,128)(2,1)S(1)}, f32[2,2,2,1024]{3,2,1,0:T(2,128)S(1)}) custom-call(bf16[4,2,256,768]{3,2,1,0:T(8,128)(2,1)S(1)} %bitcast.139, bf16[4,2,256,768]{3,2,1,0:T(8,128)(2,1)S(1)} %bitcast.140, bf16[4,2,256,768]{3,2,1,0:T(8,128)(2,1)S(1)} %bitcast.141, s32[2,1,1024]{2,1,0:T(1,128)S(1)} %fusion.61.id_row_ref, ...), custom_call_target="tpu_custom_call" | custom-call | flops 1000000 | bytes 65536 | tf_op jit(solution)/shard_map/pallas_call | solution.py:192
  175.9 5.3 collective-permute-done.1
  197.6 6.1 collective-permute-done.2
  204.6 9.3 %collective-permute-done.3 = bf16[2,256,256]{2,1,0:T(8,128)(2,1)} collective-permute-done((bf16[2,256,256]{2,1,0:T(8,128)(2,1)}, bf16[2,256,256]{2,1,0:T(8,128)(2,1)}, u32[]{:S(2)}, u32[]{:S(2)}) %collective-permute-start.3) | collective-permute-done | bytes 262176 | tf_op jit(solution)/shard_map/ppermute | solution.py:64
  223.6 18.6 %shard_map.215 = (bf16[512,1024]{1,0:T(8,128)(2,1)S(1)}, bf16[512,4096]{1,0:T(8,128)(2,1)}, bf16[512,4096]{1,0:T(8,128)(2,1)}, f32[512,1024]{1,0:T(8,128)S(1)}, bf16[512,1024]{1,0:T(8,128)(2,1)}) custom-call(f32[512,1024]{1,0:T(8,128)} %convert_add_fusion.middle_ref, f32[8,1024]{1,0:T(8,128)S(1)} %pad.20.gains_ref, f32[8,1024]{1,0:T(8,128)S(1)} %pad.21.biases_ref, ...), custom_call_target="tpu_custom_call" | custom-call | flops 1000000 | bytes 65536 | tf_op jit(solution)/shard_map/pallas_call | solution.py:315
  244.6 21.4 %collective-permute-done.6.wout_low = bf16[512,1024]{1,0:T(8,128)(2,1)S(1)} collective-permute-done((bf16[512,1024]{1,0:T(8,128)(2,1)}, bf16[512,1024]{1,0:T(8,128)(2,1)S(1)}, u32[]{:S(2)}, u32[]{:S(2)}) %collective-permute-start.6) | collective-permute-done | bytes 1048608 | tf_op jit(solution)/shard_map/ppermute | solution.py:69
  286.0 32.4 %collective-permute-done.7 = bf16[512,1024]{1,0:T(8,128)(2,1)} collective-permute-done((bf16[512,1024]{1,0:T(8,128)(2,1)}, bf16[512,1024]{1,0:T(8,128)(2,1)}, u32[]{:S(2)}, u32[]{:S(2)}) %collective-permute-start.7) | collective-permute-done | bytes 1048608 | tf_op jit(solution)/shard_map/ppermute | solution.py:64
  334.3 23.4 %shard_map.216 = (bf16[1536,2048]{1,0:T(8,128)(2,1)}, bf16[1536,2048]{1,0:T(8,128)(2,1)}, bf16[1536,1024]{1,0:T(8,128)(2,1)}, bf16[1536,1024]{1,0:T(8,128)(2,1)}...) custom-call(bf16[768,1024]{1,0:T(8,128)(2,1)} %bitcast.30.x_ref, ...), custom_call_target="tpu_custom_call" | custom-call | flops 1000000 | bytes 65536 | tf_op jit(solution)/shard_map/pallas_call | solution.py:437
  360.2 23.0 %shard_map.217 = (bf16[1536,2048]{1,0:T(8,128)(2,1)}, bf16[1536,2048]{1,0:T(8,128)(2,1)}, bf16[1536,1024]{1,0:T(8,128)(2,1)}, bf16[1536,1024]{1,0:T(8,128)(2,1)}...) custom-call(bf16[768,1024]{1,0:T(8,128)(2,1)} %bitcast.31.x_ref, ...), custom_call_target="tpu_custom_call", output_to_operand_aliasing={{0}: (9, {}), {1}: (10, {}), {2}: (11, {}), {3}: (12, {}), ... | custom-call | flops 1000000 | bytes 65536 | tf_op jit(solution)/shard_map/pallas_call | solution.py:437
  390.2 7.7 fusion.22
  397.9 12.2 %all-to-all-done.3 = bf16[8,96,1024]{2,1,0:T(8,128)(2,1)} async-done(((bf16[8,96,1024]{2,1,0:T(8,128)(2,1)}), bf16[8,96,1024]{2,1,0:T(8,128)(2,1)}, u32[]{:S(2)}, u32[]{:S(2)}) %all-to-all-start.3) | async-done | bytes 1572896 | tf_op jit(solution)/shard_map/all_to_all | solution.py:1075
  421.8 8.4 %fusion.5 = f32[1024,1024]{1,0:T(8,128)} fusion(bf16[1536,1024]{1,0:T(8,128)(2,1)} %get-tuple-element.167, bf16[1536,2048]{1,0:T(8,128)(2,1)} %get-tuple-element.166), kind=kOutput, calls=%fused_computation.16 | convolution fusion | flops 3221225472 | bytes 10485760 | tf_op jit(solution)/shard_map/dot_general | solution.py:39
  430.2 6.8 fusion.25
  446.8 11.2 %collective-permute-done.9 = bf16[512,1024]{1,0:T(8,128)(2,1)S(1)} collective-permute-done((bf16[512,1024]{1,0:T(8,128)(2,1)S(1)}, bf16[512,1024]{1,0:T(8,128)(2,1)S(1)}, u32[]{:S(2)}, u32[]{:S(2)}) %collective-permute-start.9) | collective-permute-done | bytes 1048608 | tf_op jit(solution)/shard_map/ppermute | solution.py:64
  461.9 20.8 %shard_map.218 = (bf16[512,1024]{1,0:T(8,128)(2,1)S(1)}, bf16[512,4096]{1,0:T(8,128)(2,1)}, f32[512,1024]{1,0:T(8,128)S(1)}, bf16[512,1024]{1,0:T(8,128)(2,1)S(1)}, f32[8,1024]{1,0:T(8,128)S(1)}) custom-call(f32[512,1024]{1,0:T(8,128)} %convert_add_fusion.1.back_ref, f32[512,1024]{1,0:T(8,128)} %copy-done.11, bf16[512,1024]{1,0:T(8,128)(2,1)S(1)} %bitcast.152, ...), custom_call_target="tpu_custom_call" | custom-call | flops 1000000 | bytes 65536 | tf_op jit(solution)/shard_map/pallas_call | solution.py:366
  497.3 6.1 convolution_convert_fusion
  509.4 9.9 %collective-permute-done.12 = bf16[2,256,256]{2,1,0:T(8,128)(2,1)S(1)} collective-permute-done((bf16[2,256,256]{2,1,0:T(8,128)(2,1)S(1)}, bf16[2,256,256]{2,1,0:T(8,128)(2,1)S(1)}, u32[]{:S(2)}, u32[]{:S(2)}) %collective-permute-start.12) | collective-permute-done | bytes 262176 | tf_op jit(solution)/shard_map/ppermute | solution.py:64
  542.2 21.2 %shard_map.219 = (bf16[4,2,256,256]{3,2,1,0:T(8,128)(2,1)S(1)}, bf16[4,2,256,256]{3,2,1,0:T(8,128)(2,1)S(1)}, bf16[4,2,256,256]{3,2,1,0:T(8,128)(2,1)S(1)}) custom-call(bf16[4,2,256,768]{3,2,1,0:T(8,128)(2,1)} %bitcast.142, bf16[4,2,256,768]{3,2,1,0:T(8,128)(2,1)} %bitcast.143, bf16[4,2,256,768]{3,2,1,0:T(8,128)(2,1)} %bitcast.144, ...), custom_call_target="tpu_custom_call" | custom-call | flops 1000000 | bytes 65536 | tf_op jit(solution)/shard_map/pallas_call | solution.py:212
  571.6 5.4 fusion.4
  579.4 5.9 add_bitcast_fusion.1
  601.7 13.0 %collective-permute-done.19 = bf16[128,1024]{1,0:T(8,128)(2,1)S(1)} collective-permute-done((bf16[128,1024]{1,0:T(8,128)(2,1)S(1)}, bf16[128,1024]{1,0:T(8,128)(2,1)S(1)}, u32[]{:S(2)}, u32[]{:S(2)}) %collective-permute-start.19) | collective-permute-done | bytes 262176 | tf_op jit(solution)/shard_map/ppermute | solution.py:64
  622.6 138.0 %shard_map.220 = (f32[512,1024]{1,0:T(8,128)}, f32[32,4096]{1,0:T(8,128)}, f32[128,1024]{1,0:T(8,128)}, bf16[4,32,1920]{2,1,0:T(8,128)(2,1)}) custom-call(bf16[4,512,1024]{2,1,0:T(8,128)(2,1)} %bitcast.173, bf16[4,2,2,2,32,4096]{5,4,3,2,1,0:T(8,128)(2,1)} %bitcast.172, bf16[4,2,2,32,4096]{4,3,2,1,0:T(8,128)(2,1)} %collective-permute-done.20.in_added, ...), custom_call_target="tpu_custom_call" | custom-call | bytes 104857600 | tf_op jit(solution)/shard_map/pallas_call | solution.py:957
  (319 shorter events, 219.6 us)
Async XLA Ops:
  133.3 47.9 %collective-permute-start.1 = (bf16[512,1024]{1,0:T(8,128)(2,1)S(1)}, bf16[512,1024]{1,0:T(8,128)(2,1)}, u32[]{:S(2)}, u32[]{:S(2)}) collective-permute-start(bf16[512,1024]{1,0:T(8,128)(2,1)S(1)} %bitcast.150), channel_id=1, source_target_pairs={{0,16},{8,24},{16,0},{24,8},{1,17},{9,25},{17,1},{25,9},{2,18},{10... | collective-permute-start | bytes 3145736 | tf_op jit(solution)/shard_map/ppermute | solution.py:64
  134.9 50.6 %collective-permute-start = (bf16[1024,512]{1,0:T(8,128)(2,1)}, bf16[1024,512]{1,0:T(8,128)(2,1)S(1)}, u32[]{:S(2)}, u32[]{:S(2)}) collective-permute-start(bf16[1024,512]{1,0:T(8,128)(2,1)} %get-tuple-element.249), channel_id=1, source_target_pairs={{0,8},{8,0},{16,24},{24,16},{1,9},{9,1},{17,25},{25,17},{2,10},{10... | collective-permute-start | bytes 3145736 | tf_op jit(solution)/shard_map/ppermute | solution.py:69
  185.5 81.5 %all-to-all-start = ((bf16[8,192,1024]{2,1,0:T(8,128)(2,1)}), bf16[8,192,1024]{2,1,0:T(8,128)(2,1)}, u32[]{:S(2)}, u32[]{:S(2)}) async-start(bf16[8,192,1024]{2,1,0:T(8,128)(2,1)} %pad_maximum_fusion), calls=%async_computation | async-start | bytes 6291456 | tf_op jit(solution)/shard_map/all_to_all | solution.py:1075
  192.3 21.7 %collective-permute-start.3 = (bf16[2,256,256]{2,1,0:T(8,128)(2,1)}, bf16[2,256,256]{2,1,0:T(8,128)(2,1)}, u32[]{:S(2)}, u32[]{:S(2)}) collective-permute-start(bf16[2,256,256]{2,1,0:T(8,128)(2,1)} %get-tuple-element.257), channel_id=1, source_target_pairs={{0,16},{8,24},{16,0},{24,8},{1,17},{9,25},{17,1},{25,9},{2,18},{10... | collective-permute-start | bytes 786440 | tf_op jit(solution)/shard_map/ppermute | solution.py:64
  196.7 18.2 %collective-permute-start.4 = (bf16[2,256,256]{2,1,0:T(8,128)(2,1)}, bf16[2,256,256]{2,1,0:T(8,128)(2,1)S(1)}, u32[]{:S(2)}, u32[]{:S(2)}) collective-permute-start(bf16[2,256,256]{2,1,0:T(8,128)(2,1)} %get-tuple-element.256), channel_id=1, source_target_pairs={{0,24},{8,0},{16,8},{24,16},{1,25},{9,1},{17,9},{25,17},{2,26},{10... | collective-permute-start | bytes 786440 | tf_op jit(solution)/shard_map/ppermute | solution.py:64
  216.0 28.6 %collective-permute-start.5 = (bf16[1024,512]{1,0:T(8,128)(2,1)S(1)}, bf16[1024,512]{1,0:T(8,128)(2,1)S(1)}, u32[]{:S(2)}, u32[]{:S(2)}) collective-permute-start(bf16[1024,512]{1,0:T(8,128)(2,1)S(1)} %copy-done.51), channel_id=1, source_target_pairs={{0,8},{8,0},{16,24},{24,16},{1,9},{9,1},{17,25},{25,17},{2,10},{10... | collective-permute-start | bytes 3145736 | tf_op jit(solution)/shard_map/ppermute | solution.py:69
  220.6 45.4 %collective-permute-start.6 = (bf16[512,1024]{1,0:T(8,128)(2,1)}, bf16[512,1024]{1,0:T(8,128)(2,1)S(1)}, u32[]{:S(2)}, u32[]{:S(2)}) collective-permute-start(bf16[512,1024]{1,0:T(8,128)(2,1)} %get-tuple-element.135), channel_id=1, source_target_pairs={{0,8},{8,0},{16,24},{24,16},{1,9},{9,1},{17,25},{25,17},{2,10},{10... | collective-permute-start | bytes 3145736 | tf_op jit(solution)/shard_map/ppermute | solution.py:69
  270.5 47.9 %collective-permute-start.7 = (bf16[512,1024]{1,0:T(8,128)(2,1)}, bf16[512,1024]{1,0:T(8,128)(2,1)}, u32[]{:S(2)}, u32[]{:S(2)}) collective-permute-start(bf16[512,1024]{1,0:T(8,128)(2,1)} %get-tuple-element.137), channel_id=1, source_target_pairs={{0,16},{8,24},{16,0},{24,8},{1,17},{9,25},{17,1},{25,9},{2,18},{10... | collective-permute-start | bytes 3145736 | tf_op jit(solution)/shard_map/ppermute | solution.py:64
  271.2 56.0 %all-to-all-start.1 = ((bf16[8,96,1024]{2,1,0:T(8,128)(2,1)}), bf16[8,96,1024]{2,1,0:T(8,128)(2,1)}, u32[]{:S(2)}, u32[]{:S(2)}) async-start(bf16[8,96,1024]{2,1,0:T(8,128)(2,1)} %bitcast.192), calls=%async_computation.1 | async-start | bytes 3145728 | tf_op jit(solution)/shard_map/all_to_all | solution.py:1075
  275.5 47.2 %collective-permute-start.8 = (bf16[512,1024]{1,0:T(8,128)(2,1)}, bf16[512,1024]{1,0:T(8,128)(2,1)S(1)}, u32[]{:S(2)}, u32[]{:S(2)}) collective-permute-start(bf16[512,1024]{1,0:T(8,128)(2,1)} %get-tuple-element.138), channel_id=1, source_target_pairs={{0,8},{8,0},{16,24},{24,16},{1,9},{9,1},{17,25},{25,17},{2,10},{10... | collective-permute-start | bytes 3145736 | tf_op jit(solution)/shard_map/ppermute | solution.py:69
  327.2 30.5 %all-to-all-start.2 = ((bf16[8,96,1024]{2,1,0:T(8,128)(2,1)}), bf16[8,96,1024]{2,1,0:T(8,128)(2,1)}, u32[]{:S(2)}, u32[]{:S(2)}) async-start(bf16[8,96,1024]{2,1,0:T(8,128)(2,1)} %bitcast.190), calls=%async_computation.2 | async-start | bytes 3145728 | tf_op jit(solution)/shard_map/all_to_all | solution.py:1075
  384.4 25.7 %all-to-all-start.3 = ((bf16[8,96,1024]{2,1,0:T(8,128)(2,1)}), bf16[8,96,1024]{2,1,0:T(8,128)(2,1)}, u32[]{:S(2)}, u32[]{:S(2)}) async-start(bf16[8,96,1024]{2,1,0:T(8,128)(2,1)} %bitcast.149), calls=%async_computation.3 | async-start | bytes 3145728 | tf_op jit(solution)/shard_map/all_to_all | solution.py:1075
  412.6 45.5 %collective-permute-start.9 = (bf16[512,1024]{1,0:T(8,128)(2,1)S(1)}, bf16[512,1024]{1,0:T(8,128)(2,1)S(1)}, u32[]{:S(2)}, u32[]{:S(2)}) collective-permute-start(bf16[512,1024]{1,0:T(8,128)(2,1)S(1)} %fusion.32), channel_id=1, source_target_pairs={{0,16},{8,24},{16,0},{24,8},{1,17},{9,25},{17,1},{25,9},{2,18},{10... | collective-permute-start | bytes 3145736 | tf_op jit(solution)/shard_map/ppermute | solution.py:64
  415.0 27.0 %all-to-all-start.5 = ((bf16[8,96,1024]{2,1,0:T(8,128)(2,1)}), bf16[8,96,1024]{2,1,0:T(8,128)(2,1)}, u32[]{:S(2)}, u32[]{:S(2)}) async-start(bf16[8,96,1024]{2,1,0:T(8,128)(2,1)} %bitcast.32), calls=%async_computation.5 | async-start | bytes 3145728 | tf_op jit(solution)/shard_map/all_to_all | solution.py:1075
  419.3 77.1 %collective-permute-start.10 = (bf16[1024,1024]{1,0:T(8,128)(2,1)}, bf16[1024,1024]{1,0:T(8,128)(2,1)}, u32[]{:S(2)}, u32[]{:S(2)}) collective-permute-start(bf16[1024,1024]{1,0:T(8,128)(2,1)} %fusion.22), channel_id=1, source_target_pairs={{0,8},{8,0},{16,24},{24,16},{1,9},{9,1},{17,25},{25,17},{2,10},{10... | collective-permute-start | bytes 6291464 | tf_op jit(solution)/shard_map/ppermute | solution.py:69
  442.0 79.9 %all-to-all-start.4 = ((bf16[8,192,1024]{2,1,0:T(8,128)(2,1)}), bf16[8,192,1024]{2,1,0:T(8,128)(2,1)}, u32[]{:S(2)}, u32[]{:S(2)}) async-start(bf16[8,192,1024]{2,1,0:T(8,128)(2,1)} %get-tuple-element.163), calls=%async_computation.4 | async-start | bytes 6291456 | tf_op jit(solution)/shard_map/all_to_all | solution.py:1075
  509.3 113.3 %collective-permute-start.21 = (bf16[4,2,2,128,1024]{4,3,2,1,0:T(8,128)(2,1)}, bf16[4,2,2,128,1024]{4,3,2,1,0:T(8,128)(2,1)}, u32[]{:S(2)}, u32[]{:S(2)}) collective-permute-start(bf16[4,2,2,128,1024]{4,3,2,1,0:T(8,128)(2,1)} %dynamic-slice_bitcast_fusion), channel_id=1, source_target_pairs={{0,1},{1,0},{2,3},{3,2},{4,5},{5,4},{6,7},{7,6},{8,9},{9,8},{10,11... | collective-permute-start | bytes 12582920 | tf_op jit(solution)/shard_map/ppermute | solution.py:226
  528.6 35.7 %collective-permute-start.14 = (bf16[512,1024]{1,0:T(8,128)(2,1)}, bf16[512,1024]{1,0:T(8,128)(2,1)S(1)}, u32[]{:S(2)}, u32[]{:S(2)}) collective-permute-start(bf16[512,1024]{1,0:T(8,128)(2,1)} %slice.192), channel_id=1, source_target_pairs={{0,8},{8,0},{16,24},{24,16},{1,9},{9,1},{17,25},{25,17},{2,10},{10... | collective-permute-start | bytes 3145736 | tf_op jit(solution)/shard_map/ppermute | solution.py:69
  533.8 29.9 %collective-permute-start.15 = (bf16[256,1024]{1,0:T(8,128)(2,1)S(1)}, bf16[256,1024]{1,0:T(8,128)(2,1)}, u32[]{:S(2)}, u32[]{:S(2)}) collective-permute-start(bf16[256,1024]{1,0:T(8,128)(2,1)S(1)} %slice.225), channel_id=1, source_target_pairs={{0,16},{8,24},{16,0},{24,8},{1,17},{9,25},{17,1},{25,9},{2,18},{10... | collective-permute-start | bytes 1572872 | tf_op jit(solution)/shard_map/ppermute | solution.py:64
  571.6 51.0 %collective-permute-start.20 = (bf16[4,2,2,32,4096]{4,3,2,1,0:T(8,128)(2,1)}, bf16[4,2,2,32,4096]{4,3,2,1,0:T(8,128)(2,1)}, u32[]{:S(2)}, u32[]{:S(2)}) collective-permute-start(bf16[4,2,2,32,4096]{4,3,2,1,0:T(8,128)(2,1)} %dynamic-slice_bitcast_fusion.1), channel_id=1, source_target_pairs={{0,1},{1,0},{2,3},{3,2},{4,5},{5,4},{6,7},{7,6},{8,9},{9,8},{10,11... | collective-permute-start | bytes 12582920 | tf_op jit(solution)/shard_map/ppermute | solution.py:226
  577.2 20.0 %collective-permute-start.16 = (bf16[256,1024]{1,0:T(8,128)(2,1)S(1)}, bf16[256,1024]{1,0:T(8,128)(2,1)S(1)}, u32[]{:S(2)}, u32[]{:S(2)}) collective-permute-start(bf16[256,1024]{1,0:T(8,128)(2,1)S(1)} %copy-done.55), channel_id=1, source_target_pairs={{0,8},{8,0},{16,24},{24,16},{1,9},{9,1},{17,25},{25,17},{2,10},{10... | collective-permute-start | bytes 1572872 | tf_op jit(solution)/shard_map/ppermute | solution.py:69
  577.8 17.6 %collective-permute-start.17 = (bf16[128,1024]{1,0:T(8,128)(2,1)}, bf16[128,1024]{1,0:T(8,128)(2,1)}, u32[]{:S(2)}, u32[]{:S(2)}) collective-permute-start(bf16[128,1024]{1,0:T(8,128)(2,1)} %get-tuple-element.198), channel_id=1, source_target_pairs={{0,16},{8,24},{16,0},{24,8},{1,17},{9,25},{17,1},{25,9},{2,18},{10... | collective-permute-start | bytes 786440 | tf_op jit(solution)/shard_map/ppermute | solution.py:64
  597.2 19.4 %collective-permute-start.18 = (bf16[256,1024]{1,0:T(8,128)(2,1)}, bf16[256,1024]{1,0:T(8,128)(2,1)S(1)}, u32[]{:S(2)}, u32[]{:S(2)}) collective-permute-start(bf16[256,1024]{1,0:T(8,128)(2,1)} %get-tuple-element.207), channel_id=1, source_target_pairs={{0,8},{8,0},{16,24},{24,16},{1,9},{9,1},{17,25},{25,17},{2,10},{10... | collective-permute-start | bytes 1572872 | tf_op jit(solution)/shard_map/ppermute | solution.py:69
  599.8 15.0 %collective-permute-start.19 = (bf16[128,1024]{1,0:T(8,128)(2,1)S(1)}, bf16[128,1024]{1,0:T(8,128)(2,1)S(1)}, u32[]{:S(2)}, u32[]{:S(2)}) collective-permute-start(bf16[128,1024]{1,0:T(8,128)(2,1)S(1)} %get-tuple-element.208), channel_id=1, source_target_pairs={{0,16},{8,24},{16,0},{24,8},{1,17},{9,25},{17,1},{25,9},{2,18},{10... | collective-permute-start | bytes 786440 | tf_op jit(solution)/shard_map/ppermute | solution.py:64
  (74 other events, 1067.3 us)

commit v5 on v4

--- a/solution.py
+++ b/solution.py
@@ -1020,13 +1020,15 @@
 
     depth = out_proj.shape[0]
     wide = 3 * cols + width + LANES
-    slices = qkv_proj.reshape(3, depth, seq_size, cols).transpose(2, 1, 0, 3).reshape(seq_size, depth, 3 * cols)
     small = jnp.concatenate(
         [norm_gains.reshape(-1), norm_biases.reshape(-1), centroids[0], routes.reshape(tokens).astype(BF)]
     )
     small = jnp.pad(small, (0, depth * LANES - small.shape[0])).reshape(depth, LANES)
-    slices = jnp.concatenate(
-        [slices, *[jnp.broadcast_to(v[None], (seq_size, *v.shape)) for v in (out_proj, small)]], axis=2
+    slices = jnp.stack(
+        [
+            jnp.concatenate([*[qkv_proj[j, :, i * cols : (i + 1) * cols] for j in range(3)], out_proj, small], axis=1)
+            for i in range(seq_size)
+        ]
     )
     spare = -depth % 16
     bits = fsdp_bits(False)
@@ -1174,8 +1176,8 @@
     ffin_terms = mm_tn(hidden_low, hidden_grad).astype(BF)
     proj_terms = mm_tn(attended, branch).astype(BF).reshape(seq_size, fsdp_size, depth, width)
     def split(values):
-        size = values.shape[0] // 4
-        return values[: 2 * size], values[2 * size : 3 * size], values[3 * size :]
+        size = values.shape[0] // 8
+        return values[: 4 * size], values[4 * size : 7 * size], values[7 * size :]
 
     def send_pieces(pieces):
         return [seq_pair(pieces[0])] + [seq_shift(pieces[group], -2 * group) for group in range(1, groups)]
@@ -1201,6 +1203,8 @@
     proj_terms = jnp.pad(proj_terms, ((0, 0), (0, 0), (0, spare), (3 * cols, LANES)))
     out_first, out_second = moved[:sizes], send_pieces(moved[sizes:])
     normed_low_terms = mm_nt(projected_grad, qkv_mine).astype(BF)
+    normed_low_terms, *moved = tie(normed_low_terms, *out_second, *[pieces[2] for pieces in out_pieces])
+    out_second, out_third = moved[:sizes], send_pieces(moved[sizes:])
     parts_all = norm_parts(inputs_all.astype(F32))
     unit_all = (inputs_all.astype(F32) - parts_all[0]) * parts_all[1]
     terms_wide = normed_low_terms.astype(F32)
@@ -1208,8 +1212,6 @@
     small_terms = jnp.stack([gain_one, gain_two, gain_three, bias_one, bias_two, bias_three])
 
     qkv_term = mm_tn(normed_flat, projected_grad).astype(BF).reshape(seq_size, fsdp_size, depth, 3 * cols)
-    qkv_term, *moved = tie(qkv_term, *out_second, *[pieces[2] for pieces in out_pieces])
-    out_second, out_third = moved[:sizes], send_pieces(moved[sizes:])
     small_rows = small_terms.astype(BF).reshape(6, seq_size, fsdp_size, depth).transpose(1, 2, 0, 3)
     centroid_rows = jnp.where(
         (jnp.arange(fsdp_size) == fsdp_here)[None, :, None], centroid_term.reshape(seq_size, 1, cols), 0.0
@@ -1228,8 +1230,12 @@
     )
     ffn_in_grad, ffn_out_grad = ffn_in_grad.reshape(ffn_in.shape), ffn_out_grad.reshape(ffn_out.shape)
     proj_sums = proj_sums.astype(F32)
-    qkv_grad = proj_sums[:, :depth, : 3 * cols].reshape(seq_size, depth, 3, cols)
-    qkv_grad = qkv_grad.transpose(2, 1, 0, 3).reshape(qkv_proj.shape)
+    qkv_grad = jnp.stack(
+        [
+            jnp.concatenate([proj_sums[i, :depth, j * cols : (j + 1) * cols] for i in range(seq_size)], axis=1)
+            for j in range(3)
+        ]
+    )
     out_proj_grad = jnp.sum(proj_sums[:, :depth, 3 * cols : 3 * cols + width], axis=0)
     small = jnp.sum(proj_sums[:, :depth, 3 * cols + width :], axis=0).reshape(-1)
     small_grad = small[: 6 * depth].reshape(6, depth)

time: 789 us -> 776 us (0.984)
  waiting for transfers between devices: 136 us -> 127 us
    reshape x5 -> x0, local copies, waits for them, and re-layouts: 7.96 us -> none  [the longest x3 3.88 us: on_device(): qkv_proj.reshape(3, depth, seq_size, cols).transpose(2, 1, 0, 3)]
    unnamed x152 -> x158, local copies, waits for them, and re-layouts: 24.5 us -> 28.9 us
  transfers between devices with their start and end apart: 28 -> 28, of which waited for: 17 -> 17; matrix products, arithmetic and copies ran while one was open for 17% -> 18% of each run, Pallas kernels for 14% -> 14%
where the time goes in v5:
time: 776 us; the launch traced here: 766 us
  Pallas kernels  396 us (51%)
  waiting for transfers between devices  127 us (16%)
  local copies, waits for them, and re-layouts  76.5 us (10%)
  matrix products  74.7 us (10%)
  starting transfers between devices  57.1 us (7%)
  other arithmetic  32.9 us (4%)
    pallas_call x1, Pallas kernels, finish_sums(): pl.pallas_call(functools.partial(finish_kernel, seq_size, bits), in_specs...  139 us
    pallas_call x1, Pallas kernels, start_gathers(): pl.pallas_call(functools.partial(gather_kernel, seq_size, bits), in_specs...  123 us
    ppermute x12, waiting for transfers between devices, seq_shift(): lax.ppermute(values, 'seq', [(i, (i + step) % size) for i in range(size)])  86.9 us
    dot_general x12, matrix products, mm_tn(): lax.dot_general(left, right, (((0,), (0,)), ((), ())), preferred_element_...  54.5 us
    pallas_call x2, Pallas kernels, expert_block(): pl.pallas_call(expert_kernel, grid=(own + 2,), in_specs=[whole, whole, ro...  46.4 us
    unnamed x158, local copies, waits for them, and re-layouts  28.9 us
    ppermute x8, waiting for transfers between devices, seq_pair(): return lax.ppermute(values, 'seq', [(i, i ^ 1) for i in range(size)])  28.5 us
    all_to_all x6, starting transfers between devices, swap_slots(): lax.all_to_all(values, 'fsdp', split_axis=0, concat_axis=0, tiled=True)  26.6 us
  transfers between devices with their start and end apart: 28, of which 17 were waited for; matrix products, arithmetic and copies ran while one was open for 18% of the time, Pallas kernels for 14%

profile of v5, /device:TPU:0, one launch (start us, length us, event | category | flops | bytes accessed | tf_op | source)
XLA Modules:
  0.0 766.3 jit_solution(15388524256670626862)
XLA Ops:
  9.3 123.1 %shard_map.212 = (bf16[4,2,2,2,32,1920]{5,4,3,2,1,0:T(8,128)(2,1)}, bf16[4,2,2,2,32,4096]{5,4,3,2,1,0:T(8,128)(2,1)}, bf16[4,2,2,2,128,1024]{5,4,3,2,1,0:T(8,128)(2,1)}, bf16[4,512,1024]{2,1,0:T(8,128)(2,1)}) custom-call(bf16[4,32,1920]{2,1,0:T(8,128)(2,1)} %pad_maximum_fusion.2.proj_ref, bf16[32,4096]{1,0:T(8,128)(2,1)} %in_ref.1, ...), custom_call_target="tpu_custom_call" | custom-call | bytes 104857600 | tf_op jit(solution)/shard_map/pallas_call | solution.py:675
  143.1 7.3 shard_map.213
  152.4 19.7 %shard_map.214 = (bf16[4,2,256,256]{3,2,1,0:T(8,128)(2,1)S(1)}, f32[2,2,2,1024]{3,2,1,0:T(2,128)S(1)}) custom-call(bf16[4,2,256,768]{3,2,1,0:T(8,128)(2,1)S(1)} %bitcast.201, bf16[4,2,256,768]{3,2,1,0:T(8,128)(2,1)S(1)} %bitcast.202, bf16[4,2,256,768]{3,2,1,0:T(8,128)(2,1)S(1)} %bitcast.203, s32[2,1,1024]{2,1,0:T(1,128)S(1)} %fusion.61.id_row_ref, ...), custom_call_target="tpu_custom_call" | custom-call | flops 1000000 | bytes 65536 | tf_op jit(solution)/shard_map/pallas_call | solution.py:192
  173.2 7.0 collective-permute-done.1
  196.8 6.0 collective-permute-done.2
  203.7 9.3 %collective-permute-done.3 = bf16[2,256,256]{2,1,0:T(8,128)(2,1)} collective-permute-done((bf16[2,256,256]{2,1,0:T(8,128)(2,1)}, bf16[2,256,256]{2,1,0:T(8,128)(2,1)}, u32[]{:S(2)}, u32[]{:S(2)}) %collective-permute-start.3) | collective-permute-done | bytes 262176 | tf_op jit(solution)/shard_map/ppermute | solution.py:64
  222.7 18.6 %shard_map.215 = (bf16[512,1024]{1,0:T(8,128)(2,1)S(1)}, bf16[512,4096]{1,0:T(8,128)(2,1)}, bf16[512,4096]{1,0:T(8,128)(2,1)}, f32[512,1024]{1,0:T(8,128)S(1)}, bf16[512,1024]{1,0:T(8,128)(2,1)}) custom-call(f32[512,1024]{1,0:T(8,128)} %convert_add_fusion.middle_ref, f32[8,1024]{1,0:T(8,128)S(1)} %pad.20.gains_ref, f32[8,1024]{1,0:T(8,128)S(1)} %pad.21.biases_ref, ...), custom_call_target="tpu_custom_call" | custom-call | flops 1000000 | bytes 65536 | tf_op jit(solution)/shard_map/pallas_call | solution.py:315
  243.8 21.4 %collective-permute-done.6.wout_low = bf16[512,1024]{1,0:T(8,128)(2,1)S(1)} collective-permute-done((bf16[512,1024]{1,0:T(8,128)(2,1)}, bf16[512,1024]{1,0:T(8,128)(2,1)S(1)}, u32[]{:S(2)}, u32[]{:S(2)}) %collective-permute-start.6) | collective-permute-done | bytes 1048608 | tf_op jit(solution)/shard_map/ppermute | solution.py:69
  285.8 31.8 %collective-permute-done.7 = bf16[512,1024]{1,0:T(8,128)(2,1)} collective-permute-done((bf16[512,1024]{1,0:T(8,128)(2,1)}, bf16[512,1024]{1,0:T(8,128)(2,1)}, u32[]{:S(2)}, u32[]{:S(2)}) %collective-permute-start.7) | collective-permute-done | bytes 1048608 | tf_op jit(solution)/shard_map/ppermute | solution.py:64
  334.2 23.5 %shard_map.216 = (bf16[1536,2048]{1,0:T(8,128)(2,1)}, bf16[1536,2048]{1,0:T(8,128)(2,1)}, bf16[1536,1024]{1,0:T(8,128)(2,1)}, bf16[1536,1024]{1,0:T(8,128)(2,1)}...) custom-call(bf16[768,1024]{1,0:T(8,128)(2,1)} %bitcast.45.x_ref, ...), custom_call_target="tpu_custom_call" | custom-call | flops 1000000 | bytes 65536 | tf_op jit(solution)/shard_map/pallas_call | solution.py:437
  360.1 22.9 %shard_map.217 = (bf16[1536,2048]{1,0:T(8,128)(2,1)}, bf16[1536,2048]{1,0:T(8,128)(2,1)}, bf16[1536,1024]{1,0:T(8,128)(2,1)}, bf16[1536,1024]{1,0:T(8,128)(2,1)}...) custom-call(bf16[768,1024]{1,0:T(8,128)(2,1)} %bitcast.46.x_ref, ...), custom_call_target="tpu_custom_call", output_to_operand_aliasing={{0}: (9, {}), {1}: (10, {}), {2}: (11, {}), {3}: (12, {}), ... | custom-call | flops 1000000 | bytes 65536 | tf_op jit(solution)/shard_map/pallas_call | solution.py:437
  390.6 7.7 %fusion.22 = bf16[1024,1024]{1,0:T(8,128)(2,1)} fusion(bf16[1536,1024]{1,0:T(8,128)(2,1)} %get-tuple-element.168, bf16[1536,2048]{1,0:T(8,128)(2,1)} %get-tuple-element.169), kind=kOutput, calls=%fused_computation.39 | convolution fusion | flops 3222274048 | bytes 8388608 | tf_op jit(solution)/shard_map/dot_general | solution.py:39
  398.3 11.0 %all-to-all-done.3 = bf16[8,96,1024]{2,1,0:T(8,128)(2,1)S(1)} async-done(((bf16[8,96,1024]{2,1,0:T(8,128)(2,1)}), bf16[8,96,1024]{2,1,0:T(8,128)(2,1)S(1)}, u32[]{:S(2)}, u32[]{:S(2)}) %all-to-all-start.3) | async-done | bytes 1572896 | tf_op jit(solution)/shard_map/all_to_all | solution.py:1077
  420.6 8.5 %fusion.5 = f32[1024,1024]{1,0:T(8,128)} fusion(bf16[1536,1024]{1,0:T(8,128)(2,1)} %get-tuple-element.167, bf16[1536,2048]{1,0:T(8,128)(2,1)} %get-tuple-element.166), kind=kOutput, calls=%fused_computation.16 | convolution fusion | flops 3221225472 | bytes 10485760 | tf_op jit(solution)/shard_map/dot_general | solution.py:39
  433.8 5.1 fusion.7
  443.8 13.4 %collective-permute-done.9 = bf16[512,1024]{1,0:T(8,128)(2,1)} collective-permute-done((bf16[512,1024]{1,0:T(8,128)(2,1)}, bf16[512,1024]{1,0:T(8,128)(2,1)}, u32[]{:S(2)}, u32[]{:S(2)}) %collective-permute-start.9) | collective-permute-done | bytes 1048608 | tf_op jit(solution)/shard_map/ppermute | solution.py:64
  464.1 20.7 %shard_map.218 = (bf16[512,1024]{1,0:T(8,128)(2,1)S(1)}, bf16[512,4096]{1,0:T(8,128)(2,1)}, f32[512,1024]{1,0:T(8,128)S(1)}, bf16[512,1024]{1,0:T(8,128)(2,1)S(1)}, f32[8,1024]{1,0:T(8,128)S(1)}) custom-call(f32[512,1024]{1,0:T(8,128)} %convert_add_fusion.1.back_ref, f32[512,1024]{1,0:T(8,128)} %copy-done.11, bf16[512,1024]{1,0:T(8,128)(2,1)S(1)} %bitcast.214, ...), custom_call_target="tpu_custom_call" | custom-call | flops 1000000 | bytes 65536 | tf_op jit(solution)/shard_map/pallas_call | solution.py:366
  496.7 7.0 convolution_convert_fusion
  510.0 8.9 %collective-permute-done.12 = bf16[2,256,256]{2,1,0:T(8,128)(2,1)S(1)} collective-permute-done((bf16[2,256,256]{2,1,0:T(8,128)(2,1)S(1)}, bf16[2,256,256]{2,1,0:T(8,128)(2,1)S(1)}, u32[]{:S(2)}, u32[]{:S(2)}) %collective-permute-start.12) | collective-permute-done | bytes 262176 | tf_op jit(solution)/shard_map/ppermute | solution.py:64
  528.3 5.0 convolution_convert_fusion.1
  541.4 21.1 %shard_map.219 = (bf16[4,2,256,256]{3,2,1,0:T(8,128)(2,1)S(1)}, bf16[4,2,256,256]{3,2,1,0:T(8,128)(2,1)S(1)}, bf16[4,2,256,256]{3,2,1,0:T(8,128)(2,1)S(1)}) custom-call(bf16[4,2,256,768]{3,2,1,0:T(8,128)(2,1)} %bitcast.204, bf16[4,2,256,768]{3,2,1,0:T(8,128)(2,1)} %bitcast.205, bf16[4,2,256,768]{3,2,1,0:T(8,128)(2,1)} %bitcast.206, ...), custom_call_target="tpu_custom_call" | custom-call | flops 1000000 | bytes 65536 | tf_op jit(solution)/shard_map/pallas_call | solution.py:212
  583.1 5.8 add_bitcast_fusion.1
  601.7 5.5 collective-permute-done.19
  615.0 139.3 %shard_map.220 = (f32[512,1024]{1,0:T(8,128)}, f32[32,4096]{1,0:T(8,128)}, f32[128,1024]{1,0:T(8,128)}, bf16[4,32,1920]{2,1,0:T(8,128)(2,1)}) custom-call(bf16[4,512,1024]{2,1,0:T(8,128)(2,1)} %bitcast.219, bf16[4,2,2,2,32,4096]{5,4,3,2,1,0:T(8,128)(2,1)} %bitcast.235, bf16[4,2,2,32,4096]{4,3,2,1,0:T(8,128)(2,1)} %collective-permute-done.20.in_added, ...), custom_call_target="tpu_custom_call" | custom-call | bytes 104857600 | tf_op jit(solution)/shard_map/pallas_call | solution.py:957
  (325 shorter events, 214.4 us)
Async XLA Ops:
  132.4 47.9 %collective-permute-start.1 = (bf16[512,1024]{1,0:T(8,128)(2,1)S(1)}, bf16[512,1024]{1,0:T(8,128)(2,1)}, u32[]{:S(2)}, u32[]{:S(2)}) collective-permute-start(bf16[512,1024]{1,0:T(8,128)(2,1)S(1)} %bitcast.212), channel_id=1, source_target_pairs={{0,16},{8,24},{16,0},{24,8},{1,17},{9,25},{17,1},{25,9},{2,18},{10... | collective-permute-start | bytes 3145736 | tf_op jit(solution)/shard_map/ppermute | solution.py:64
  135.5 49.2 %collective-permute-start = (bf16[1024,512]{1,0:T(8,128)(2,1)}, bf16[1024,512]{1,0:T(8,128)(2,1)S(1)}, u32[]{:S(2)}, u32[]{:S(2)}) collective-permute-start(bf16[1024,512]{1,0:T(8,128)(2,1)} %get-tuple-element.247), channel_id=1, source_target_pairs={{0,8},{8,0},{16,24},{24,16},{1,9},{9,1},{17,25},{25,17},{2,10},{10... | collective-permute-start | bytes 3145736 | tf_op jit(solution)/shard_map/ppermute | solution.py:69
  184.6 81.6 %all-to-all-start = ((bf16[8,192,1024]{2,1,0:T(8,128)(2,1)}), bf16[8,192,1024]{2,1,0:T(8,128)(2,1)}, u32[]{:S(2)}, u32[]{:S(2)}) async-start(bf16[8,192,1024]{2,1,0:T(8,128)(2,1)} %pad_maximum_fusion), calls=%async_computation | async-start | bytes 6291456 | tf_op jit(solution)/shard_map/all_to_all | solution.py:1077
  191.2 11.5 %collective-permute-start.2 = (bf16[2,256,256]{2,1,0:T(8,128)(2,1)}, bf16[2,256,256]{2,1,0:T(8,128)(2,1)}, u32[]{:S(2)}, u32[]{:S(2)}) collective-permute-start(bf16[2,256,256]{2,1,0:T(8,128)(2,1)} %get-tuple-element.254), channel_id=1, source_target_pairs={{0,8},{8,16},{16,24},{24,0},{1,9},{9,17},{17,25},{25,1},{2,10},{10... | collective-permute-start | bytes 786440 | tf_op jit(solution)/shard_map/ppermute | solution.py:64
  191.4 21.7 %collective-permute-start.3 = (bf16[2,256,256]{2,1,0:T(8,128)(2,1)}, bf16[2,256,256]{2,1,0:T(8,128)(2,1)}, u32[]{:S(2)}, u32[]{:S(2)}) collective-permute-start(bf16[2,256,256]{2,1,0:T(8,128)(2,1)} %get-tuple-element.253), channel_id=1, source_target_pairs={{0,16},{8,24},{16,0},{24,8},{1,17},{9,25},{17,1},{25,9},{2,18},{10... | collective-permute-start | bytes 786440 | tf_op jit(solution)/shard_map/ppermute | solution.py:64
  195.9 18.2 %collective-permute-start.4 = (bf16[2,256,256]{2,1,0:T(8,128)(2,1)}, bf16[2,256,256]{2,1,0:T(8,128)(2,1)S(1)}, u32[]{:S(2)}, u32[]{:S(2)}) collective-permute-start(bf16[2,256,256]{2,1,0:T(8,128)(2,1)} %get-tuple-element.252), channel_id=1, source_target_pairs={{0,24},{8,0},{16,8},{24,16},{1,25},{9,1},{17,9},{25,17},{2,26},{10... | collective-permute-start | bytes 786440 | tf_op jit(solution)/shard_map/ppermute | solution.py:64
  215.2 28.6 %collective-permute-start.5 = (bf16[1024,512]{1,0:T(8,128)(2,1)S(1)}, bf16[1024,512]{1,0:T(8,128)(2,1)S(1)}, u32[]{:S(2)}, u32[]{:S(2)}) collective-permute-start(bf16[1024,512]{1,0:T(8,128)(2,1)S(1)} %copy-done.47), channel_id=1, source_target_pairs={{0,8},{8,0},{16,24},{24,16},{1,9},{9,1},{17,25},{25,17},{2,10},{10... | collective-permute-start | bytes 3145736 | tf_op jit(solution)/shard_map/ppermute | solution.py:69
  219.8 45.4 %collective-permute-start.6 = (bf16[512,1024]{1,0:T(8,128)(2,1)}, bf16[512,1024]{1,0:T(8,128)(2,1)S(1)}, u32[]{:S(2)}, u32[]{:S(2)}) collective-permute-start(bf16[512,1024]{1,0:T(8,128)(2,1)} %get-tuple-element.135), channel_id=1, source_target_pairs={{0,8},{8,0},{16,24},{24,16},{1,9},{9,1},{17,25},{25,17},{2,10},{10... | collective-permute-start | bytes 3145736 | tf_op jit(solution)/shard_map/ppermute | solution.py:69
  269.7 47.9 %collective-permute-start.7 = (bf16[512,1024]{1,0:T(8,128)(2,1)}, bf16[512,1024]{1,0:T(8,128)(2,1)}, u32[]{:S(2)}, u32[]{:S(2)}) collective-permute-start(bf16[512,1024]{1,0:T(8,128)(2,1)} %get-tuple-element.137), channel_id=1, source_target_pairs={{0,16},{8,24},{16,0},{24,8},{1,17},{9,25},{17,1},{25,9},{2,18},{10... | collective-permute-start | bytes 3145736 | tf_op jit(solution)/shard_map/ppermute | solution.py:64
  270.4 55.9 %all-to-all-start.1 = ((bf16[8,96,1024]{2,1,0:T(8,128)(2,1)}), bf16[8,96,1024]{2,1,0:T(8,128)(2,1)}, u32[]{:S(2)}, u32[]{:S(2)}) async-start(bf16[8,96,1024]{2,1,0:T(8,128)(2,1)} %bitcast.254), calls=%async_computation.1 | async-start | bytes 3145728 | tf_op jit(solution)/shard_map/all_to_all | solution.py:1077
  274.7 47.2 %collective-permute-start.8 = (bf16[512,1024]{1,0:T(8,128)(2,1)}, bf16[512,1024]{1,0:T(8,128)(2,1)S(1)}, u32[]{:S(2)}, u32[]{:S(2)}) collective-permute-start(bf16[512,1024]{1,0:T(8,128)(2,1)} %get-tuple-element.138), channel_id=1, source_target_pairs={{0,8},{8,0},{16,24},{24,16},{1,9},{9,1},{17,25},{25,17},{2,10},{10... | collective-permute-start | bytes 3145736 | tf_op jit(solution)/shard_map/ppermute | solution.py:69
  326.3 31.4 %all-to-all-start.2 = ((bf16[8,96,1024]{2,1,0:T(8,128)(2,1)}), bf16[8,96,1024]{2,1,0:T(8,128)(2,1)}, u32[]{:S(2)}, u32[]{:S(2)}) async-start(bf16[8,96,1024]{2,1,0:T(8,128)(2,1)} %bitcast.253), calls=%async_computation.2 | async-start | bytes 3145728 | tf_op jit(solution)/shard_map/all_to_all | solution.py:1077
  384.1 25.2 %all-to-all-start.3 = ((bf16[8,96,1024]{2,1,0:T(8,128)(2,1)}), bf16[8,96,1024]{2,1,0:T(8,128)(2,1)S(1)}, u32[]{:S(2)}, u32[]{:S(2)}) async-start(bf16[8,96,1024]{2,1,0:T(8,128)(2,1)} %bitcast.211), calls=%async_computation.3 | async-start | bytes 3145728 | tf_op jit(solution)/shard_map/all_to_all | solution.py:1077
  411.3 45.9 %collective-permute-start.9 = (bf16[512,1024]{1,0:T(8,128)(2,1)}, bf16[512,1024]{1,0:T(8,128)(2,1)}, u32[]{:S(2)}, u32[]{:S(2)}) collective-permute-start(bf16[512,1024]{1,0:T(8,128)(2,1)} %fusion.32), channel_id=1, source_target_pairs={{0,16},{8,24},{16,0},{24,8},{1,17},{9,25},{17,1},{25,9},{2,18},{10... | collective-permute-start | bytes 3145736 | tf_op jit(solution)/shard_map/ppermute | solution.py:64
  413.7 25.5 %all-to-all-start.5 = ((bf16[8,96,1024]{2,1,0:T(8,128)(2,1)}), bf16[8,96,1024]{2,1,0:T(8,128)(2,1)}, u32[]{:S(2)}, u32[]{:S(2)}) async-start(bf16[8,96,1024]{2,1,0:T(8,128)(2,1)} %bitcast.47), calls=%async_computation.5 | async-start | bytes 3145728 | tf_op jit(solution)/shard_map/all_to_all | solution.py:1077
  418.2 76.7 %collective-permute-start.10 = (bf16[1024,1024]{1,0:T(8,128)(2,1)}, bf16[1024,1024]{1,0:T(8,128)(2,1)}, u32[]{:S(2)}, u32[]{:S(2)}) collective-permute-start(bf16[1024,1024]{1,0:T(8,128)(2,1)} %fusion.22), channel_id=1, source_target_pairs={{0,8},{8,0},{16,24},{24,16},{1,9},{9,1},{17,25},{25,17},{2,10},{10... | collective-permute-start | bytes 6291464 | tf_op jit(solution)/shard_map/ppermute | solution.py:69
  439.2 82.4 %all-to-all-start.4 = ((bf16[8,192,1024]{2,1,0:T(8,128)(2,1)}), bf16[8,192,1024]{2,1,0:T(8,128)(2,1)}, u32[]{:S(2)}, u32[]{:S(2)}) async-start(bf16[8,192,1024]{2,1,0:T(8,128)(2,1)} %get-tuple-element.163), calls=%async_computation.4 | async-start | bytes 6291456 | tf_op jit(solution)/shard_map/all_to_all | solution.py:1077
  506.0 12.9 %collective-permute-start.12 = (bf16[2,256,256]{2,1,0:T(8,128)(2,1)S(1)}, bf16[2,256,256]{2,1,0:T(8,128)(2,1)S(1)}, u32[]{:S(2)}, u32[]{:S(2)}) collective-permute-start(bf16[2,256,256]{2,1,0:T(8,128)(2,1)S(1)} %get-tuple-element.178), channel_id=1, source_target_pairs={{0,16},{8,24},{16,0},{24,8},{1,17},{9,25},{17,1},{25,9},{2,18},{10... | collective-permute-start | bytes 786440 | tf_op jit(solution)/shard_map/ppermute | solution.py:64
  510.0 105.1 %collective-permute-start.21 = (bf16[4,2,2,128,1024]{4,3,2,1,0:T(8,128)(2,1)}, bf16[4,2,2,128,1024]{4,3,2,1,0:T(8,128)(2,1)}, u32[]{:S(2)}, u32[]{:S(2)}) collective-permute-start(bf16[4,2,2,128,1024]{4,3,2,1,0:T(8,128)(2,1)} %dynamic-slice_bitcast_fusion), channel_id=1, source_target_pairs={{0,1},{1,0},{2,3},{3,2},{4,5},{5,4},{6,7},{7,6},{8,9},{9,8},{10,11... | collective-permute-start | bytes 12582920 | tf_op jit(solution)/shard_map/ppermute | solution.py:226
  528.2 35.9 %collective-permute-start.14 = (bf16[512,1024]{1,0:T(8,128)(2,1)}, bf16[512,1024]{1,0:T(8,128)(2,1)}, u32[]{:S(2)}, u32[]{:S(2)}) collective-permute-start(bf16[512,1024]{1,0:T(8,128)(2,1)} %slice.273), channel_id=1, source_target_pairs={{0,8},{8,0},{16,24},{24,16},{1,9},{9,1},{17,25},{25,17},{2,10},{10... | collective-permute-start | bytes 3145736 | tf_op jit(solution)/shard_map/ppermute | solution.py:69
  533.4 29.5 %collective-permute-start.15 = (bf16[256,1024]{1,0:T(8,128)(2,1)}, bf16[256,1024]{1,0:T(8,128)(2,1)S(1)}, u32[]{:S(2)}, u32[]{:S(2)}) collective-permute-start(bf16[256,1024]{1,0:T(8,128)(2,1)} %slice.317), channel_id=1, source_target_pairs={{0,16},{8,24},{16,0},{24,8},{1,17},{9,25},{17,1},{25,9},{2,18},{10... | collective-permute-start | bytes 1572872 | tf_op jit(solution)/shard_map/ppermute | solution.py:64
  567.0 25.5 %collective-permute-start.16 = (bf16[384,1024]{1,0:T(8,128)(2,1)S(1)}, bf16[384,1024]{1,0:T(8,128)(2,1)S(1)}, u32[]{:S(2)}, u32[]{:S(2)}) collective-permute-start(bf16[384,1024]{1,0:T(8,128)(2,1)S(1)} %copy-done.48), channel_id=1, source_target_pairs={{0,8},{8,0},{16,24},{24,16},{1,9},{9,1},{17,25},{25,17},{2,10},{10... | collective-permute-start | bytes 2359304 | tf_op jit(solution)/shard_map/ppermute | solution.py:69
  568.0 22.9 %collective-permute-start.17 = (bf16[192,1024]{1,0:T(8,128)(2,1)}, bf16[192,1024]{1,0:T(8,128)(2,1)}, u32[]{:S(2)}, u32[]{:S(2)}) collective-permute-start(bf16[192,1024]{1,0:T(8,128)(2,1)} %slice.318), channel_id=1, source_target_pairs={{0,16},{8,24},{16,0},{24,8},{1,17},{9,25},{17,1},{25,9},{2,18},{10... | collective-permute-start | bytes 1179656 | tf_op jit(solution)/shard_map/ppermute | solution.py:64
  571.6 43.5 %collective-permute-start.20 = (bf16[4,2,2,32,4096]{4,3,2,1,0:T(8,128)(2,1)}, bf16[4,2,2,32,4096]{4,3,2,1,0:T(8,128)(2,1)}, u32[]{:S(2)}, u32[]{:S(2)}) collective-permute-start(bf16[4,2,2,32,4096]{4,3,2,1,0:T(8,128)(2,1)} %dynamic-slice_bitcast_fusion.1), channel_id=1, source_target_pairs={{0,1},{1,0},{2,3},{3,2},{4,5},{5,4},{6,7},{7,6},{8,9},{9,8},{10,11... | collective-permute-start | bytes 12582920 | tf_op jit(solution)/shard_map/ppermute | solution.py:226
  (74 other events, 1133.6 us)

commit v6 on v5

--- a/solution.py
+++ b/solution.py
@@ -418,7 +418,7 @@
         result = total[...]
         gated_ref[...] = (gate * result).astype(BF).reshape(groups_of)
         dl = jnp.sum(dr_ref[...].astype(F32) * result, axis=1, keepdims=True) * gate * (1.0 - gate)
-        dx_ref[...] = (back[...] + dl * centroid_ref[:1].astype(F32)).astype(BF)
+        dx_ref[...] = (back[...] + dl * centroid_ref[:16].astype(F32)[:1]).astype(BF)
         term_ref[...] = jnp.broadcast_to(jnp.sum(dl * x.astype(F32), axis=0, keepdims=True), term_ref.shape)
 
 
@@ -1084,14 +1084,13 @@
     grad_moved = [seq_shift(dr_mine, 2 * group) for group in range(1, groups)]
     grad_slots = [slots_of(placings[group], ([grad_tokens] + grad_moved)[group]) for group in range(groups)]
     grad_slots = jnp.concatenate(grad_slots, axis=1)
-    attended_mine, pair_in_low, grad_slots = tie(attended_mine, pair_in_low, grad_slots)
+    attended_mine, pair_in_low, grad_slots, win_high = tie(attended_mine, pair_in_low, grad_slots, win_mine[:, win_half:])
     grad_slots = swap_slots(grad_slots)
     attended = seq_exchange(attended_mine)
     attended = attended.transpose(1, 2, 0, 3).reshape(tokens, width)
-    attended, pair_in_high, pair_out_low, wout_high = tie(
-        attended, win_mine[:, win_half:], wout_mine[:wout_half], wout_mine[wout_half:]
-    )
-    pair_in_high, pair_out_low = seq_pair(pair_in_high), seq_pair(pair_out_low)
+    pair_in_high = seq_pair(win_high)
+    attended, pair_out_low, wout_high = tie(attended, wout_mine[:wout_half], wout_mine[wout_half:])
+    pair_out_low = seq_pair(pair_out_low)
 
     resid_in = tokens_in.astype(F32)
     middle = resid_in + mm(attended, out_all)

time: 776 us -> 768 us (0.990)
    ppermute x8, waiting for transfers between devices: 28.5 us -> 19.8 us  [seq_pair(): return lax.ppermute(values, 'seq', [(i, i ^ 1) for i in range(size)])]
    unnamed x158 -> x156, local copies, waits for them, and re-layouts: 28.9 us -> 29.6 us
  transfers between devices with their start and end apart: 28 -> 28, of which waited for: 17 -> 17; matrix products, arithmetic and copies ran while one was open for 18% -> 19% of each run, Pallas kernels for 14% -> 15%
where the time goes in v6:
time: 768 us; the launch traced here: 756 us
  Pallas kernels  392 us (51%)
  waiting for transfers between devices  120 us (16%)
  local copies, waits for them, and re-layouts  80.4 us (10%)
  matrix products  74.7 us (10%)
  starting transfers between devices  53.8 us (7%)
  other arithmetic  32.9 us (4%)
    pallas_call x1, Pallas kernels, finish_sums(): pl.pallas_call(functools.partial(finish_kernel, seq_size, bits), in_specs...  135 us
    pallas_call x1, Pallas kernels, start_gathers(): pl.pallas_call(functools.partial(gather_kernel, seq_size, bits), in_specs...  123 us
    ppermute x12, waiting for transfers between devices, seq_shift(): lax.ppermute(values, 'seq', [(i, (i + step) % size) for i in range(size)])  87.5 us
    dot_general x12, matrix products, mm_tn(): lax.dot_general(left, right, (((0,), (0,)), ((), ())), preferred_element_...  54.5 us
    pallas_call x2, Pallas kernels, expert_block(): pl.pallas_call(expert_kernel, grid=(own + 2,), in_specs=[whole, whole, ro...  46.3 us
    unnamed x156, local copies, waits for them, and re-layouts  29.6 us
    all_to_all x6, starting transfers between devices, swap_slots(): lax.all_to_all(values, 'fsdp', split_axis=0, concat_axis=0, tiled=True)  26.6 us
    pallas_call x1, Pallas kernels, attend_back(): pl.pallas_call(functools.partial(attend_back_kernel, min(256, length)), g...  21.1 us
  transfers between devices with their start and end apart: 28, of which 17 were waited for; matrix products, arithmetic and copies ran while one was open for 19% of the time, Pallas kernels for 15%

profile of v6, /device:TPU:0, one launch (start us, length us, event | category | flops | bytes accessed | tf_op | source)
XLA Modules:
  0.0 756.2 jit_solution(4396786460110008353)
XLA Ops:
  9.3 123.1 %shard_map.212 = (bf16[4,2,2,2,32,1920]{5,4,3,2,1,0:T(8,128)(2,1)}, bf16[4,2,2,2,32,4096]{5,4,3,2,1,0:T(8,128)(2,1)}, bf16[4,2,2,2,128,1024]{5,4,3,2,1,0:T(8,128)(2,1)}, bf16[4,512,1024]{2,1,0:T(8,128)(2,1)}) custom-call(bf16[4,32,1920]{2,1,0:T(8,128)(2,1)} %pad_maximum_fusion.2.proj_ref, bf16[32,4096]{1,0:T(8,128)(2,1)} %in_ref.1, ...), custom_call_target="tpu_custom_call" | custom-call | bytes 104857600 | tf_op jit(solution)/shard_map/pallas_call | solution.py:675
  143.1 7.3 shard_map.213
  152.4 19.7 %shard_map.214 = (bf16[4,2,256,256]{3,2,1,0:T(8,128)(2,1)S(1)}, f32[2,2,2,1024]{3,2,1,0:T(2,128)S(1)}) custom-call(bf16[4,2,256,768]{3,2,1,0:T(8,128)(2,1)S(1)} %bitcast.201, bf16[4,2,256,768]{3,2,1,0:T(8,128)(2,1)S(1)} %bitcast.202, bf16[4,2,256,768]{3,2,1,0:T(8,128)(2,1)S(1)} %bitcast.203, s32[2,1,1024]{2,1,0:T(1,128)S(1)} %fusion.61.id_row_ref, ...), custom_call_target="tpu_custom_call" | custom-call | flops 1000000 | bytes 65536 | tf_op jit(solution)/shard_map/pallas_call | solution.py:192
  173.2 7.0 collective-permute-done.1
  197.9 4.7 collective-permute-done.2
  204.3 8.6 %collective-permute-done.3 = bf16[2,256,256]{2,1,0:T(8,128)(2,1)} collective-permute-done((bf16[2,256,256]{2,1,0:T(8,128)(2,1)}, bf16[2,256,256]{2,1,0:T(8,128)(2,1)}, u32[]{:S(2)}, u32[]{:S(2)}) %collective-permute-start.3) | collective-permute-done | bytes 262176 | tf_op jit(solution)/shard_map/ppermute | solution.py:64
  224.4 18.6 %shard_map.215 = (bf16[512,1024]{1,0:T(8,128)(2,1)S(1)}, bf16[512,4096]{1,0:T(8,128)(2,1)}, bf16[512,4096]{1,0:T(8,128)(2,1)}, f32[512,1024]{1,0:T(8,128)S(1)}, bf16[512,1024]{1,0:T(8,128)(2,1)}) custom-call(f32[512,1024]{1,0:T(8,128)} %convert_add_fusion.middle_ref, f32[8,1024]{1,0:T(8,128)S(1)} %pad.20.gains_ref, f32[8,1024]{1,0:T(8,128)S(1)} %pad.21.biases_ref, ...), custom_call_target="tpu_custom_call" | custom-call | flops 1000000 | bytes 65536 | tf_op jit(solution)/shard_map/pallas_call | solution.py:315
  245.3 11.8 %collective-permute-done.6.wout_low = bf16[512,1024]{1,0:T(8,128)(2,1)S(1)} collective-permute-done((bf16[512,1024]{1,0:T(8,128)(2,1)S(1)}, bf16[512,1024]{1,0:T(8,128)(2,1)S(1)}, u32[]{:S(2)}, u32[]{:S(2)}) %collective-permute-start.6) | collective-permute-done | bytes 1048608 | tf_op jit(solution)/shard_map/ppermute | solution.py:69
  277.7 31.8 %collective-permute-done.7 = bf16[512,1024]{1,0:T(8,128)(2,1)} collective-permute-done((bf16[512,1024]{1,0:T(8,128)(2,1)}, bf16[512,1024]{1,0:T(8,128)(2,1)}, u32[]{:S(2)}, u32[]{:S(2)}) %collective-permute-start.7) | collective-permute-done | bytes 1048608 | tf_op jit(solution)/shard_map/ppermute | solution.py:64
  309.4 6.0 collective-permute-done.8.wout_high
  327.7 23.4 %shard_map.216 = (bf16[1536,2048]{1,0:T(8,128)(2,1)}, bf16[1536,2048]{1,0:T(8,128)(2,1)}, bf16[1536,1024]{1,0:T(8,128)(2,1)}, bf16[1536,1024]{1,0:T(8,128)(2,1)}...) custom-call(bf16[768,1024]{1,0:T(8,128)(2,1)} %bitcast.45.x_ref, ...), custom_call_target="tpu_custom_call" | custom-call | flops 1000000 | bytes 65536 | tf_op jit(solution)/shard_map/pallas_call | solution.py:437
  353.6 22.9 %shard_map.217 = (bf16[1536,2048]{1,0:T(8,128)(2,1)}, bf16[1536,2048]{1,0:T(8,128)(2,1)}, bf16[1536,1024]{1,0:T(8,128)(2,1)}, bf16[1536,1024]{1,0:T(8,128)(2,1)}...) custom-call(bf16[768,1024]{1,0:T(8,128)(2,1)} %bitcast.46.x_ref, ...), custom_call_target="tpu_custom_call", output_to_operand_aliasing={{0}: (9, {}), {1}: (10, {}), {2}: (11, {}), {3}: (12, {}), ... | custom-call | flops 1000000 | bytes 65536 | tf_op jit(solution)/shard_map/pallas_call | solution.py:437
  384.1 7.7 %fusion.22 = bf16[1024,1024]{1,0:T(8,128)(2,1)} fusion(bf16[1536,1024]{1,0:T(8,128)(2,1)} %get-tuple-element.168, bf16[1536,2048]{1,0:T(8,128)(2,1)} %get-tuple-element.169), kind=kOutput, calls=%fused_computation.39 | convolution fusion | flops 3222274048 | bytes 8388608 | tf_op jit(solution)/shard_map/dot_general | solution.py:39
  391.8 11.0 %all-to-all-done.3 = bf16[8,96,1024]{2,1,0:T(8,128)(2,1)S(1)} async-done(((bf16[8,96,1024]{2,1,0:T(8,128)(2,1)}), bf16[8,96,1024]{2,1,0:T(8,128)(2,1)S(1)}, u32[]{:S(2)}, u32[]{:S(2)}) %all-to-all-start.3) | async-done | bytes 1572896 | tf_op jit(solution)/shard_map/all_to_all | solution.py:1077
  410.0 8.5 %fusion.5 = f32[1024,1024]{1,0:T(8,128)} fusion(bf16[1536,1024]{1,0:T(8,128)(2,1)} %get-tuple-element.167, bf16[1536,2048]{1,0:T(8,128)(2,1)} %get-tuple-element.166), kind=kOutput, calls=%fused_computation.16 | convolution fusion | flops 3221225472 | bytes 10485760 | tf_op jit(solution)/shard_map/dot_general | solution.py:39
  423.2 5.1 fusion.7
  434.9 14.9 %collective-permute-done.9 = bf16[512,1024]{1,0:T(8,128)(2,1)} collective-permute-done((bf16[512,1024]{1,0:T(8,128)(2,1)}, bf16[512,1024]{1,0:T(8,128)(2,1)}, u32[]{:S(2)}, u32[]{:S(2)}) %collective-permute-start.9) | collective-permute-done | bytes 1048608 | tf_op jit(solution)/shard_map/ppermute | solution.py:64
  456.6 20.7 %shard_map.218 = (bf16[512,1024]{1,0:T(8,128)(2,1)S(1)}, bf16[512,4096]{1,0:T(8,128)(2,1)}, f32[512,1024]{1,0:T(8,128)S(1)}, bf16[512,1024]{1,0:T(8,128)(2,1)S(1)}, f32[8,1024]{1,0:T(8,128)S(1)}) custom-call(f32[512,1024]{1,0:T(8,128)} %convert_add_fusion.1.back_ref, f32[512,1024]{1,0:T(8,128)} %copy-done.11, bf16[512,1024]{1,0:T(8,128)(2,1)S(1)} %bitcast.214, ...), custom_call_target="tpu_custom_call" | custom-call | flops 1000000 | bytes 65536 | tf_op jit(solution)/shard_map/pallas_call | solution.py:366
  488.9 7.0 convolution_convert_fusion
  501.6 9.9 %collective-permute-done.12 = bf16[2,256,256]{2,1,0:T(8,128)(2,1)S(1)} collective-permute-done((bf16[2,256,256]{2,1,0:T(8,128)(2,1)S(1)}, bf16[2,256,256]{2,1,0:T(8,128)(2,1)S(1)}, u32[]{:S(2)}, u32[]{:S(2)}) %collective-permute-start.12) | collective-permute-done | bytes 262176 | tf_op jit(solution)/shard_map/ppermute | solution.py:64
  520.9 5.0 convolution_convert_fusion.1
  534.7 21.1 %shard_map.219 = (bf16[4,2,256,256]{3,2,1,0:T(8,128)(2,1)S(1)}, bf16[4,2,256,256]{3,2,1,0:T(8,128)(2,1)S(1)}, bf16[4,2,256,256]{3,2,1,0:T(8,128)(2,1)S(1)}) custom-call(bf16[4,2,256,768]{3,2,1,0:T(8,128)(2,1)} %bitcast.204, bf16[4,2,256,768]{3,2,1,0:T(8,128)(2,1)} %bitcast.205, bf16[4,2,256,768]{3,2,1,0:T(8,128)(2,1)} %bitcast.206, ...), custom_call_target="tpu_custom_call" | custom-call | flops 1000000 | bytes 65536 | tf_op jit(solution)/shard_map/pallas_call | solution.py:212
  577.4 5.8 add_bitcast_fusion.1
  609.1 135.1 %shard_map.220 = (f32[512,1024]{1,0:T(8,128)}, f32[32,4096]{1,0:T(8,128)}, f32[128,1024]{1,0:T(8,128)}, bf16[4,32,1920]{2,1,0:T(8,128)(2,1)}) custom-call(bf16[4,512,1024]{2,1,0:T(8,128)(2,1)} %bitcast.219, bf16[4,2,2,2,32,4096]{5,4,3,2,1,0:T(8,128)(2,1)} %bitcast.235, bf16[4,2,2,32,4096]{4,3,2,1,0:T(8,128)(2,1)} %collective-permute-done.20.in_added, ...), custom_call_target="tpu_custom_call" | custom-call | bytes 104857600 | tf_op jit(solution)/shard_map/pallas_call | solution.py:957
  (323 shorter events, 217.4 us)
Async XLA Ops:
  132.4 47.9 %collective-permute-start.1 = (bf16[512,1024]{1,0:T(8,128)(2,1)S(1)}, bf16[512,1024]{1,0:T(8,128)(2,1)}, u32[]{:S(2)}, u32[]{:S(2)}) collective-permute-start(bf16[512,1024]{1,0:T(8,128)(2,1)S(1)} %bitcast.212), channel_id=1, source_target_pairs={{0,16},{8,24},{16,0},{24,8},{1,17},{9,25},{17,1},{25,9},{2,18},{10... | collective-permute-start | bytes 3145736 | tf_op jit(solution)/shard_map/ppermute | solution.py:64
  135.5 49.2 %collective-permute-start = (bf16[1024,512]{1,0:T(8,128)(2,1)}, bf16[1024,512]{1,0:T(8,128)(2,1)S(1)}, u32[]{:S(2)}, u32[]{:S(2)}) collective-permute-start(bf16[1024,512]{1,0:T(8,128)(2,1)} %get-tuple-element.247), channel_id=1, source_target_pairs={{0,8},{8,0},{16,24},{24,16},{1,9},{9,1},{17,25},{25,17},{2,10},{10... | collective-permute-start | bytes 3145736 | tf_op jit(solution)/shard_map/ppermute | solution.py:69
  184.6 73.5 %all-to-all-start = ((bf16[8,192,1024]{2,1,0:T(8,128)(2,1)}), bf16[8,192,1024]{2,1,0:T(8,128)(2,1)}, u32[]{:S(2)}, u32[]{:S(2)}) async-start(bf16[8,192,1024]{2,1,0:T(8,128)(2,1)} %pad_maximum_fusion), calls=%async_computation | async-start | bytes 6291456 | tf_op jit(solution)/shard_map/all_to_all | solution.py:1077
  191.2 11.4 %collective-permute-start.2 = (bf16[2,256,256]{2,1,0:T(8,128)(2,1)}, bf16[2,256,256]{2,1,0:T(8,128)(2,1)}, u32[]{:S(2)}, u32[]{:S(2)}) collective-permute-start(bf16[2,256,256]{2,1,0:T(8,128)(2,1)} %get-tuple-element.254), channel_id=1, source_target_pairs={{0,8},{8,16},{16,24},{24,0},{1,9},{9,17},{17,25},{25,1},{2,10},{10... | collective-permute-start | bytes 786440 | tf_op jit(solution)/shard_map/ppermute | solution.py:64
  191.2 21.7 %collective-permute-start.3 = (bf16[2,256,256]{2,1,0:T(8,128)(2,1)}, bf16[2,256,256]{2,1,0:T(8,128)(2,1)}, u32[]{:S(2)}, u32[]{:S(2)}) collective-permute-start(bf16[2,256,256]{2,1,0:T(8,128)(2,1)} %get-tuple-element.253), channel_id=1, source_target_pairs={{0,16},{8,24},{16,0},{24,8},{1,17},{9,25},{17,1},{25,9},{2,18},{10... | collective-permute-start | bytes 786440 | tf_op jit(solution)/shard_map/ppermute | solution.py:64
  195.7 18.9 %collective-permute-start.4 = (bf16[2,256,256]{2,1,0:T(8,128)(2,1)}, bf16[2,256,256]{2,1,0:T(8,128)(2,1)S(1)}, u32[]{:S(2)}, u32[]{:S(2)}) collective-permute-start(bf16[2,256,256]{2,1,0:T(8,128)(2,1)} %get-tuple-element.252), channel_id=1, source_target_pairs={{0,24},{8,0},{16,8},{24,16},{1,25},{9,1},{17,9},{25,17},{2,26},{10... | collective-permute-start | bytes 786440 | tf_op jit(solution)/shard_map/ppermute | solution.py:64
  196.8 48.5 %collective-permute-start.5 = (bf16[1024,512]{1,0:T(8,128)(2,1)}, bf16[1024,512]{1,0:T(8,128)(2,1)S(1)}, u32[]{:S(2)}, u32[]{:S(2)}) collective-permute-start(bf16[1024,512]{1,0:T(8,128)(2,1)} %get-tuple-element.134), channel_id=1, source_target_pairs={{0,8},{8,0},{16,24},{24,16},{1,9},{9,1},{17,25},{25,17},{2,10},{10... | collective-permute-start | bytes 3145736 | tf_op jit(solution)/shard_map/ppermute | solution.py:69
  217.6 39.5 %collective-permute-start.6 = (bf16[512,1024]{1,0:T(8,128)(2,1)S(1)}, bf16[512,1024]{1,0:T(8,128)(2,1)S(1)}, u32[]{:S(2)}, u32[]{:S(2)}) collective-permute-start(bf16[512,1024]{1,0:T(8,128)(2,1)S(1)} %copy-done.46), channel_id=1, source_target_pairs={{0,8},{8,0},{16,24},{24,16},{1,9},{9,1},{17,25},{25,17},{2,10},{10... | collective-permute-start | bytes 3145736 | tf_op jit(solution)/shard_map/ppermute | solution.py:69
  261.6 47.9 %collective-permute-start.7 = (bf16[512,1024]{1,0:T(8,128)(2,1)}, bf16[512,1024]{1,0:T(8,128)(2,1)}, u32[]{:S(2)}, u32[]{:S(2)}) collective-permute-start(bf16[512,1024]{1,0:T(8,128)(2,1)} %get-tuple-element.137), channel_id=1, source_target_pairs={{0,16},{8,24},{16,0},{24,8},{1,17},{9,25},{17,1},{25,9},{2,18},{10... | collective-permute-start | bytes 3145736 | tf_op jit(solution)/shard_map/ppermute | solution.py:64
  263.1 56.8 %all-to-all-start.1 = ((bf16[8,96,1024]{2,1,0:T(8,128)(2,1)}), bf16[8,96,1024]{2,1,0:T(8,128)(2,1)}, u32[]{:S(2)}, u32[]{:S(2)}) async-start(bf16[8,96,1024]{2,1,0:T(8,128)(2,1)} %bitcast.254), calls=%async_computation.1 | async-start | bytes 3145728 | tf_op jit(solution)/shard_map/all_to_all | solution.py:1077
  267.4 48.0 %collective-permute-start.8 = (bf16[512,1024]{1,0:T(8,128)(2,1)}, bf16[512,1024]{1,0:T(8,128)(2,1)S(1)}, u32[]{:S(2)}, u32[]{:S(2)}) collective-permute-start(bf16[512,1024]{1,0:T(8,128)(2,1)} %get-tuple-element.138), channel_id=1, source_target_pairs={{0,8},{8,0},{16,24},{24,16},{1,9},{9,1},{17,25},{25,17},{2,10},{10... | collective-permute-start | bytes 3145736 | tf_op jit(solution)/shard_map/ppermute | solution.py:69
  319.9 31.3 %all-to-all-start.2 = ((bf16[8,96,1024]{2,1,0:T(8,128)(2,1)}), bf16[8,96,1024]{2,1,0:T(8,128)(2,1)}, u32[]{:S(2)}, u32[]{:S(2)}) async-start(bf16[8,96,1024]{2,1,0:T(8,128)(2,1)} %bitcast.253), calls=%async_computation.2 | async-start | bytes 3145728 | tf_op jit(solution)/shard_map/all_to_all | solution.py:1077
  377.6 25.2 %all-to-all-start.3 = ((bf16[8,96,1024]{2,1,0:T(8,128)(2,1)}), bf16[8,96,1024]{2,1,0:T(8,128)(2,1)S(1)}, u32[]{:S(2)}, u32[]{:S(2)}) async-start(bf16[8,96,1024]{2,1,0:T(8,128)(2,1)} %bitcast.211), calls=%async_computation.3 | async-start | bytes 3145728 | tf_op jit(solution)/shard_map/all_to_all | solution.py:1077
  404.8 45.0 %collective-permute-start.9 = (bf16[512,1024]{1,0:T(8,128)(2,1)}, bf16[512,1024]{1,0:T(8,128)(2,1)}, u32[]{:S(2)}, u32[]{:S(2)}) collective-permute-start(bf16[512,1024]{1,0:T(8,128)(2,1)} %fusion.32), channel_id=1, source_target_pairs={{0,16},{8,24},{16,0},{24,8},{1,17},{9,25},{17,1},{25,9},{2,18},{10... | collective-permute-start | bytes 3145736 | tf_op jit(solution)/shard_map/ppermute | solution.py:64
  404.8 25.5 %all-to-all-start.5 = ((bf16[8,96,1024]{2,1,0:T(8,128)(2,1)}), bf16[8,96,1024]{2,1,0:T(8,128)(2,1)}, u32[]{:S(2)}, u32[]{:S(2)}) async-start(bf16[8,96,1024]{2,1,0:T(8,128)(2,1)} %bitcast.47), calls=%async_computation.5 | async-start | bytes 3145728 | tf_op jit(solution)/shard_map/all_to_all | solution.py:1077
  409.3 78.2 %collective-permute-start.10 = (bf16[1024,1024]{1,0:T(8,128)(2,1)}, bf16[1024,1024]{1,0:T(8,128)(2,1)}, u32[]{:S(2)}, u32[]{:S(2)}) collective-permute-start(bf16[1024,1024]{1,0:T(8,128)(2,1)} %fusion.22), channel_id=1, source_target_pairs={{0,8},{8,0},{16,24},{24,16},{1,9},{9,1},{17,25},{25,17},{2,10},{10... | collective-permute-start | bytes 6291464 | tf_op jit(solution)/shard_map/ppermute | solution.py:69
  430.3 83.5 %all-to-all-start.4 = ((bf16[8,192,1024]{2,1,0:T(8,128)(2,1)}), bf16[8,192,1024]{2,1,0:T(8,128)(2,1)}, u32[]{:S(2)}, u32[]{:S(2)}) async-start(bf16[8,192,1024]{2,1,0:T(8,128)(2,1)} %get-tuple-element.163), calls=%async_computation.4 | async-start | bytes 6291456 | tf_op jit(solution)/shard_map/all_to_all | solution.py:1077
  498.8 12.7 %collective-permute-start.12 = (bf16[2,256,256]{2,1,0:T(8,128)(2,1)S(1)}, bf16[2,256,256]{2,1,0:T(8,128)(2,1)S(1)}, u32[]{:S(2)}, u32[]{:S(2)}) collective-permute-start(bf16[2,256,256]{2,1,0:T(8,128)(2,1)S(1)} %get-tuple-element.178), channel_id=1, source_target_pairs={{0,16},{8,24},{16,0},{24,8},{1,17},{9,25},{17,1},{25,9},{2,18},{10... | collective-permute-start | bytes 786440 | tf_op jit(solution)/shard_map/ppermute | solution.py:64
  501.6 107.5 %collective-permute-start.21 = (bf16[4,2,2,128,1024]{4,3,2,1,0:T(8,128)(2,1)}, bf16[4,2,2,128,1024]{4,3,2,1,0:T(8,128)(2,1)}, u32[]{:S(2)}, u32[]{:S(2)}) collective-permute-start(bf16[4,2,2,128,1024]{4,3,2,1,0:T(8,128)(2,1)} %dynamic-slice_bitcast_fusion), channel_id=1, source_target_pairs={{0,1},{1,0},{2,3},{3,2},{4,5},{5,4},{6,7},{7,6},{8,9},{9,8},{10,11... | collective-permute-start | bytes 12582920 | tf_op jit(solution)/shard_map/ppermute | solution.py:226
  520.8 35.9 %collective-permute-start.14 = (bf16[512,1024]{1,0:T(8,128)(2,1)}, bf16[512,1024]{1,0:T(8,128)(2,1)}, u32[]{:S(2)}, u32[]{:S(2)}) collective-permute-start(bf16[512,1024]{1,0:T(8,128)(2,1)} %slice.273), channel_id=1, source_target_pairs={{0,8},{8,0},{16,24},{24,16},{1,9},{9,1},{17,25},{25,17},{2,10},{10... | collective-permute-start | bytes 3145736 | tf_op jit(solution)/shard_map/ppermute | solution.py:69
  525.9 30.2 %collective-permute-start.15 = (bf16[256,1024]{1,0:T(8,128)(2,1)}, bf16[256,1024]{1,0:T(8,128)(2,1)S(1)}, u32[]{:S(2)}, u32[]{:S(2)}) collective-permute-start(bf16[256,1024]{1,0:T(8,128)(2,1)} %slice.317), channel_id=1, source_target_pairs={{0,16},{8,24},{16,0},{24,8},{1,17},{9,25},{17,1},{25,9},{2,18},{10... | collective-permute-start | bytes 1572872 | tf_op jit(solution)/shard_map/ppermute | solution.py:64
  560.3 26.8 %collective-permute-start.16 = (bf16[384,1024]{1,0:T(8,128)(2,1)S(1)}, bf16[384,1024]{1,0:T(8,128)(2,1)S(1)}, u32[]{:S(2)}, u32[]{:S(2)}) collective-permute-start(bf16[384,1024]{1,0:T(8,128)(2,1)S(1)} %copy-done.47), channel_id=1, source_target_pairs={{0,8},{8,0},{16,24},{24,16},{1,9},{9,1},{17,25},{25,17},{2,10},{10... | collective-permute-start | bytes 2359304 | tf_op jit(solution)/shard_map/ppermute | solution.py:69
  562.4 24.0 %collective-permute-start.17 = (bf16[192,1024]{1,0:T(8,128)(2,1)}, bf16[192,1024]{1,0:T(8,128)(2,1)}, u32[]{:S(2)}, u32[]{:S(2)}) collective-permute-start(bf16[192,1024]{1,0:T(8,128)(2,1)} %slice.318), channel_id=1, source_target_pairs={{0,16},{8,24},{16,0},{24,8},{1,17},{9,25},{17,1},{25,9},{2,18},{10... | collective-permute-start | bytes 1179656 | tf_op jit(solution)/shard_map/ppermute | solution.py:64
  565.9 43.2 %collective-permute-start.20 = (bf16[4,2,2,32,4096]{4,3,2,1,0:T(8,128)(2,1)}, bf16[4,2,2,32,4096]{4,3,2,1,0:T(8,128)(2,1)}, u32[]{:S(2)}, u32[]{:S(2)}) collective-permute-start(bf16[4,2,2,32,4096]{4,3,2,1,0:T(8,128)(2,1)} %dynamic-slice_bitcast_fusion.1), channel_id=1, source_target_pairs={{0,1},{1,0},{2,3},{3,2},{4,5},{5,4},{6,7},{7,6},{8,9},{9,8},{10,11... | collective-permute-start | bytes 12582920 | tf_op jit(solution)/shard_map/ppermute | solution.py:226
  (73 other events, 1110.8 us)
